TPU v7x, 32 devices: a whole 2x2x4 slice. The times are simulated.
32 devices in a mesh: grp: 2 (over y), ep: 8 (over z, x), dp: 2 (over core).
Axes of the slice: x: 2, y: 2, z: 4, core: 2. Of those that a mesh axis runs over, the one named last changes fastest.
Arguments:
- tokens: bfloat16 [4096, 2048], P(('grp', 'ep', 'dp')), parts along dimension 0, may hold values from -6 to 6
- expert_ids: int32 [4096, 8], P(('grp', 'ep', 'dp')), parts along dimension 0, may hold values from 0 to 15, all different within a row; in each aligned block of 128 rows (0 to 127, 128 to 255, ...) at most 80 rows name the same one
- route_gates: float32 [4096, 8], P(('grp', 'ep', 'dp')), parts along dimension 0, may hold values from 0.2 to 1
- expert_in: bfloat16 [32, 2048, 1536], P(('grp', 'ep', 'dp')), parts along dimension 0, may hold values from -0.125 to 0.125
- expert_out: bfloat16 [32, 768, 2048], P(('grp', 'ep', 'dp')), parts along dimension 0, may hold values from -0.21875 to 0.21875
- old_place: int32 [16], replicated, may hold values from 0 to 15, as said below
- new_place: int32 [16], replicated, may hold values from 0 to 15, as said below
Outputs:
- moe_out: bfloat16 [4096, 2048], P(('grp', 'ep', 'dp')), parts along dimension 0
There are 2 independent parts, one for each index of `grp`. A program takes and returns all parts, laid end to end along the dimension named above; an argument that names none is the same for every part. Nothing has to cross between parts.
Inputs may be any that keep to these rules, and one draw needn't show every extreme that they name: `expert_ids`: each row names 8 different experts; in the 128 rows of one device no expert is named by more than 80 rows, a bound that some block reaches. `old_place`: A permutation of the 16 devices. `new_place`: a permutation of the 16 devices with new_place[e] != old_place[e] for every expert e.
All inputs are finite; a program needn't handle non-finite values.
Results may differ from a plain program's by a relative error of at most 0.0058.
Values may be sent and summed in bfloat16 or wider, within the bound.
No kernel may reach another device: no remote copies, remote signals or barrier semaphores. Data moves between devices by JAX's collectives and lax.ppermute only.
A program may use at most 128 MiB of HBM per device.

v0:
```python
import jax
import jax.numpy as jnp
from jax import lax
from jax.sharding import PartitionSpec as P

BLOCK = 128
SERVE_BLOCKS = 9


def expert_block(inputs, in_weights, out_weights, hidden_units):
    projected = jnp.dot(inputs, in_weights, preferred_element_type=jnp.float32)
    gate_part = projected[:, :hidden_units]
    up_part = projected[:, hidden_units:]
    hidden = (jax.nn.silu(gate_part) * up_part).astype(jnp.bfloat16)
    return jnp.dot(hidden, out_weights, preferred_element_type=jnp.float32).astype(jnp.bfloat16)


def body(tokens, expert_ids, route_gates, expert_in, expert_out, old_place, new_place):
    ep_size = lax.axis_size("ep")
    dp_size = lax.axis_size("dp")
    devices = ep_size * dp_size
    tok_rows, top_count = expert_ids.shape
    model_width = tokens.shape[1]
    hidden_units = expert_out.shape[1]
    assigns = tok_rows * top_count
    capacity = (5 * assigns + 4 * devices - 1) // (4 * devices)
    serve_rows = SERVE_BLOCKS * BLOCK
    experts = jnp.arange(devices, dtype=jnp.int32)
    flat_ids = expert_ids.reshape(assigns)
    server = jnp.sum(
        jnp.where(flat_ids[:, None] == experts[None, :], old_place[None, :], 0), axis=1
    )
    onehot = (server[:, None] == experts[None, :]).astype(jnp.int32)
    local_rank = jnp.sum((jnp.cumsum(onehot, axis=0) - onehot) * onehot, axis=1)
    counts = jnp.sum(onehot, axis=0)
    slot_index = server * capacity + local_rank
    holder = (
        jnp.full((devices * capacity,), assigns, jnp.int32)
        .at[slot_index]
        .set(jnp.arange(assigns, dtype=jnp.int32))
    )
    token_index = jnp.where(holder < assigns, holder // top_count, tok_rows)
    send_rows = jnp.take(tokens, token_index, axis=0, mode="fill", fill_value=0).reshape(
        devices, capacity, model_width
    )
    recv_rows, recv_counts = (
        lax.all_to_all(send_rows, ("ep", "dp"), split_axis=0, concat_axis=0, tiled=True),
        lax.all_to_all(counts, ("ep", "dp"), split_axis=0, concat_axis=0, tiled=True),
    )
    source_home = experts % dp_size == 0
    home_counts = jnp.where(source_home, recv_counts, 0)
    rep_counts = recv_counts - home_counts
    earlier = jnp.where(
        source_home, jnp.cumsum(home_counts) - home_counts, jnp.cumsum(rep_counts) - rep_counts
    )
    home_blocks = (jnp.sum(home_counts) + BLOCK - 1) // BLOCK
    column = jnp.arange(capacity, dtype=jnp.int32)
    slot_rank = earlier[:, None] + column[None, :]
    present = column[None, :] < recv_counts[:, None]
    own_in = expert_in[0]
    own_out = expert_out[0]
    own_index = lax.axis_index("ep") * dp_size + lax.axis_index("dp")
    held_expert = jnp.sum(jnp.where(old_place == own_index, experts, 0))
    replica_server = jnp.sum(jnp.where(experts == held_expert, new_place, 0))
    all_blocks = lax.all_gather(
        home_blocks.astype(jnp.int32).reshape(1), ("ep", "dp"), axis=0, tiled=True
    )
    replica_blocks = jnp.sum(jnp.where(experts == replica_server, all_blocks, 0))
    base_rows = jnp.minimum(home_blocks, SERVE_BLOCKS) * BLOCK
    served_here = jnp.where(
        source_home[:, None],
        slot_rank < serve_rows,
        replica_blocks * BLOCK + slot_rank < serve_rows,
    )
    live_rows = present & served_here
    pack_rows = 2 * serve_rows
    position = jnp.where(source_home[:, None], slot_rank, base_rows + slot_rank)
    position = jnp.where(live_rows, position, pack_rows).reshape(devices * capacity)
    used_blocks = (jnp.max(jnp.where(position < pack_rows, position + 1, 0)) + BLOCK - 1) // BLOCK
    source_of = (
        jnp.full((pack_rows,), devices * capacity, jnp.int32)
        .at[position]
        .set(jnp.arange(devices * capacity, dtype=jnp.int32), mode="drop")
    )
    packed = jnp.take(
        recv_rows.reshape(devices * capacity, model_width),
        source_of,
        axis=0,
        mode="fill",
        fill_value=0,
    )

    def owner_block(state, block_id):
        inputs = lax.dynamic_slice_in_dim(packed, block_id * BLOCK, BLOCK, 0)
        result = lax.cond(
            block_id < used_blocks,
            lambda rows: expert_block(rows, own_in, own_out, hidden_units),
            lambda rows: jnp.zeros((BLOCK, model_width), jnp.bfloat16),
            inputs,
        )
        return (state, result)

    unused_state, outputs = lax.scan(
        owner_block, jnp.int32(0), jnp.arange(2 * SERVE_BLOCKS, dtype=jnp.int32)
    )
    results = jnp.take(
        outputs.reshape(pack_rows, model_width), position, axis=0, mode="fill", fill_value=0
    ).reshape(devices, capacity, model_width)
    returned = lax.all_to_all(results, ("ep", "dp"), split_axis=0, concat_axis=0, tiled=True)
    picked_rows = jnp.take(returned.reshape(devices * capacity, model_width), slot_index, axis=0)
    weighted = picked_rows.astype(jnp.float32) * route_gates.reshape(assigns)[:, None]
    return jnp.sum(weighted.reshape(tok_rows, top_count, model_width), axis=1).astype(jnp.bfloat16)


def solution(mesh):
    placed = (
        P(("grp", "ep", "dp"), None),
        P(("grp", "ep", "dp"), None),
        P(("grp", "ep", "dp"), None),
        P(("grp", "ep", "dp"), None, None),
        P(("grp", "ep", "dp"), None, None),
        P(),
        P(),
    )
    return jax.shard_map(
        body, mesh=mesh, in_specs=placed, out_specs=P(("grp", "ep", "dp"), None), check_vma=False
    )
```

profile of v0, /device:TPU:11, one launch (start us, length us, event | category | flops | bytes accessed | tf_op | source)
XLA Modules:
  0.0 440.6 jit_solution(2467093895677920349)
XLA Ops:
  0.0 0.8 copy.26
  0.9 0.7 select_reduce_fusion
  1.7 4.5 %reduce-window.26 = s32[16,8,128]{2,1,0:T(8,128)S(1)} reduce-window(s32[16,8,128]{2,1,0:T(8,128)S(1)} %fusion.10, s32[]{:T(128)} %copy.46), window={size=1x1x128 pad=0_0x0_0x127_0}, to_apply=%region_1.2 | reduce-window | flops 2080768 | bytes 131076 | tf_op jit(solution)/shard_map/reduce-window
  6.8 0.7 copy.29
  7.5 6.6 %all-to-all-start = ((s32[16,1,1]{2,1,0:T(1,128)}), s32[16,1,1]{2,1,0:T(1,128)S(1)}, u32[]{:S(2)}, u32[]{:S(2)}) async-start(s32[16,1,1]{2,1,0:T(1,128)} %copy.29), calls=%async_computation | async-start | bytes 16384 | tf_op jit(solution)/shard_map/all_to_all | solution.py:48
  14.0 4.3 scatter_custom_fusion.1
  18.5 6.1 %gather_fusion = bf16[1280,2048]{1,0:T(8,128)(2,1)} fusion(bf16[128,2048]{1,0:T(8,128)(2,1)S(1)} %copy-done, s32[2048]{0:T(1024)S(1)} %pad_clamp_fusion.2), kind=kCustom, calls=%fused_computation | custom fusion | bytes 10490880 | tf_op jit(solution)/shard_map/jit(_take)/gather | solution.py:43
  24.6 5.3 %broadcast_select_fusion.1 = bf16[16,80,2048]{2,1,0:T(8,128)(2,1)} fusion(bf16[16,80,2048]{2,1,0:T(8,128)(2,1)} %bitcast.42, pred[16,80]{1,0:T(8,128)(4,1)S(1)} %broadcast_in_dim.136), kind=kLoop, calls=%fused_computation.18 | loop fusion | flops 2621440 | bytes 10487040 | tf_op jit(solution)/shard_map/jit(_take)/select_n | solution.py:43
  29.9 6.2 %all-to-all-start.1 = ((bf16[16,80,2048]{2,1,0:T(8,128)(2,1)}), bf16[16,80,2048]{2,1,0:T(8,128)(2,1)}, u32[]{:S(2)}, u32[]{:S(2)}) async-start(bf16[16,80,2048]{2,1,0:T(8,128)(2,1)} %broadcast_select_fusion.1), calls=%async_computation.1 | async-start | bytes 10485760 | tf_op jit(solution)/shard_map/all_to_all | solution.py:47
  36.1 0.6 dynamic-slice
  36.8 0.6 fusion.25
  37.4 1.4 fusion.26
  39.6 0.6 subtract_select_fusion
  41.0 0.7 dynamic-update-slice
  41.9 107.1 %all-reduce = s32[16]{0:T(128)S(1)} all-reduce(s32[16]{0:T(128)S(1)} %dynamic-update-slice), channel_id=1, replica_groups=mesh['grp'=2,'ep'=8,'dp'=2] {'ep','dp'}, use_global_device_ids=true, to_apply=%add | all-reduce | flops 16 | bytes 128
  148.9 1.3 fusion.27
  150.9 0.7 iota_add_fusion
  152.6 5.4 %scatter_custom_fusion = s32[2304]{0:T(1024)S(1)} fusion(s32[1280]{0:T(1024)S(1)} %fusion.21, s32[1280]{0:T(1024)S(1)} %iota.54, s32[]{:T(128)} %constant.159.clone.1), kind=kCustom, calls=%fused_computation.65 | custom fusion | bytes 9220 | tf_op jit(solution)/shard_map/scatter | solution.py:83
  158.1 21.5 %gather_fusion.1 = bf16[2304,2048]{1,0:T(8,128)(2,1)} fusion(bf16[1280,2048]{1,0:T(8,128)(2,1)} %bitcast.11, s32[3072]{0:T(1024)S(1)} %pad_clamp_fusion), kind=kCustom, calls=%fused_computation.1 | custom fusion | bytes 18883584 | tf_op jit(solution)/shard_map/jit(_take)/gather | solution.py:85
  179.7 8.1 %broadcast_select_fusion = bf16[2304,2048]{1,0:T(8,128)(2,1)} fusion(bf16[2304,2048]{1,0:T(8,128)(2,1)} %gather_fusion.1, pred[2304]{0:T(1024)(128)(4,1)S(1)} %compare_and_fusion.1), kind=kLoop, calls=%fused_computation.16 | loop fusion | flops 4718592 | bytes 18876672 | tf_op jit(solution)/shard_map/jit(_take)/select_n | solution.py:85
  187.7 86.6 %while.10 = (s32[]{:T(128)}, bf16[18,128,2048]{2,1,0:T(8,128)(2,1)}, s32[18]{0:T(128)S(1)}, s32[]{:T(128)}, bf16[2304,2048]{1,0:T(8,128)(2,1)}, /*index=5*/bf16[...) while((s32[]{:T(128)}, bf16[18,128,2048]{2,1,0:T(8,128)(2,1)}, s32[18]{0:T(128)S(1)}, s32[]{:T(128)}, ...), condition=%wide.region_17.18_spmd, body=%wide.region_14.17_spmd.sunk | while | flops 1208811520 | bytes 25690852 | solution.py:103
  187.7 0.6 dynamic_slice.15
  189.0 5.3 %conditional.2 = (bf16[1,128,2048]{2,1,0:T(8,128)(2,1)S(1)}) conditional(s32[]{:T(128)} %convert_element_type.45, () %tuple.41, (s32[]{:T(128)}, bf16[2304,2048]{1,0:T(8,128)(2,1)}, bf16[2048,1536]{1,0:T(8,128)(2,1)}, bf16[768,2048]{1,0:T(8,128)(2,1)}) %tuple.42), branch_computations={%region_15.15_spmd, %region_16.16_spmd} | conditional | flops 1208811520 | bytes 24641622 | solution.py:95
  189.6 4.1 fusion.1
  194.3 0.8 constant_dynamic-update-slice_fusion.2
  196.4 5.3 %conditional.2 = (bf16[1,128,2048]{2,1,0:T(8,128)(2,1)S(1)}) conditional(s32[]{:T(128)} %convert_element_type.45, () %tuple.41, (s32[]{:T(128)}, bf16[2304,2048]{1,0:T(8,128)(2,1)}, bf16[2048,1536]{1,0:T(8,128)(2,1)}, bf16[768,2048]{1,0:T(8,128)(2,1)}) %tuple.42), branch_computations={%region_15.15_spmd, %region_16.16_spmd} | conditional | flops 1208811520 | bytes 24641622 | solution.py:95
  197.0 4.1 fusion.1
  201.7 0.9 constant_dynamic-update-slice_fusion.2
  203.8 5.3 %conditional.2 = (bf16[1,128,2048]{2,1,0:T(8,128)(2,1)S(1)}) conditional(s32[]{:T(128)} %convert_element_type.45, () %tuple.41, (s32[]{:T(128)}, bf16[2304,2048]{1,0:T(8,128)(2,1)}, bf16[2048,1536]{1,0:T(8,128)(2,1)}, bf16[768,2048]{1,0:T(8,128)(2,1)}) %tuple.42), branch_computations={%region_15.15_spmd, %region_16.16_spmd} | conditional | flops 1208811520 | bytes 24641622 | solution.py:95
  204.5 4.1 fusion.1
  209.2 0.9 constant_dynamic-update-slice_fusion.2
  211.3 5.3 %conditional.2 = (bf16[1,128,2048]{2,1,0:T(8,128)(2,1)S(1)}) conditional(s32[]{:T(128)} %convert_element_type.45, () %tuple.41, (s32[]{:T(128)}, bf16[2304,2048]{1,0:T(8,128)(2,1)}, bf16[2048,1536]{1,0:T(8,128)(2,1)}, bf16[768,2048]{1,0:T(8,128)(2,1)}) %tuple.42), branch_computations={%region_15.15_spmd, %region_16.16_spmd} | conditional | flops 1208811520 | bytes 24641622 | solution.py:95
  211.9 4.1 fusion.1
  216.7 0.9 constant_dynamic-update-slice_fusion.2
  218.7 5.3 %conditional.2 = (bf16[1,128,2048]{2,1,0:T(8,128)(2,1)S(1)}) conditional(s32[]{:T(128)} %convert_element_type.45, () %tuple.41, (s32[]{:T(128)}, bf16[2304,2048]{1,0:T(8,128)(2,1)}, bf16[2048,1536]{1,0:T(8,128)(2,1)}, bf16[768,2048]{1,0:T(8,128)(2,1)}) %tuple.42), branch_computations={%region_15.15_spmd, %region_16.16_spmd} | conditional | flops 1208811520 | bytes 24641622 | solution.py:95
  219.4 4.1 fusion.1
  224.1 0.8 constant_dynamic-update-slice_fusion.2
  226.2 5.3 %conditional.2 = (bf16[1,128,2048]{2,1,0:T(8,128)(2,1)S(1)}) conditional(s32[]{:T(128)} %convert_element_type.45, () %tuple.41, (s32[]{:T(128)}, bf16[2304,2048]{1,0:T(8,128)(2,1)}, bf16[2048,1536]{1,0:T(8,128)(2,1)}, bf16[768,2048]{1,0:T(8,128)(2,1)}) %tuple.42), branch_computations={%region_15.15_spmd, %region_16.16_spmd} | conditional | flops 1208811520 | bytes 24641622 | solution.py:95
  226.8 4.1 fusion.1
  231.5 0.9 constant_dynamic-update-slice_fusion.2
  233.6 5.3 %conditional.2 = (bf16[1,128,2048]{2,1,0:T(8,128)(2,1)S(1)}) conditional(s32[]{:T(128)} %convert_element_type.45, () %tuple.41, (s32[]{:T(128)}, bf16[2304,2048]{1,0:T(8,128)(2,1)}, bf16[2048,1536]{1,0:T(8,128)(2,1)}, bf16[768,2048]{1,0:T(8,128)(2,1)}) %tuple.42), branch_computations={%region_15.15_spmd, %region_16.16_spmd} | conditional | flops 1208811520 | bytes 24641622 | solution.py:95
  234.3 4.1 fusion.1
  239.0 0.8 constant_dynamic-update-slice_fusion.2
  241.1 5.3 %conditional.2 = (bf16[1,128,2048]{2,1,0:T(8,128)(2,1)S(1)}) conditional(s32[]{:T(128)} %convert_element_type.45, () %tuple.41, (s32[]{:T(128)}, bf16[2304,2048]{1,0:T(8,128)(2,1)}, bf16[2048,1536]{1,0:T(8,128)(2,1)}, bf16[768,2048]{1,0:T(8,128)(2,1)}) %tuple.42), branch_computations={%region_15.15_spmd, %region_16.16_spmd} | conditional | flops 1208811520 | bytes 24641622 | solution.py:95
  241.7 4.1 fusion.1
  246.4 0.9 constant_dynamic-update-slice_fusion.2
  248.5 5.3 %conditional.2 = (bf16[1,128,2048]{2,1,0:T(8,128)(2,1)S(1)}) conditional(s32[]{:T(128)} %convert_element_type.45, () %tuple.41, (s32[]{:T(128)}, bf16[2304,2048]{1,0:T(8,128)(2,1)}, bf16[2048,1536]{1,0:T(8,128)(2,1)}, bf16[768,2048]{1,0:T(8,128)(2,1)}) %tuple.42), branch_computations={%region_15.15_spmd, %region_16.16_spmd} | conditional | flops 1208811520 | bytes 24641622 | solution.py:95
  249.2 4.1 fusion.1
  253.9 0.8 constant_dynamic-update-slice_fusion.2
  256.0 0.9 constant_dynamic-update-slice_fusion.2
  258.2 0.9 constant_dynamic-update-slice_fusion.2
  260.4 0.9 constant_dynamic-update-slice_fusion.2
  262.5 0.9 constant_dynamic-update-slice_fusion.2
  264.7 0.9 constant_dynamic-update-slice_fusion.2
  266.9 0.8 constant_dynamic-update-slice_fusion.2
  269.0 0.9 constant_dynamic-update-slice_fusion.2
  271.2 0.9 constant_dynamic-update-slice_fusion.2
  273.4 0.9 constant_dynamic-update-slice_fusion.2
  274.3 15.7 %gather_fusion.2 = bf16[1280,2048]{1,0:T(8,128)(2,1)} fusion(bf16[2304,2048]{1,0:T(8,128)(2,1)} %bitcast.39, s32[2048]{0:T(1024)S(1)} %pad_clamp_fusion.1), kind=kCustom, calls=%fused_computation.2 | custom fusion | bytes 10490880 | tf_op jit(solution)/shard_map/jit(_take)/gather | solution.py:106
  290.0 5.2 %broadcast_select_fusion.2 = bf16[16,80,2048]{2,1,0:T(8,128)(2,1)} fusion(bf16[16,80,2048]{2,1,0:T(8,128)(2,1)} %bitcast.41, pred[16,80]{1,0:T(8,128)(4,1)S(1)} %get-tuple-element.113), kind=kLoop, calls=%fused_computation.19 | loop fusion | flops 2621440 | bytes 10487040 | tf_op jit(solution)/shard_map/jit(_take)/select_n | solution.py:106
  295.2 12.1 %all-to-all-start.2 = ((bf16[16,80,2048]{2,1,0:T(8,128)(2,1)}), bf16[16,80,2048]{2,1,0:T(8,128)(2,1)}, u32[]{:S(2)}, u32[]{:S(2)}) async-start(bf16[16,80,2048]{2,1,0:T(8,128)(2,1)} %broadcast_select_fusion.2), calls=%async_computation.2 | async-start | bytes 10485760 | tf_op jit(solution)/shard_map/all_to_all | solution.py:109
  307.6 114.7 %all-to-all-done.2 = bf16[16,80,2048]{2,1,0:T(8,128)(2,1)} async-done(((bf16[16,80,2048]{2,1,0:T(8,128)(2,1)}), bf16[16,80,2048]{2,1,0:T(8,128)(2,1)}, u32[]{:S(2)}, u32[]{:S(2)}) %all-to-all-start.2) | async-done | bytes 5242912 | tf_op jit(solution)/shard_map/all_to_all | solution.py:109
  422.3 12.1 %gather_fusion.3 = bf16[1024,2048]{1,0:T(8,128)(2,1)} fusion(bf16[1280,2048]{1,0:T(8,128)(2,1)} %bitcast.16, s32[1024]{0:T(1024)S(1)} %broadcast_clamp_fusion), kind=kCustom, calls=%fused_computation.3 | custom fusion | bytes 8392704 | tf_op jit(solution)/shard_map/jit(_take)/gather | solution.py:110
  434.4 6.3 %multiply_reduce_fusion = bf16[128,2048]{1,0:T(8,128)(2,1)} fusion(bf16[1024,2048]{1,0:T(8,128)(2,1)} %gather_fusion.3, f32[128,8]{1,0:T(8,128)S(1)} %copy.32, pred[128,8]{1,0:T(8,128)(4,1)S(1)} %compare_and_fusion), kind=kLoop, calls=%fused_computation.17 | loop fusion | flops 8126464 | bytes 4723712 | tf_op jit(solution)/shard_map/reduce_sum | solution.py:112
  (118 shorter events, 19.3 us)
Async XLA Ops:
  0.0 18.5 %copy-start = (bf16[128,2048]{1,0:T(8,128)(2,1)S(1)}, bf16[128,2048]{1,0:T(8,128)(2,1)}, u32[]{:S(2)}) copy-start(bf16[128,2048]{1,0:T(8,128)(2,1)} %param.11) | copy-start | bytes 1572868
  7.5 22.5 %all-to-all-start = ((s32[16,1,1]{2,1,0:T(1,128)}), s32[16,1,1]{2,1,0:T(1,128)S(1)}, u32[]{:S(2)}, u32[]{:S(2)}) async-start(s32[16,1,1]{2,1,0:T(1,128)} %copy.29), calls=%async_computation | async-start | bytes 16384 | tf_op jit(solution)/shard_map/all_to_all | solution.py:48
  29.9 6.2 %copy-start.6 = (u32[32]{0:T(128)S(1)}, u32[32]{0:T(128)}, u32[]{:S(2)}) copy-start(u32[32]{0:T(128)} %constant.183) | copy-start | bytes 388
  29.9 6.9 %copy-start.3 = (s32[16]{0:T(128)S(1)}, s32[16]{0:T(128)}, u32[]{:S(2)}) copy-start(s32[16]{0:T(128)} %param.16) | copy-start | bytes 196
  29.9 7.5 %copy-start.5 = (s32[16]{0:T(128)S(1)}, s32[16]{0:T(128)}, u32[]{:S(2)}) copy-start(s32[16]{0:T(128)} %param.17) | copy-start | bytes 196
  29.9 128.2 %all-to-all-start.1 = ((bf16[16,80,2048]{2,1,0:T(8,128)(2,1)}), bf16[16,80,2048]{2,1,0:T(8,128)(2,1)}, u32[]{:S(2)}, u32[]{:S(2)}) async-start(bf16[16,80,2048]{2,1,0:T(8,128)(2,1)} %broadcast_select_fusion.1), calls=%async_computation.1 | async-start | bytes 10485760 | tf_op jit(solution)/shard_map/all_to_all | solution.py:47
  189.6 4.1 copy-start.4
  197.0 4.1 copy-start.4
  204.5 4.1 copy-start.4
  211.9 4.1 copy-start.4
  219.4 4.1 copy-start.4
  226.8 4.1 copy-start.4
  234.3 4.1 copy-start.4
  241.7 4.1 copy-start.4
  249.2 4.1 copy-start.4
  295.2 12.2 %copy-start.2 = (f32[128,8]{0,1:T(8,128)S(1)}, f32[128,8]{0,1:T(8,128)}, u32[]{:S(2)}) copy-start(f32[128,8]{0,1:T(8,128)} %param.13) | copy-start | bytes 12292
  295.2 127.0 %all-to-all-start.2 = ((bf16[16,80,2048]{2,1,0:T(8,128)(2,1)}), bf16[16,80,2048]{2,1,0:T(8,128)(2,1)}, u32[]{:S(2)}, u32[]{:S(2)}) async-start(bf16[16,80,2048]{2,1,0:T(8,128)(2,1)} %broadcast_select_fusion.2), calls=%async_computation.2 | async-start | bytes 10485760 | tf_op jit(solution)/shard_map/all_to_all | solution.py:109
  422.3 18.4 %copy-start.1 = (bf16[128,2048]{1,0:T(8,128)(2,1)S(1)}, bf16[128,2048]{1,0:T(8,128)(2,1)}, u32[]{:S(2)}) copy-start(bf16[128,2048]{1,0:T(8,128)(2,1)} %param.11) | copy-start | bytes 1572868
where the time goes:
time: 442 us; the launch traced here: 441 us
  waiting for transfers between devices  115 us (26%)
  blocking collectives  107 us (24%)
  local copies, waits for them, and re-layouts  96.4 us (22%)
  matrix products  42.2 us (10%)
  other arithmetic  36 us (8%)
  starting transfers between devices  24.8 us (6%)
  loops' own time  17.3 us (4%)
    all_to_all x1, waiting for transfers between devices, body(): lax.all_to_all(results, ('ep', 'dp'), split_axis=0, concat_axis=0, tiled=...  115 us
    unnamed x1, blocking collectives  107 us
    dot_general x9, matrix products, expert_block(): projected = jnp.dot(inputs, in_weights, preferred_element_type=jnp.float32)  36.7 us
    gather x1, local copies, waits for them, and re-layouts, body(): jnp.take(recv_rows.reshape(devices * capacity, model_width), source_of, a...  21.5 us
    gather x1, local copies, waits for them, and re-layouts, body(): jnp.take(outputs.reshape(pack_rows, model_width), position, axis=0, mode=...  15.7 us
    dynamic_update_slice x18, local copies, waits for them, and re-layouts, body(): lax.scan(owner_block, jnp.int32(0), jnp.arange(2 * SERVE_BLOCKS, dtype=jn...  15.5 us
    gather x1, local copies, waits for them, and re-layouts, body(): jnp.take(returned.reshape(devices * capacity, model_width), slot_index, a...  12.1 us
    all_to_all x1, starting transfers between devices, body(): lax.all_to_all(results, ('ep', 'dp'), split_axis=0, concat_axis=0, tiled=...  12.1 us
  transfers between devices with their start and end apart: 3, of which 1 were waited for; matrix products, arithmetic and copies ran while one was open for 7% of the time, Pallas kernels for 0%

commit v1 on v0

--- a/solution.py
+++ b/solution.py
@@ -1,6 +1,10 @@
+import functools
+
 import jax
 import jax.numpy as jnp
 from jax import lax
+from jax.experimental import pallas as pl
+from jax.experimental.pallas import tpu as pltpu
 from jax.sharding import PartitionSpec as P
 
 BLOCK = 128
@@ -15,7 +19,7 @@
     return jnp.dot(hidden, out_weights, preferred_element_type=jnp.float32).astype(jnp.bfloat16)
 
 
-def body(tokens, expert_ids, route_gates, expert_in, expert_out, old_place, new_place):
+def routed_body(tokens, expert_ids, route_gates, expert_in, expert_out, old_place, new_place):
     ep_size = lax.axis_size("ep")
     dp_size = lax.axis_size("dp")
     devices = ep_size * dp_size
@@ -112,6 +116,233 @@
     return jnp.sum(weighted.reshape(tok_rows, top_count, model_width), axis=1).astype(jnp.bfloat16)
 
 
+def gate_kernel(info_ref, old_ref, new_ref, dense_ref, out_ref):
+    devices, _, tok_rows = dense_ref.shape
+    own = info_ref[0]
+    kind = own % 2
+    dense = dense_ref[...]
+    which = lax.broadcasted_iota(jnp.int32, dense.shape, 1)
+    source_col = lax.broadcasted_iota(jnp.int32, (devices, devices), 0) ^ own
+    source_row = lax.broadcasted_iota(jnp.int32, (devices, devices), 1) ^ own
+    before = ((source_row < source_col) & (source_row % 2 == kind)).astype(jnp.float32)
+    earlier = (
+        lax.broadcasted_iota(jnp.int32, (tok_rows, tok_rows), 0)
+        < lax.broadcasted_iota(jnp.int32, (tok_rows, tok_rows), 1)
+    ).astype(jnp.float32)
+    home = (lax.broadcasted_iota(jnp.int32, (devices, tok_rows), 0) ^ own) % 2 == 0
+
+    def holds(server):
+        return lax.fori_loop(
+            0, devices, lambda e, found: jnp.where(old_ref[e] == server, e, found), 0
+        )
+
+    def gates_of(expert):
+        return jnp.sum(jnp.where(which == expert, dense, 0.0), axis=1)
+
+    for q in range(2):
+        expert = holds(own ^ q)
+        gates = gates_of(expert)
+        chosen = (gates > 0.0).astype(jnp.float32)
+        exact = functools.partial(
+            jnp.dot, preferred_element_type=jnp.float32, precision=lax.Precision.HIGHEST
+        )
+        totals = jnp.sum(chosen, axis=1, keepdims=True)
+        ahead = exact(before, jnp.broadcast_to(totals, (devices, tok_rows)))
+        rank = exact(chosen, earlier) + ahead
+        other = gates_of(holds(new_ref[expert]))
+        home_total = jnp.sum(jnp.where(home & (other > 0.0), 1.0, 0.0))
+        home_rows = ((home_total.astype(jnp.int32) + (BLOCK - 1)) // BLOCK) * BLOCK
+        base = jnp.where(kind == 0, 0, home_rows)
+        position = rank.astype(jnp.int32) + base
+        served = jnp.where(position < SERVE_BLOCKS * BLOCK, gates, 0.0)
+        out_ref[q] = served.T
+
+
+def expert_kernel(blocks, info_ref, gates_ref, *refs):
+    halves = 2 * blocks
+    x_refs = refs[:halves]
+    weights = refs[halves : halves + 6]
+    out_refs = refs[halves + 6 : 2 * halves + 6]
+    x_all, total, partial = refs[2 * halves + 6 :]
+    q, f = pl.program_id(0), pl.program_id(1)
+    last = pl.num_programs(1) - 1
+    half = x_refs[0].shape[0]
+
+    @pl.when((q == 0) & (f == 0))
+    def _():
+        for i in range(halves):
+            x_all[i * half : (i + 1) * half, :] = x_refs[i][...]
+
+    def step(gate_ref, up_ref, down_ref):
+        x = x_all[...]
+        gate = jnp.dot(x, gate_ref[0], preferred_element_type=jnp.float32)
+        up = jnp.dot(x, up_ref[0], preferred_element_type=jnp.float32)
+        hidden = (gate / (1.0 + jnp.exp(-gate)) * up).astype(jnp.bfloat16)
+        part = jnp.dot(hidden, down_ref[0], preferred_element_type=jnp.float32)
+
+        @pl.when(f == 0)
+        def _():
+            partial[...] = part
+
+        @pl.when(f != 0)
+        def _():
+            partial[...] += part
+
+    @pl.when(q == 0)
+    def _():
+        step(*weights[:3])
+
+    @pl.when(q == 1)
+    def _():
+        step(*weights[3:])
+
+    def column(block):
+        table = gates_ref[q]
+        lane = lax.broadcasted_iota(jnp.int32, table.shape, 1)
+        return jnp.sum(jnp.where(lane == info_ref[block], table, 0.0), axis=1, keepdims=True)
+
+    @pl.when(f == last)
+    def _():
+        for block in range(blocks):
+            rows = slice(block * 2 * half, (block + 1) * 2 * half)
+            made = partial[rows, :].astype(jnp.bfloat16).astype(jnp.float32) * column(block)
+
+            @pl.when(q == 0)
+            def _():
+                total[rows, :] = made
+
+            @pl.when(q == 1)
+            def _():
+                whole = (total[rows, :] + made).astype(jnp.bfloat16)
+                out_refs[2 * block][...] = whole[:half]
+                out_refs[2 * block + 1][...] = whole[half:]
+
+
+def expert_call(halves, columns, gates, weights):
+    blocks = len(halves) // 2
+    half, width = halves[0].shape
+    own_in, own_out, other_in, other_out = weights
+    hidden_units = own_out.shape[1]
+    tile = 256
+    steps = hidden_units // tile
+    whole = pl.BlockSpec((half, width), lambda q, f, info: (0, 0))
+
+    def own(shift):
+        return lambda q, f, info: (0, 0, jnp.where(q == 0, f, steps - 1) + shift)
+
+    def other(shift):
+        return lambda q, f, info: (0, 0, jnp.where(q == 0, 0, f) + shift)
+
+    return pl.pallas_call(
+        functools.partial(expert_kernel, blocks),
+        out_shape=[jax.ShapeDtypeStruct((half, width), jnp.bfloat16)] * len(halves),
+        grid_spec=pltpu.PrefetchScalarGridSpec(
+            num_scalar_prefetch=1,
+            grid=(2, steps),
+            in_specs=[pl.BlockSpec(gates.shape, lambda q, f, info: (0, 0, 0))]
+            + [whole] * len(halves)
+            + [
+                pl.BlockSpec((1, width, tile), own(0)),
+                pl.BlockSpec((1, width, tile), own(steps)),
+                pl.BlockSpec((1, tile, width), lambda q, f, info: (0, jnp.where(q == 0, f, steps - 1), 0)),
+                pl.BlockSpec((1, width, tile), other(0)),
+                pl.BlockSpec((1, width, tile), other(steps)),
+                pl.BlockSpec((1, tile, width), lambda q, f, info: (0, jnp.where(q == 0, 0, f), 0)),
+            ],
+            out_specs=[whole] * len(halves),
+            scratch_shapes=[
+                pltpu.VMEM((half * len(halves), width), jnp.bfloat16),
+                pltpu.VMEM((half * len(halves), width), jnp.float32),
+                pltpu.VMEM((half * len(halves), width), jnp.float32),
+            ],
+        ),
+        compiler_params=pltpu.CompilerParams(vmem_limit_bytes=40 * 2**20),
+        cost_estimate=pl.CostEstimate(
+            flops=2 * 2 * half * len(halves) * width * 3 * hidden_units,
+            bytes_accessed=2 * 3 * 2 * width * hidden_units,
+            transcendentals=0,
+        ),
+    )(columns, gates, *halves, own_in, own_in, own_out, other_in, other_in, other_out)
+
+
+def gathered_body(tokens, expert_ids, route_gates, expert_in, expert_out, old_place, new_place):
+    ep_size = lax.axis_size("ep")
+    devices = ep_size * 2
+    tok_rows, top_count = expert_ids.shape
+    half = tok_rows // 2
+    reach = ep_size // 2
+    ring = [*range(0, ep_size, 2), *range(ep_size - 1, 0, -2)]
+    ahead = [(ring[i], ring[(i + 1) % ep_size]) for i in range(ep_size)]
+    back = [(b, a) for a, b in ahead]
+    ep = lax.axis_index("ep")
+    own = ep * 2 + lax.axis_index("dp")
+
+    def swap_cores(x):
+        return lax.ppermute(x, "dp", [(0, 1), (1, 0)])
+
+    def go(x, way):
+        return lax.ppermute(x, "ep", ahead if way > 0 else back)
+
+    ids_t, gates_t = expert_ids.T, route_gates.T
+    experts = jnp.arange(devices, dtype=jnp.int32)
+    dense = jnp.sum(
+        jnp.where(ids_t[None] == experts[:, None, None], gates_t[None], 0.0), axis=1
+    )[None]
+    dense = jnp.concatenate([dense, swap_cores(dense)])
+    bit = 1
+    while bit < ep_size:
+        pairs = [(i, i ^ bit) for i in range(ep_size)]
+        dense = jnp.concatenate([dense, lax.ppermute(dense, "ep", pairs)])
+        bit *= 2
+
+    weights = (expert_in, expert_out, swap_cores(expert_in), swap_cores(expert_out))
+
+    held = {0: [tokens[:half], tokens[half:]]}
+    for d in range(1, reach):
+        held[-d] = [go(x, 1) for x in held[1 - d]]
+        held[d] = [go(x, -1) for x in held[d - 1]]
+    held[reach] = [go(held[1 - reach][0], 1), go(held[reach - 1][1], -1)]
+
+    gates = pl.pallas_call(
+        gate_kernel,
+        out_shape=jax.ShapeDtypeStruct((2, tok_rows, devices), jnp.float32),
+        in_specs=[pl.BlockSpec(memory_space=pltpu.SMEM)] * 3
+        + [pl.BlockSpec(memory_space=pltpu.VMEM)],
+    )(own.reshape(1), old_place, new_place, dense)
+
+    ring_at = jnp.array(ring, jnp.int32)
+    place = jnp.sum(jnp.where(ring_at == ep, jnp.arange(ep_size, dtype=jnp.int32), 0))
+
+    def columns(distances):
+        at = (place + jnp.array(distances, jnp.int32)) % ep_size
+        there = jnp.sum(
+            jnp.where(at[:, None] == jnp.arange(ep_size)[None], ring_at[None], 0), axis=1
+        )
+        return ((there ^ ep) * 2).astype(jnp.int32)
+
+    groups = [[0, -1, 1], [-2, 2], [-3, 3, 4]]
+    part = {}
+    for group in groups:
+        outs = expert_call([x for d in group for x in held[d]], columns(group), gates, weights)
+        for i, d in enumerate(group):
+            part[d] = outs[2 * i : 2 * i + 2]
+
+    def add(*xs):
+        return sum(x.astype(jnp.float32) for x in xs).astype(jnp.bfloat16)
+
+    sums = {(1, 0): part[reach][0], (-1, 1): part[reach][1]}
+    sums = {k: go(x, k[0]) for k, x in sums.items()}
+    for d in range(reach - 1, 0, -1):
+        for way in (1, -1):
+            for h in (0, 1):
+                mine = part[way * d][h]
+                so_far = sums.get((way, h))
+                sums[way, h] = go(mine if so_far is None else add(so_far, mine), way)
+    return jnp.concatenate(
+        [add(part[0][h], sums[1, h], sums[-1, h]) for h in (0, 1)]
+    )
+
+
 def solution(mesh):
     placed = (
         P(("grp", "ep", "dp"), None),
@@ -122,6 +353,12 @@
         P(),
         P(),
     )
+
+    def body(tokens, expert_ids, *rest):
+        devices = lax.axis_size("ep") * lax.axis_size("dp")
+        gathered = devices <= 2 * expert_ids.shape[1]
+        return (gathered_body if gathered else routed_body)(tokens, expert_ids, *rest)
+
     return jax.shard_map(
         body, mesh=mesh, in_specs=placed, out_specs=P(("grp", "ep", "dp"), None), check_vma=False
     )

time: 442 us -> 154 us (0.35)
  the two profiles are of different devices: /device:TPU:11 before, /device:TPU:0 now
where the time goes in v1:
time: 154 us; the launch traced here: 153 us
  waiting for transfers between devices  50.2 us (33%)
  Pallas kernels  48 us (31%)
  starting transfers between devices  35.6 us (23%)
  local copies, waits for them, and re-layouts  9.91 us (6%)
  other arithmetic  9.12 us (6%)
    pallas_call x3, Pallas kernels, expert_call(): pl.pallas_call(functools.partial(expert_kernel, blocks), out_shape=[jax.S...  44.8 us
    ppermute x28, waiting for transfers between devices, go(): return lax.ppermute(x, 'ep', ahead if way > 0 else back)  40.6 us
    ppermute x28, starting transfers between devices, go(): return lax.ppermute(x, 'ep', ahead if way > 0 else back)  28.8 us
    unnamed x24, local copies, waits for them, and re-layouts  7.29 us
    ppermute x3, starting transfers between devices, gathered_body(): dense = jnp.concatenate([dense, lax.ppermute(dense, 'ep', pairs)])  5.78 us
    ppermute x3, waiting for transfers between devices, swap_cores(): return lax.ppermute(x, 'dp', [(0, 1), (1, 0)])  5.65 us
    ppermute x3, waiting for transfers between devices, gathered_body(): dense = jnp.concatenate([dense, lax.ppermute(dense, 'ep', pairs)])  3.94 us
    pallas_call x1, Pallas kernels, gathered_body(): pl.pallas_call(gate_kernel, out_shape=jax.ShapeDtypeStruct((2, tok_rows,...  3.17 us
  transfers between devices with their start and end apart: 34, of which 18 were waited for; matrix products, arithmetic and copies ran while one was open for 8% of the time, Pallas kernels for 21%

profile of v1, /device:TPU:0, one launch (start us, length us, event | category | flops | bytes accessed | tf_op | source)
XLA Modules:
  0.0 153.0 jit_solution(8362111679174126006)
XLA Ops:
  0.0 0.5 collective-permute-start.8
  0.5 0.7 select_reduce_fusion
  1.2 0.5 collective-permute-start
  1.8 1.8 %fusion.5 = (bf16[64,2048]{1,0:T(8,128)(2,1)S(1)}, bf16[64,2048]{1,0:T(8,128)(2,1)}) fusion(bf16[128,2048]{1,0:T(8,128)(2,1)} %param.11), kind=kLoop, calls=%fused_computation.46 | loop fusion | bytes 1048576 | tf_op jit(solution)/shard_map/slice | solution.py:300
  3.5 2.6 %collective-permute-start.4 = (bf16[64,2048]{1,0:T(8,128)(2,1)}, bf16[64,2048]{1,0:T(8,128)(2,1)}, u32[]{:S(2)}, u32[]{:S(2)}) collective-permute-start(bf16[64,2048]{1,0:T(8,128)(2,1)} %get-tuple-element.40.refs_0_), channel_id=1, source_target_pairs={{0,4},{4,8},{8,12},{12,14},{14,10},{10,6},{6,2},{2,0},{1,5},{5,9},... | collective-permute-start | bytes 786440 | tf_op jit(solution)/shard_map/ppermute | solution.py:284
  6.1 1.6 %collective-permute-start.5 = (bf16[64,2048]{1,0:T(8,128)(2,1)S(1)}, bf16[64,2048]{1,0:T(8,128)(2,1)}, u32[]{:S(2)}, u32[]{:S(2)}) collective-permute-start(bf16[64,2048]{1,0:T(8,128)(2,1)S(1)} %get-tuple-element.39.refs_1_), channel_id=1, source_target_pairs={{0,4},{4,8},{8,12},{12,14},{14,10},{10,6},{6,2},{2,0},{1,5},{5,9},... | collective-permute-start | bytes 786440 | tf_op jit(solution)/shard_map/ppermute | solution.py:284
  7.7 1.3 fusion.4
  9.0 5.6 %collective-permute-done = f32[1,16,128]{2,1,0:T(8,128)S(1)} collective-permute-done((f32[1,16,128]{2,1,0:T(8,128)S(1)}, f32[1,16,128]{2,1,0:T(8,128)S(1)}, u32[]{:S(2)}, u32[]{:S(2)}) %collective-permute-start) | collective-permute-done | bytes 8224 | tf_op jit(solution)/shard_map/ppermute | solution.py:281
  14.7 2.0 %collective-permute-start.1 = (f32[2,16,128]{2,1,0:T(8,128)S(1)}, f32[2,16,128]{2,1,0:T(8,128)S(1)}, u32[]{:S(2)}, u32[]{:S(2)}) collective-permute-start(f32[2,16,128]{2,1,0:T(8,128)S(1)} %pad_maximum_fusion.3), channel_id=1, source_target_pairs={{0,2},{2,0},{4,6},{6,4},{8,10},{10,8},{12,14},{14,12},{1,3},{3,1},... | collective-permute-start | bytes 49160 | tf_op jit(solution)/shard_map/ppermute | solution.py:295
  16.7 1.3 and_select_fusion.1
  18.0 1.2 collective-permute-done.1
  19.2 1.3 collective-permute-start.2
  20.5 1.3 and_select_fusion
  21.8 1.3 collective-permute-done.2
  23.1 2.4 %collective-permute-start.3 = (f32[8,16,128]{2,1,0:T(8,128)S(1)}, f32[8,16,128]{2,1,0:T(8,128)S(1)}, u32[]{:S(2)}, u32[]{:S(2)}) collective-permute-start(f32[8,16,128]{2,1,0:T(8,128)S(1)} %pad_maximum_fusion.1), channel_id=1, source_target_pairs={{0,8},{2,10},{4,12},{6,14},{8,0},{10,2},{12,4},{14,6},{1,9},{3,11}... | collective-permute-start | bytes 196616 | tf_op jit(solution)/shard_map/ppermute | solution.py:295
  25.5 1.4 select_reduce_fusion.1
  26.9 1.5 collective-permute-done.3
  28.3 1.2 collective-permute-start.6
  29.6 1.7 %collective-permute-start.7 = (bf16[64,2048]{1,0:T(8,128)(2,1)S(1)}, bf16[64,2048]{1,0:T(8,128)(2,1)}, u32[]{:S(2)}, u32[]{:S(2)}) collective-permute-start(bf16[64,2048]{1,0:T(8,128)(2,1)S(1)} %get-tuple-element.39.refs_1_), channel_id=1, source_target_pairs={{4,0},{8,4},{12,8},{14,12},{10,14},{6,10},{2,6},{0,2},{5,1},{9,5},... | collective-permute-start | bytes 786440 | tf_op jit(solution)/shard_map/ppermute | solution.py:284
  31.3 0.3 collective-permute-start.10
  31.6 0.8 fusion
  32.5 5.4 %collective-permute-done.6.refs_4_ = bf16[64,2048]{1,0:T(8,128)(2,1)} collective-permute-done((bf16[64,2048]{1,0:T(8,128)(2,1)}, bf16[64,2048]{1,0:T(8,128)(2,1)}, u32[]{:S(2)}, u32[]{:S(2)}) %collective-permute-start.6) | collective-permute-done | bytes 262176 | tf_op jit(solution)/shard_map/ppermute | solution.py:284
  37.9 0.5 collective-permute-start.12
  38.4 2.5 %collective-permute-done.7.refs_5_ = bf16[64,2048]{1,0:T(8,128)(2,1)} collective-permute-done((bf16[64,2048]{1,0:T(8,128)(2,1)S(1)}, bf16[64,2048]{1,0:T(8,128)(2,1)}, u32[]{:S(2)}, u32[]{:S(2)}) %collective-permute-start.7) | collective-permute-done | bytes 262176 | tf_op jit(solution)/shard_map/ppermute | solution.py:284
  40.9 0.6 collective-permute-start.14
  41.5 1.9 %collective-permute-start.16 = (bf16[64,2048]{1,0:T(8,128)(2,1)}, bf16[64,2048]{1,0:T(8,128)(2,1)}, u32[]{:S(2)}, u32[]{:S(2)}) collective-permute-start(bf16[64,2048]{1,0:T(8,128)(2,1)} %collective-permute-done.7.refs_5_), channel_id=1, source_target_pairs={{4,0},{8,4},{12,8},{14,12},{10,14},{6,10},{2,6},{0,2},{5,1},{9,5},... | collective-permute-start | bytes 786440 | tf_op jit(solution)/shard_map/ppermute | solution.py:284
  43.5 1.8 %collective-permute-done.12.refs_1_ = bf16[64,2048]{1,0:T(8,128)(2,1)} collective-permute-done((bf16[64,2048]{1,0:T(8,128)(2,1)}, bf16[64,2048]{1,0:T(8,128)(2,1)}, u32[]{:S(2)}, u32[]{:S(2)}) %collective-permute-start.12) | collective-permute-done | bytes 262176 | tf_op jit(solution)/shard_map/ppermute | solution.py:284
  45.3 1.4 collective-permute-start.11
  46.6 3.1 %collective-permute-done.14.refs_2_ = bf16[64,2048]{1,0:T(8,128)(2,1)} collective-permute-done((bf16[64,2048]{1,0:T(8,128)(2,1)}, bf16[64,2048]{1,0:T(8,128)(2,1)}, u32[]{:S(2)}, u32[]{:S(2)}) %collective-permute-start.14) | collective-permute-done | bytes 262176 | tf_op jit(solution)/shard_map/ppermute | solution.py:284
  49.8 3.2 %collective-permute-done.16.refs_3_ = bf16[64,2048]{1,0:T(8,128)(2,1)} collective-permute-done((bf16[64,2048]{1,0:T(8,128)(2,1)}, bf16[64,2048]{1,0:T(8,128)(2,1)}, u32[]{:S(2)}, u32[]{:S(2)}) %collective-permute-start.16) | collective-permute-done | bytes 262176 | tf_op jit(solution)/shard_map/ppermute | solution.py:284
  53.3 0.6 xor_multiply_fusion.1.info_ref
  53.9 0.7 constant_dynamic-update-slice_fusion.3
  54.6 2.2 %collective-permute-start.15 = (bf16[64,2048]{1,0:T(8,128)(2,1)}, bf16[64,2048]{1,0:T(8,128)(2,1)}, u32[]{:S(2)}, u32[]{:S(2)}) collective-permute-start(bf16[64,2048]{1,0:T(8,128)(2,1)} %collective-permute-done.14.refs_2_), channel_id=1, source_target_pairs={{4,0},{8,4},{12,8},{14,12},{10,14},{6,10},{2,6},{0,2},{5,1},{9,5},... | collective-permute-start | bytes 786440 | tf_op jit(solution)/shard_map/ppermute | solution.py:284
  56.8 1.0 collective-permute-done.13.refs_1_
  57.8 0.7 copy-done.3
  58.5 4.1 %collective-permute-done.17.refs_3_ = bf16[64,2048]{1,0:T(8,128)(2,1)} collective-permute-done((bf16[64,2048]{1,0:T(8,128)(2,1)}, bf16[64,2048]{1,0:T(8,128)(2,1)}, u32[]{:S(2)}, u32[]{:S(2)}) %collective-permute-start.17) | collective-permute-done | bytes 262176 | tf_op jit(solution)/shard_map/ppermute | solution.py:284
  62.6 0.3 collective-permute-start.19
  62.9 0.7 constant_dynamic-update-slice_fusion.2
  63.6 0.8 constant_dynamic-update-slice_fusion.1
  64.3 0.8 constant_dynamic-update-slice_fusion.dense_ref
  65.2 0.6 copy-done.5
  65.8 3.2 %shard_map.109.gates_ref = f32[2,128,16]{2,1,0:T(8,128)} custom-call(s32[1]{0:T(128)} %bitcast.info_ref, s32[16]{0:T(128)} %old_ref.1, s32[16]{0:T(128)} %new_ref.1, f32[16,16,128]{2,1,0:T(8,128)} %copy-done.5), custom_call_target="tpu_custom_call" | custom-call | tf_op jit(solution)/shard_map/pallas_call | solution.py:306
  69.0 0.4 collective-permute-done.19.refs_5_
  69.4 1.9 %copy-done = bf16[1,768,2048]{2,1,0:T(8,128)(2,1)S(1)} copy-done((bf16[1,768,2048]{2,1,0:T(8,128)(2,1)S(1)}, bf16[1,768,2048]{2,1,0:T(8,128)(2,1)}, u32[]{:S(2)}) %copy-start) | copy-done | bytes 3145752
  71.3 0.9 copy-done.2
  72.2 0.9 copy-done.4
  73.2 16.1 %shard_map.111 = (bf16[64,2048]{1,0:T(8,128)(2,1)S(1)}, bf16[64,2048]{1,0:T(8,128)(2,1)S(1)}, bf16[64,2048]{1,0:T(8,128)(2,1)S(1)}, bf16[64,2048]{1,0:T(8,128)(2...) custom-call(s32[3]{0:T(128)S(1)} %xor_multiply_fusion.1.info_ref, f32[2,128,16]{2,1,0:T(8,128)S(1)} %copy-done.2, ...), custom_call_target="tpu_custom_call" | custom-call | flops 7247757312 | bytes 18874368 | tf_op jit(solution)/shard_map/pallas_call | solution.py:236
  89.3 1.9 %collective-permute-start.30 = (bf16[64,2048]{1,0:T(8,128)(2,1)S(1)}, bf16[64,2048]{1,0:T(8,128)(2,1)S(1)}, u32[]{:S(2)}, u32[]{:S(2)}) collective-permute-start(bf16[64,2048]{1,0:T(8,128)(2,1)S(1)} %get-tuple-element.33), channel_id=1, source_target_pairs={{4,0},{8,4},{12,8},{14,12},{10,14},{6,10},{2,6},{0,2},{5,1},{9,5},... | collective-permute-start | bytes 786440 | tf_op jit(solution)/shard_map/ppermute | solution.py:284
  91.4 1.8 %collective-permute-start.24 = (bf16[64,2048]{1,0:T(8,128)(2,1)S(1)}, bf16[64,2048]{1,0:T(8,128)(2,1)S(1)}, u32[]{:S(2)}, u32[]{:S(2)}) collective-permute-start(bf16[64,2048]{1,0:T(8,128)(2,1)S(1)} %get-tuple-element.26), channel_id=1, source_target_pairs={{4,0},{8,4},{12,8},{14,12},{10,14},{6,10},{2,6},{0,2},{5,1},{9,5},... | collective-permute-start | bytes 786440 | tf_op jit(solution)/shard_map/ppermute | solution.py:284
  93.4 15.8 %shard_map.110 = (bf16[64,2048]{1,0:T(8,128)(2,1)S(1)}, bf16[64,2048]{1,0:T(8,128)(2,1)S(1)}, bf16[64,2048]{1,0:T(8,128)(2,1)S(1)}, bf16[64,2048]{1,0:T(8,128)(2...) custom-call(s32[3]{0:T(128)S(1)} %xor_multiply_fusion.2.info_ref, f32[2,128,16]{2,1,0:T(8,128)S(1)} %copy-done.2, ...), custom_call_target="tpu_custom_call" | custom-call | flops 7247757312 | bytes 18874368 | tf_op jit(solution)/shard_map/pallas_call | solution.py:236
  109.2 12.9 %shard_map.112 = (bf16[64,2048]{1,0:T(8,128)(2,1)S(1)}, bf16[64,2048]{1,0:T(8,128)(2,1)S(1)}, bf16[64,2048]{1,0:T(8,128)(2,1)S(1)}, bf16[64,2048]{1,0:T(8,128)(2,1)S(1)}) custom-call(s32[2]{0:T(128)S(1)} %xor_multiply_fusion.info_ref, f32[2,128,16]{2,1,0:T(8,128)S(1)} %copy-done.2, bf16[64,2048]{1,0:T(8,128)(2,1)} %collective-permute-done.10.refs_0_, ...), custom_call_target="tpu_custom_call" | custom-call | flops 4831838208 | bytes 18874368 | tf_op jit(solution)/shard_map/pallas_call | solution.py:236
  122.2 1.9 %collective-permute-start.31 = (bf16[64,2048]{1,0:T(8,128)(2,1)S(1)}, bf16[64,2048]{1,0:T(8,128)(2,1)S(1)}, u32[]{:S(2)}, u32[]{:S(2)}) collective-permute-start(bf16[64,2048]{1,0:T(8,128)(2,1)S(1)} %add_convert_fusion.3), channel_id=1, source_target_pairs={{4,0},{8,4},{12,8},{14,12},{10,14},{6,10},{2,6},{0,2},{5,1},{9,5},... | collective-permute-start | bytes 786440 | tf_op jit(solution)/shard_map/ppermute | solution.py:284
  124.5 1.9 %collective-permute-start.25 = (bf16[64,2048]{1,0:T(8,128)(2,1)S(1)}, bf16[64,2048]{1,0:T(8,128)(2,1)S(1)}, u32[]{:S(2)}, u32[]{:S(2)}) collective-permute-start(bf16[64,2048]{1,0:T(8,128)(2,1)S(1)} %add_convert_fusion.8), channel_id=1, source_target_pairs={{4,0},{8,4},{12,8},{14,12},{10,14},{6,10},{2,6},{0,2},{5,1},{9,5},... | collective-permute-start | bytes 786440 | tf_op jit(solution)/shard_map/ppermute | solution.py:284
  126.7 4.8 %collective-permute-done.31 = bf16[64,2048]{1,0:T(8,128)(2,1)S(1)} collective-permute-done((bf16[64,2048]{1,0:T(8,128)(2,1)S(1)}, bf16[64,2048]{1,0:T(8,128)(2,1)S(1)}, u32[]{:S(2)}, u32[]{:S(2)}) %collective-permute-start.31) | collective-permute-done | bytes 262176 | tf_op jit(solution)/shard_map/ppermute | solution.py:284
  131.6 1.9 %collective-permute-start.32 = (bf16[64,2048]{1,0:T(8,128)(2,1)S(1)}, bf16[64,2048]{1,0:T(8,128)(2,1)S(1)}, u32[]{:S(2)}, u32[]{:S(2)}) collective-permute-start(bf16[64,2048]{1,0:T(8,128)(2,1)S(1)} %add_convert_fusion.2), channel_id=1, source_target_pairs={{4,0},{8,4},{12,8},{14,12},{10,14},{6,10},{2,6},{0,2},{5,1},{9,5},... | collective-permute-start | bytes 786440 | tf_op jit(solution)/shard_map/ppermute | solution.py:284
  133.8 3.3 %collective-permute-done.25 = bf16[64,2048]{1,0:T(8,128)(2,1)S(1)} collective-permute-done((bf16[64,2048]{1,0:T(8,128)(2,1)S(1)}, bf16[64,2048]{1,0:T(8,128)(2,1)S(1)}, u32[]{:S(2)}, u32[]{:S(2)}) %collective-permute-start.25) | collective-permute-done | bytes 262176 | tf_op jit(solution)/shard_map/ppermute | solution.py:284
  137.2 1.9 %collective-permute-start.26 = (bf16[64,2048]{1,0:T(8,128)(2,1)S(1)}, bf16[64,2048]{1,0:T(8,128)(2,1)S(1)}, u32[]{:S(2)}, u32[]{:S(2)}) collective-permute-start(bf16[64,2048]{1,0:T(8,128)(2,1)S(1)} %add_convert_fusion.7), channel_id=1, source_target_pairs={{4,0},{8,4},{12,8},{14,12},{10,14},{6,10},{2,6},{0,2},{5,1},{9,5},... | collective-permute-start | bytes 786440 | tf_op jit(solution)/shard_map/ppermute | solution.py:284
  139.4 2.5 %collective-permute-done.32 = bf16[64,2048]{1,0:T(8,128)(2,1)S(1)} collective-permute-done((bf16[64,2048]{1,0:T(8,128)(2,1)S(1)}, bf16[64,2048]{1,0:T(8,128)(2,1)S(1)}, u32[]{:S(2)}, u32[]{:S(2)}) %collective-permute-start.32) | collective-permute-done | bytes 262176 | tf_op jit(solution)/shard_map/ppermute | solution.py:284
  142.0 0.4 collective-permute-start.33
  142.4 3.2 %collective-permute-done.22 = bf16[64,2048]{1,0:T(8,128)(2,1)S(1)} collective-permute-done((bf16[64,2048]{1,0:T(8,128)(2,1)S(1)}, bf16[64,2048]{1,0:T(8,128)(2,1)S(1)}, u32[]{:S(2)}, u32[]{:S(2)}) %collective-permute-start.22) | collective-permute-done | bytes 262176 | tf_op jit(solution)/shard_map/ppermute | solution.py:284
  145.6 1.1 collective-permute-start.23
  146.7 1.7 %collective-permute-done.33 = bf16[64,2048]{1,0:T(8,128)(2,1)S(1)} collective-permute-done((bf16[64,2048]{1,0:T(8,128)(2,1)S(1)}, bf16[64,2048]{1,0:T(8,128)(2,1)S(1)}, u32[]{:S(2)}, u32[]{:S(2)}) %collective-permute-start.33) | collective-permute-done | bytes 262176 | tf_op jit(solution)/shard_map/ppermute | solution.py:284
  148.5 3.5 %collective-permute-done.23 = bf16[64,2048]{1,0:T(8,128)(2,1)S(1)} collective-permute-done((bf16[64,2048]{1,0:T(8,128)(2,1)S(1)}, bf16[64,2048]{1,0:T(8,128)(2,1)S(1)}, u32[]{:S(2)}, u32[]{:S(2)}) %collective-permute-start.23) | collective-permute-done | bytes 262176 | tf_op jit(solution)/shard_map/ppermute | solution.py:284
  152.2 0.8 pad_maximum_fusion
  (59 shorter events, 2.6 us)
Async XLA Ops:
  0.0 69.4 %collective-permute-start.8 = (bf16[1,2048,1536]{2,1,0:T(8,128)(2,1)}, bf16[1,2048,1536]{2,1,0:T(8,128)(2,1)}, u32[]{:S(2)}, u32[]{:S(2)}) collective-permute-start(bf16[1,2048,1536]{2,1,0:T(8,128)(2,1)} %refs_5_.1), channel_id=1, source_target_pairs={{0,1},{1,0},{2,3},{3,2},{4,5},{5,4},{6,7},{7,6},{8,9},{9,8},{10,11... | collective-permute-start | bytes 18874376 | tf_op jit(solution)/shard_map/ppermute | solution.py:281
  0.5 69.0 %collective-permute-start.9 = (bf16[1,768,2048]{2,1,0:T(8,128)(2,1)}, bf16[1,768,2048]{2,1,0:T(8,128)(2,1)S(1)}, u32[]{:S(2)}, u32[]{:S(2)}) collective-permute-start(bf16[1,768,2048]{2,1,0:T(8,128)(2,1)} %refs_6_.5), channel_id=1, source_target_pairs={{0,1},{1,0},{2,3},{3,2},{4,5},{5,4},{6,7},{7,6},{8,9},{9,8},{10,11... | collective-permute-start | bytes 9437192 | tf_op jit(solution)/shard_map/ppermute | solution.py:281
  1.2 13.4 %collective-permute-start = (f32[1,16,128]{2,1,0:T(8,128)S(1)}, f32[1,16,128]{2,1,0:T(8,128)S(1)}, u32[]{:S(2)}, u32[]{:S(2)}) collective-permute-start(f32[1,16,128]{2,1,0:T(8,128)S(1)} %bitcast.5), channel_id=1, source_target_pairs={{0,1},{1,0},{2,3},{3,2},{4,5},{5,4},{6,7},{7,6},{8,9},{9,8},{10,11... | collective-permute-start | bytes 24584 | tf_op jit(solution)/shard_map/ppermute | solution.py:281
  3.5 26.1 %collective-permute-start.4 = (bf16[64,2048]{1,0:T(8,128)(2,1)}, bf16[64,2048]{1,0:T(8,128)(2,1)}, u32[]{:S(2)}, u32[]{:S(2)}) collective-permute-start(bf16[64,2048]{1,0:T(8,128)(2,1)} %get-tuple-element.40.refs_0_), channel_id=1, source_target_pairs={{0,4},{4,8},{8,12},{12,14},{14,10},{10,6},{6,2},{2,0},{1,5},{5,9},... | collective-permute-start | bytes 786440 | tf_op jit(solution)/shard_map/ppermute | solution.py:284
  6.1 25.2 %collective-permute-start.5 = (bf16[64,2048]{1,0:T(8,128)(2,1)S(1)}, bf16[64,2048]{1,0:T(8,128)(2,1)}, u32[]{:S(2)}, u32[]{:S(2)}) collective-permute-start(bf16[64,2048]{1,0:T(8,128)(2,1)S(1)} %get-tuple-element.39.refs_1_), channel_id=1, source_target_pairs={{0,4},{4,8},{8,12},{12,14},{14,10},{10,6},{6,2},{2,0},{1,5},{5,9},... | collective-permute-start | bytes 786440 | tf_op jit(solution)/shard_map/ppermute | solution.py:284
  14.6 17.8 %copy-start.8 = (f32[1,16,128]{2,1,0:T(8,128)}, f32[1,16,128]{2,1,0:T(8,128)S(1)}, u32[]{:S(2)}) copy-start(f32[1,16,128]{2,1,0:T(8,128)S(1)} %collective-permute-done) | copy-start | bytes 24580
  14.7 4.5 %collective-permute-start.1 = (f32[2,16,128]{2,1,0:T(8,128)S(1)}, f32[2,16,128]{2,1,0:T(8,128)S(1)}, u32[]{:S(2)}, u32[]{:S(2)}) collective-permute-start(f32[2,16,128]{2,1,0:T(8,128)S(1)} %pad_maximum_fusion.3), channel_id=1, source_target_pairs={{0,2},{2,0},{4,6},{6,4},{8,10},{10,8},{12,14},{14,12},{1,3},{3,1},... | collective-permute-start | bytes 49160 | tf_op jit(solution)/shard_map/ppermute | solution.py:295
  19.2 22.4 %copy-start.6 = (f32[2,16,128]{2,1,0:T(8,128)}, f32[2,16,128]{2,1,0:T(8,128)S(1)}, u32[]{:S(2)}) copy-start(f32[2,16,128]{2,1,0:T(8,128)S(1)} %collective-permute-done.1) | copy-start | bytes 49156
  19.2 3.9 %collective-permute-start.2 = (f32[4,16,128]{2,1,0:T(8,128)S(1)}, f32[4,16,128]{2,1,0:T(8,128)S(1)}, u32[]{:S(2)}, u32[]{:S(2)}) collective-permute-start(f32[4,16,128]{2,1,0:T(8,128)S(1)} %pad_maximum_fusion.2), channel_id=1, source_target_pairs={{0,4},{2,6},{4,0},{6,2},{8,12},{10,14},{12,8},{14,10},{1,5},{3,7},... | collective-permute-start | bytes 98312 | tf_op jit(solution)/shard_map/ppermute | solution.py:295
  23.1 20.3 %copy-start.7 = (f32[4,16,128]{2,1,0:T(8,128)}, f32[4,16,128]{2,1,0:T(8,128)S(1)}, u32[]{:S(2)}) copy-start(f32[4,16,128]{2,1,0:T(8,128)S(1)} %collective-permute-done.2) | copy-start | bytes 98308
  23.1 5.2 %collective-permute-start.3 = (f32[8,16,128]{2,1,0:T(8,128)S(1)}, f32[8,16,128]{2,1,0:T(8,128)S(1)}, u32[]{:S(2)}, u32[]{:S(2)}) collective-permute-start(f32[8,16,128]{2,1,0:T(8,128)S(1)} %pad_maximum_fusion.1), channel_id=1, source_target_pairs={{0,8},{2,10},{4,12},{6,14},{8,0},{10,2},{12,4},{14,6},{1,9},{3,11}... | collective-permute-start | bytes 196616 | tf_op jit(solution)/shard_map/ppermute | solution.py:295
  28.3 15.1 %copy-start.9 = (f32[8,16,128]{2,1,0:T(8,128)}, f32[8,16,128]{2,1,0:T(8,128)S(1)}, u32[]{:S(2)}) copy-start(f32[8,16,128]{2,1,0:T(8,128)S(1)} %collective-permute-done.3) | copy-start | bytes 196612
  28.3 9.6 %collective-permute-start.6 = (bf16[64,2048]{1,0:T(8,128)(2,1)}, bf16[64,2048]{1,0:T(8,128)(2,1)}, u32[]{:S(2)}, u32[]{:S(2)}) collective-permute-start(bf16[64,2048]{1,0:T(8,128)(2,1)} %get-tuple-element.40.refs_0_), channel_id=1, source_target_pairs={{4,0},{8,4},{12,8},{14,12},{10,14},{6,10},{2,6},{0,2},{5,1},{9,5},... | collective-permute-start | bytes 786440 | tf_op jit(solution)/shard_map/ppermute | solution.py:284
  29.6 11.3 %collective-permute-start.7 = (bf16[64,2048]{1,0:T(8,128)(2,1)S(1)}, bf16[64,2048]{1,0:T(8,128)(2,1)}, u32[]{:S(2)}, u32[]{:S(2)}) collective-permute-start(bf16[64,2048]{1,0:T(8,128)(2,1)S(1)} %get-tuple-element.39.refs_1_), channel_id=1, source_target_pairs={{4,0},{8,4},{12,8},{14,12},{10,14},{6,10},{2,6},{0,2},{5,1},{9,5},... | collective-permute-start | bytes 786440 | tf_op jit(solution)/shard_map/ppermute | solution.py:284
  31.3 10.2 %collective-permute-start.10 = (bf16[64,2048]{1,0:T(8,128)(2,1)}, bf16[64,2048]{1,0:T(8,128)(2,1)}, u32[]{:S(2)}, u32[]{:S(2)}) collective-permute-start(bf16[64,2048]{1,0:T(8,128)(2,1)} %collective-permute-done.4.refs_2_), channel_id=1, source_target_pairs={{0,4},{4,8},{8,12},{12,14},{14,10},{10,6},{6,2},{2,0},{1,5},{5,9},... | collective-permute-start | bytes 786440 | tf_op jit(solution)/shard_map/ppermute | solution.py:284
  37.9 7.3 %collective-permute-start.12 = (bf16[64,2048]{1,0:T(8,128)(2,1)}, bf16[64,2048]{1,0:T(8,128)(2,1)}, u32[]{:S(2)}, u32[]{:S(2)}) collective-permute-start(bf16[64,2048]{1,0:T(8,128)(2,1)} %collective-permute-done.5.refs_3_), channel_id=1, source_target_pairs={{0,4},{4,8},{8,12},{12,14},{14,10},{10,6},{6,2},{2,0},{1,5},{5,9},... | collective-permute-start | bytes 786440 | tf_op jit(solution)/shard_map/ppermute | solution.py:284
  40.9 8.8 %collective-permute-start.14 = (bf16[64,2048]{1,0:T(8,128)(2,1)}, bf16[64,2048]{1,0:T(8,128)(2,1)}, u32[]{:S(2)}, u32[]{:S(2)}) collective-permute-start(bf16[64,2048]{1,0:T(8,128)(2,1)} %collective-permute-done.6.refs_4_), channel_id=1, source_target_pairs={{4,0},{8,4},{12,8},{14,12},{10,14},{6,10},{2,6},{0,2},{5,1},{9,5},... | collective-permute-start | bytes 786440 | tf_op jit(solution)/shard_map/ppermute | solution.py:284
  41.5 11.5 %collective-permute-start.16 = (bf16[64,2048]{1,0:T(8,128)(2,1)}, bf16[64,2048]{1,0:T(8,128)(2,1)}, u32[]{:S(2)}, u32[]{:S(2)}) collective-permute-start(bf16[64,2048]{1,0:T(8,128)(2,1)} %collective-permute-done.7.refs_5_), channel_id=1, source_target_pairs={{4,0},{8,4},{12,8},{14,12},{10,14},{6,10},{2,6},{0,2},{5,1},{9,5},... | collective-permute-start | bytes 786440 | tf_op jit(solution)/shard_map/ppermute | solution.py:284
  45.3 9.4 %collective-permute-start.11 = (bf16[64,2048]{1,0:T(8,128)(2,1)}, bf16[64,2048]{1,0:T(8,128)(2,1)}, u32[]{:S(2)}, u32[]{:S(2)}) collective-permute-start(bf16[64,2048]{1,0:T(8,128)(2,1)} %collective-permute-done.10.refs_0_), channel_id=1, source_target_pairs={{0,4},{4,8},{8,12},{12,14},{14,10},{10,6},{6,2},{2,0},{1,5},{5,9},... | collective-permute-start | bytes 786440 | tf_op jit(solution)/shard_map/ppermute | solution.py:284
  49.8 8.0 %collective-permute-start.13 = (bf16[64,2048]{1,0:T(8,128)(2,1)}, bf16[64,2048]{1,0:T(8,128)(2,1)S(1)}, u32[]{:S(2)}, u32[]{:S(2)}) collective-permute-start(bf16[64,2048]{1,0:T(8,128)(2,1)} %collective-permute-done.12.refs_1_), channel_id=1, source_target_pairs={{0,4},{4,8},{8,12},{12,14},{14,10},{10,6},{6,2},{2,0},{1,5},{5,9},... | collective-permute-start | bytes 786440 | tf_op jit(solution)/shard_map/ppermute | solution.py:284
  53.0 9.6 %collective-permute-start.17 = (bf16[64,2048]{1,0:T(8,128)(2,1)}, bf16[64,2048]{1,0:T(8,128)(2,1)}, u32[]{:S(2)}, u32[]{:S(2)}) collective-permute-start(bf16[64,2048]{1,0:T(8,128)(2,1)} %collective-permute-done.16.refs_3_), channel_id=1, source_target_pairs={{4,0},{8,4},{12,8},{14,12},{10,14},{6,10},{2,6},{0,2},{5,1},{9,5},... | collective-permute-start | bytes 786440 | tf_op jit(solution)/shard_map/ppermute | solution.py:284
  54.6 14.4 %collective-permute-start.15 = (bf16[64,2048]{1,0:T(8,128)(2,1)}, bf16[64,2048]{1,0:T(8,128)(2,1)}, u32[]{:S(2)}, u32[]{:S(2)}) collective-permute-start(bf16[64,2048]{1,0:T(8,128)(2,1)} %collective-permute-done.14.refs_2_), channel_id=1, source_target_pairs={{4,0},{8,4},{12,8},{14,12},{10,14},{6,10},{2,6},{0,2},{5,1},{9,5},... | collective-permute-start | bytes 786440 | tf_op jit(solution)/shard_map/ppermute | solution.py:284
  57.8 0.7 copy-start.3
  58.5 10.5 %collective-permute-start.18 = (bf16[64,2048]{1,0:T(8,128)(2,1)}, bf16[64,2048]{1,0:T(8,128)(2,1)}, u32[]{:S(2)}, u32[]{:S(2)}) collective-permute-start(bf16[64,2048]{1,0:T(8,128)(2,1)} %collective-permute-done.11.refs_0_), channel_id=1, source_target_pairs={{0,4},{4,8},{8,12},{12,14},{14,10},{10,6},{6,2},{2,0},{1,5},{5,9},... | collective-permute-start | bytes 786440 | tf_op jit(solution)/shard_map/ppermute | solution.py:284
  62.6 6.9 %collective-permute-start.19 = (bf16[64,2048]{1,0:T(8,128)(2,1)}, bf16[64,2048]{1,0:T(8,128)(2,1)}, u32[]{:S(2)}, u32[]{:S(2)}) collective-permute-start(bf16[64,2048]{1,0:T(8,128)(2,1)} %collective-permute-done.17.refs_3_), channel_id=1, source_target_pairs={{4,0},{8,4},{12,8},{14,12},{10,14},{6,10},{2,6},{0,2},{5,1},{9,5},... | collective-permute-start | bytes 786440 | tf_op jit(solution)/shard_map/ppermute | solution.py:284
  65.2 0.6 copy-start.5
  69.4 1.9 %copy-start = (bf16[1,768,2048]{2,1,0:T(8,128)(2,1)S(1)}, bf16[1,768,2048]{2,1,0:T(8,128)(2,1)}, u32[]{:S(2)}) copy-start(bf16[1,768,2048]{2,1,0:T(8,128)(2,1)} %refs_6_.5) | copy-start | bytes 9437188
  71.3 0.9 copy-start.2
  72.2 0.9 copy-start.4
  73.2 20.2 %copy-start.1 = (bf16[1,768,2048]{2,1,0:T(8,128)(2,1)S(1)}, bf16[1,768,2048]{2,1,0:T(8,128)(2,1)}, u32[]{:S(2)}) copy-start(bf16[1,768,2048]{2,1,0:T(8,128)(2,1)} %refs_6_.5) | copy-start | bytes 9437188
  89.3 32.8 %collective-permute-start.30 = (bf16[64,2048]{1,0:T(8,128)(2,1)S(1)}, bf16[64,2048]{1,0:T(8,128)(2,1)S(1)}, u32[]{:S(2)}, u32[]{:S(2)}) collective-permute-start(bf16[64,2048]{1,0:T(8,128)(2,1)S(1)} %get-tuple-element.33), channel_id=1, source_target_pairs={{4,0},{8,4},{12,8},{14,12},{10,14},{6,10},{2,6},{0,2},{5,1},{9,5},... | collective-permute-start | bytes 786440 | tf_op jit(solution)/shard_map/ppermute | solution.py:284
  91.2 32.9 %collective-permute-start.27 = (bf16[64,2048]{1,0:T(8,128)(2,1)S(1)}, bf16[64,2048]{1,0:T(8,128)(2,1)S(1)}, u32[]{:S(2)}, u32[]{:S(2)}) collective-permute-start(bf16[64,2048]{1,0:T(8,128)(2,1)S(1)} %get-tuple-element.30), channel_id=1, source_target_pairs={{0,4},{4,8},{8,12},{12,14},{14,10},{10,6},{6,2},{2,0},{1,5},{5,9},... | collective-permute-start | bytes 786440 | tf_op jit(solution)/shard_map/ppermute | solution.py:284
  91.4 33.0 %collective-permute-start.24 = (bf16[64,2048]{1,0:T(8,128)(2,1)S(1)}, bf16[64,2048]{1,0:T(8,128)(2,1)S(1)}, u32[]{:S(2)}, u32[]{:S(2)}) collective-permute-start(bf16[64,2048]{1,0:T(8,128)(2,1)S(1)} %get-tuple-element.26), channel_id=1, source_target_pairs={{4,0},{8,4},{12,8},{14,12},{10,14},{6,10},{2,6},{0,2},{5,1},{9,5},... | collective-permute-start | bytes 786440 | tf_op jit(solution)/shard_map/ppermute | solution.py:284
  93.2 33.2 %collective-permute-start.20 = (bf16[64,2048]{1,0:T(8,128)(2,1)S(1)}, bf16[64,2048]{1,0:T(8,128)(2,1)S(1)}, u32[]{:S(2)}, u32[]{:S(2)}) collective-permute-start(bf16[64,2048]{1,0:T(8,128)(2,1)S(1)} %get-tuple-element.22), channel_id=1, source_target_pairs={{0,4},{4,8},{8,12},{12,14},{14,10},{10,6},{6,2},{2,0},{1,5},{5,9},... | collective-permute-start | bytes 786440 | tf_op jit(solution)/shard_map/ppermute | solution.py:284
  122.2 9.3 %collective-permute-start.31 = (bf16[64,2048]{1,0:T(8,128)(2,1)S(1)}, bf16[64,2048]{1,0:T(8,128)(2,1)S(1)}, u32[]{:S(2)}, u32[]{:S(2)}) collective-permute-start(bf16[64,2048]{1,0:T(8,128)(2,1)S(1)} %add_convert_fusion.3), channel_id=1, source_target_pairs={{4,0},{8,4},{12,8},{14,12},{10,14},{6,10},{2,6},{0,2},{5,1},{9,5},... | collective-permute-start | bytes 786440 | tf_op jit(solution)/shard_map/ppermute | solution.py:284
  124.2 9.3 %collective-permute-start.28 = (bf16[64,2048]{1,0:T(8,128)(2,1)S(1)}, bf16[64,2048]{1,0:T(8,128)(2,1)S(1)}, u32[]{:S(2)}, u32[]{:S(2)}) collective-permute-start(bf16[64,2048]{1,0:T(8,128)(2,1)S(1)} %add_convert_fusion.5), channel_id=1, source_target_pairs={{0,4},{4,8},{8,12},{12,14},{14,10},{10,6},{6,2},{2,0},{1,5},{5,9},... | collective-permute-start | bytes 786440 | tf_op jit(solution)/shard_map/ppermute | solution.py:284
  124.5 12.6 %collective-permute-start.25 = (bf16[64,2048]{1,0:T(8,128)(2,1)S(1)}, bf16[64,2048]{1,0:T(8,128)(2,1)S(1)}, u32[]{:S(2)}, u32[]{:S(2)}) collective-permute-start(bf16[64,2048]{1,0:T(8,128)(2,1)S(1)} %add_convert_fusion.8), channel_id=1, source_target_pairs={{4,0},{8,4},{12,8},{14,12},{10,14},{6,10},{2,6},{0,2},{5,1},{9,5},... | collective-permute-start | bytes 786440 | tf_op jit(solution)/shard_map/ppermute | solution.py:284
  126.4 12.6 %collective-permute-start.21 = (bf16[64,2048]{1,0:T(8,128)(2,1)S(1)}, bf16[64,2048]{1,0:T(8,128)(2,1)S(1)}, u32[]{:S(2)}, u32[]{:S(2)}) collective-permute-start(bf16[64,2048]{1,0:T(8,128)(2,1)S(1)} %add_convert_fusion.11), channel_id=1, source_target_pairs={{0,4},{4,8},{8,12},{12,14},{14,10},{10,6},{6,2},{2,0},{1,5},{5,9},... | collective-permute-start | bytes 786440 | tf_op jit(solution)/shard_map/ppermute | solution.py:284
  131.6 10.4 %collective-permute-start.32 = (bf16[64,2048]{1,0:T(8,128)(2,1)S(1)}, bf16[64,2048]{1,0:T(8,128)(2,1)S(1)}, u32[]{:S(2)}, u32[]{:S(2)}) collective-permute-start(bf16[64,2048]{1,0:T(8,128)(2,1)S(1)} %add_convert_fusion.2), channel_id=1, source_target_pairs={{4,0},{8,4},{12,8},{14,12},{10,14},{6,10},{2,6},{0,2},{5,1},{9,5},... | collective-permute-start | bytes 786440 | tf_op jit(solution)/shard_map/ppermute | solution.py:284
  133.5 13.2 %collective-permute-start.29 = (bf16[64,2048]{1,0:T(8,128)(2,1)S(1)}, bf16[64,2048]{1,0:T(8,128)(2,1)S(1)}, u32[]{:S(2)}, u32[]{:S(2)}) collective-permute-start(bf16[64,2048]{1,0:T(8,128)(2,1)S(1)} %add_convert_fusion.4), channel_id=1, source_target_pairs={{0,4},{4,8},{8,12},{12,14},{14,10},{10,6},{6,2},{2,0},{1,5},{5,9},... | collective-permute-start | bytes 786440 | tf_op jit(solution)/shard_map/ppermute | solution.py:284
  137.2 11.3 %collective-permute-start.26 = (bf16[64,2048]{1,0:T(8,128)(2,1)S(1)}, bf16[64,2048]{1,0:T(8,128)(2,1)S(1)}, u32[]{:S(2)}, u32[]{:S(2)}) collective-permute-start(bf16[64,2048]{1,0:T(8,128)(2,1)S(1)} %add_convert_fusion.7), channel_id=1, source_target_pairs={{4,0},{8,4},{12,8},{14,12},{10,14},{6,10},{2,6},{0,2},{5,1},{9,5},... | collective-permute-start | bytes 786440 | tf_op jit(solution)/shard_map/ppermute | solution.py:284
  139.1 6.4 %collective-permute-start.22 = (bf16[64,2048]{1,0:T(8,128)(2,1)S(1)}, bf16[64,2048]{1,0:T(8,128)(2,1)S(1)}, u32[]{:S(2)}, u32[]{:S(2)}) collective-permute-start(bf16[64,2048]{1,0:T(8,128)(2,1)S(1)} %add_convert_fusion.10), channel_id=1, source_target_pairs={{0,4},{4,8},{8,12},{12,14},{14,10},{10,6},{6,2},{2,0},{1,5},{5,9},... | collective-permute-start | bytes 786440 | tf_op jit(solution)/shard_map/ppermute | solution.py:284
  142.0 6.4 %collective-permute-start.33 = (bf16[64,2048]{1,0:T(8,128)(2,1)S(1)}, bf16[64,2048]{1,0:T(8,128)(2,1)S(1)}, u32[]{:S(2)}, u32[]{:S(2)}) collective-permute-start(bf16[64,2048]{1,0:T(8,128)(2,1)S(1)} %add_convert_fusion.1), channel_id=1, source_target_pairs={{4,0},{8,4},{12,8},{14,12},{10,14},{6,10},{2,6},{0,2},{5,1},{9,5},... | collective-permute-start | bytes 786440 | tf_op jit(solution)/shard_map/ppermute | solution.py:284
  145.6 6.4 %collective-permute-start.23 = (bf16[64,2048]{1,0:T(8,128)(2,1)S(1)}, bf16[64,2048]{1,0:T(8,128)(2,1)S(1)}, u32[]{:S(2)}, u32[]{:S(2)}) collective-permute-start(bf16[64,2048]{1,0:T(8,128)(2,1)S(1)} %add_convert_fusion.9), channel_id=1, source_target_pairs={{0,4},{4,8},{8,12},{12,14},{14,10},{10,6},{6,2},{2,0},{1,5},{5,9},... | collective-permute-start | bytes 786440 | tf_op jit(solution)/shard_map/ppermute | solution.py:284

commit v2 on v0

--- a/solution.py
+++ b/solution.py
@@ -1,6 +1,10 @@
+import functools
+
 import jax
 import jax.numpy as jnp
 from jax import lax
+from jax.experimental import pallas as pl
+from jax.experimental.pallas import tpu as pltpu
 from jax.sharding import PartitionSpec as P
 
 BLOCK = 128
@@ -15,7 +19,7 @@
     return jnp.dot(hidden, out_weights, preferred_element_type=jnp.float32).astype(jnp.bfloat16)
 
 
-def body(tokens, expert_ids, route_gates, expert_in, expert_out, old_place, new_place):
+def routed_body(tokens, expert_ids, route_gates, expert_in, expert_out, old_place, new_place):
     ep_size = lax.axis_size("ep")
     dp_size = lax.axis_size("dp")
     devices = ep_size * dp_size
@@ -112,6 +116,259 @@
     return jnp.sum(weighted.reshape(tok_rows, top_count, model_width), axis=1).astype(jnp.bfloat16)
 
 
+def dense_kernel(ids_ref, gates_ref, out_ref):
+    _, experts, tok_rows = out_ref.shape
+    expert = lax.broadcasted_iota(jnp.int32, (experts, tok_rows), 0)
+    dense = jnp.zeros((experts, tok_rows), jnp.float32)
+    for k in range(ids_ref.shape[0]):
+        dense += jnp.where(ids_ref[k : k + 1, :] == expert, gates_ref[k : k + 1, :], 0.0)
+    out_ref[0] = dense
+
+
+def join_kernel(mine_ref, theirs_ref, out_ref):
+    count = mine_ref.shape[0]
+    out_ref[:count] = mine_ref[...]
+    out_ref[count:] = theirs_ref[...]
+
+
+def gate_kernel(info_ref, old_ref, new_ref, mine_ref, theirs_ref, out_ref):
+    sources, experts, tok_rows = mine_ref.shape
+    own = info_ref[0]
+    kind = own % 2
+    ep = own // 2
+    mine, theirs = mine_ref[...], theirs_ref[...]
+    which = lax.broadcasted_iota(jnp.int32, mine.shape, 1)
+    source_col = lax.broadcasted_iota(jnp.int32, (sources, sources), 0) ^ ep
+    source_row = lax.broadcasted_iota(jnp.int32, (sources, sources), 1) ^ ep
+    before = (source_row < source_col).astype(jnp.float32)
+    earlier = (
+        lax.broadcasted_iota(jnp.int32, (tok_rows, tok_rows), 0)
+        < lax.broadcasted_iota(jnp.int32, (tok_rows, tok_rows), 1)
+    ).astype(jnp.float32)
+    exact = functools.partial(
+        jnp.dot, preferred_element_type=jnp.float32, precision=lax.Precision.HIGHEST
+    )
+
+    place = jnp.where(ep % 2 == 0, ep // 2, sources - (ep + 1) // 2)
+    turn = (place + lax.broadcasted_iota(jnp.int32, (sources, sources), 0)) % sources
+    there = jnp.where(2 * turn < sources, 2 * turn, 2 * (sources - turn) - 1)
+    in_ring = (
+        lax.broadcasted_iota(jnp.int32, (sources, sources), 1) == (there ^ ep)
+    ).astype(jnp.float32)
+
+    def holds(server):
+        return lax.fori_loop(
+            0, experts, lambda e, found: jnp.where(old_ref[e] == server, e, found), 0
+        )
+
+    def gates_of(expert, table):
+        return jnp.sum(jnp.where(which == expert, table, 0.0), axis=1)
+
+    for q in range(2):
+        expert = holds(own ^ q)
+        gates = gates_of(expert, mine)
+        chosen = (gates > 0.0).astype(jnp.float32)
+        totals = jnp.sum(chosen, axis=1, keepdims=True)
+        rank = exact(chosen, earlier) + exact(before, jnp.broadcast_to(totals, gates.shape))
+        booked = gates_of(holds(new_ref[expert]), theirs)
+        home_total = jnp.sum(jnp.where(booked > 0.0, 1.0, 0.0)).astype(jnp.int32)
+        home_rows = ((home_total + (BLOCK - 1)) // BLOCK) * BLOCK
+        position = rank.astype(jnp.int32) + jnp.where(kind == 0, 0, home_rows)
+        served = jnp.where(position < SERVE_BLOCKS * BLOCK, gates, 0.0)
+        out_ref[q] = exact(in_ring, served).T
+
+
+def load_kernel(*refs):
+    count = len(refs) // 2
+    copies = [pltpu.make_async_copy(refs[i], refs[count + i], refs[-1].at[i]) for i in range(count)]
+    for copy in copies:
+        copy.start()
+    for copy in copies:
+        copy.wait()
+
+
+def load_call(*arrays):
+    return pl.pallas_call(
+        load_kernel,
+        out_shape=[jax.ShapeDtypeStruct(x.shape, x.dtype) for x in arrays],
+        in_specs=[pl.BlockSpec(memory_space=pl.ANY)] * len(arrays),
+        out_specs=[pl.BlockSpec(memory_space=pltpu.VMEM)] * len(arrays),
+        scratch_shapes=[pltpu.SemaphoreType.DMA((len(arrays),))],
+        compiler_params=pltpu.CompilerParams(vmem_limit_bytes=16 * 2**20),
+        cost_estimate=pl.CostEstimate(
+            flops=0, bytes_accessed=sum(4 * x.size for x in arrays), transcendentals=0
+        ),
+    )(*arrays)
+
+
+def expert_kernel(columns, gates_ref, *refs):
+    refs = list(refs)
+    x_all, hidden, total, x_sems = refs[-4:]
+    halves = 2 * len(columns)
+    x_refs, weights, out_refs = refs[:halves], refs[halves : halves + 4], refs[halves + 4 : -4]
+    half = x_all.shape[0] // halves
+    rows = 2 * half
+    hidden_units, width = hidden.shape[1], x_all.shape[1]
+    tile, step = hidden_units // 3, width // 4
+    copies = [
+        pltpu.make_async_copy(ref, x_all.at[pl.ds(i * half, half)], x_sems.at[i])
+        for i, ref in enumerate(x_refs)
+    ]
+    for copy in copies:
+        copy.start()
+    for copy in copies:
+        copy.wait()
+    for q in range(2):
+        in_ref, down_ref = weights[2 * q : 2 * q + 2]
+        for f in range(0, hidden_units, tile):
+            x = x_all[...]
+            gate = jnp.dot(x, in_ref[0, :, f : f + tile], preferred_element_type=jnp.float32)
+            up = jnp.dot(
+                x,
+                in_ref[0, :, hidden_units + f : hidden_units + f + tile],
+                preferred_element_type=jnp.float32,
+            )
+            hidden[:, f : f + tile] = (gate / (1.0 + jnp.exp(-gate)) * up).astype(jnp.bfloat16)
+        column = jnp.concatenate([gates_ref[q, :, d : d + 1] for d in columns])
+        for n in range(0, width, step):
+            out = jnp.dot(
+                hidden[...], down_ref[0, :, n : n + step], preferred_element_type=jnp.float32
+            )
+            out = out.astype(jnp.bfloat16).astype(jnp.float32) * column
+            if q == 0:
+                total[:, n : n + step] = out
+            else:
+                out = (total[:, n : n + step] + out).astype(jnp.bfloat16)
+                for i, ref in enumerate(out_refs):
+                    ref[:, n : n + step] = out[i * half : (i + 1) * half]
+
+
+def expert_call(halves, columns, gates, weights):
+    half, width = halves[0].shape
+    hidden_units = weights[1].shape[1]
+    rows = half * len(halves)
+    return pl.pallas_call(
+        functools.partial(expert_kernel, columns),
+        out_shape=[jax.ShapeDtypeStruct((half, width), jnp.bfloat16)] * len(halves),
+        in_specs=[pl.BlockSpec(memory_space=pltpu.VMEM)]
+        + [pl.BlockSpec(memory_space=pl.ANY)] * len(halves)
+        + [pl.BlockSpec(memory_space=pltpu.VMEM)] * 4,
+        out_specs=[pl.BlockSpec(memory_space=pltpu.VMEM)] * len(halves),
+        scratch_shapes=[
+            pltpu.VMEM((rows, width), jnp.bfloat16),
+            pltpu.VMEM((rows, hidden_units), jnp.bfloat16),
+            pltpu.VMEM((rows, width), jnp.float32),
+            pltpu.SemaphoreType.DMA((len(halves),)),
+        ],
+        compiler_params=pltpu.CompilerParams(vmem_limit_bytes=16 * 2**20),
+        cost_estimate=pl.CostEstimate(
+            flops=2 * 2 * rows * width * 3 * hidden_units,
+            bytes_accessed=2 * 2 * 3 * width * hidden_units,
+            transcendentals=0,
+        ),
+    )(gates, *halves, *weights)
+
+
+def gathered_body(tokens, expert_ids, route_gates, expert_in, expert_out, old_place, new_place):
+    ep_size = lax.axis_size("ep")
+    devices = ep_size * 2
+    tok_rows = expert_ids.shape[0]
+    half = tok_rows // 2
+    reach = ep_size // 2
+    ring = [*range(0, ep_size, 2), *range(ep_size - 1, 0, -2)]
+    ahead = [(ring[i], ring[(i + 1) % ep_size]) for i in range(ep_size)]
+    back = [(b, a) for a, b in ahead]
+    ep = lax.axis_index("ep")
+    own = ep * 2 + lax.axis_index("dp")
+
+    def swap_cores(x):
+        return lax.ppermute(x, "dp", [(0, 1), (1, 0)])
+
+    def go(x, way):
+        return lax.ppermute(x, "ep", ahead if way > 0 else back)
+
+    def after(x, *others):
+        return lax.optimization_barrier((x, *others))[0]
+
+    vmem = pl.BlockSpec(memory_space=pltpu.VMEM)
+
+    dense = pl.pallas_call(
+        dense_kernel,
+        out_shape=jax.ShapeDtypeStruct((1, devices, tok_rows), jnp.float32),
+        in_specs=[vmem, vmem],
+        out_specs=vmem,
+    )(expert_ids.T, route_gates.T)
+
+    def gather_gates(dense, step, *others):
+        theirs = lax.ppermute(dense, "ep", [(i, i ^ (1 << step)) for i in range(ep_size)])
+        return pl.pallas_call(
+            join_kernel,
+            out_shape=jax.ShapeDtypeStruct((2 << step, devices, tok_rows), jnp.float32),
+            in_specs=[vmem, vmem],
+            out_specs=vmem,
+        )(after(dense, *others), theirs)
+
+    weights = (expert_in, expert_out, swap_cores(expert_in), swap_cores(expert_out))
+    held = {0: [tokens[:half], tokens[half:]]}
+
+    def pass_on(d, *waits):
+        held[-d] = [go(after(x, *w), 1) for x, w in zip(held[1 - d], waits)]
+        held[d] = [go(after(x, *w), -1) for x, w in zip(held[d - 1], waits)]
+
+    pass_on(1, [], [])
+    for step in range(ep_size.bit_length() - 1):
+        at = min(step + 1, reach - 1)
+        if step + 1 < reach - 1:
+            pass_on(step + 2, [], [])
+        dense = gather_gates(dense, step, held[-at][1], held[at][1])
+    held[reach] = [go(held[1 - reach][0], 1), go(held[reach - 1][1], -1)]
+    weights = (*weights[:2], *load_call(*[after(w, dense) for w in weights[2:]]))
+    gates = pl.pallas_call(
+        gate_kernel,
+        out_shape=jax.ShapeDtypeStruct((2, tok_rows, ep_size), jnp.float32),
+        in_specs=[pl.BlockSpec(memory_space=pltpu.SMEM)] * 3 + [vmem] * 2,
+        out_specs=vmem,
+    )(own.reshape(1), old_place, new_place, dense, swap_cores(dense))
+
+    part = {}
+
+    def compute(distances, *waits):
+        halves = [x for d in distances for x in held[d]]
+        outs = expert_call(
+            [after(halves[0], *waits), *halves[1:]],
+            [d % ep_size for d in distances],
+            gates,
+            weights,
+        )
+        for i, d in enumerate(distances):
+            part[d] = outs[2 * i : 2 * i + 2]
+        return outs[0]
+
+    def add(*xs):
+        return sum(x.astype(jnp.float32) for x in xs).astype(jnp.bfloat16)
+
+    compute([1 - reach, reach - 1])
+    compute([reach])
+    far, near = {1: 0, -1: 1}, {1: 1, -1: 0}
+    moving = {way: part[reach][far[way]] for way in (1, -1)}
+    late = {}
+    for d in range(reach - 1, 0, -1):
+        compute([1 - d, d - 1] if d > 1 else [0], *moving.values())
+        moving = {way: go(x, way) for way, x in moving.items()}
+        late = {
+            way: go(add(*([late[way]] if late else []), part[way * d][near[way]]), way)
+            for way in (1, -1)
+        }
+        first = part[1 - d][0]
+        moving = {
+            way: add(after(moving[way], first), part[way * d][far[way]]) for way in (1, -1)
+        }
+    moving = {way: go(x, way) for way, x in moving.items()}
+    return jnp.concatenate(
+        [add(part[0][0], moving[1], late[-1]), add(part[0][1], moving[-1], late[1])]
+    )
+
+
 def solution(mesh):
     placed = (
         P(("grp", "ep", "dp"), None),
@@ -122,6 +379,12 @@
         P(),
         P(),
     )
+
+    def body(tokens, expert_ids, *rest):
+        devices = lax.axis_size("ep") * lax.axis_size("dp")
+        gathered = devices <= 2 * expert_ids.shape[1]
+        return (gathered_body if gathered else routed_body)(tokens, expert_ids, *rest)
+
     return jax.shard_map(
         body, mesh=mesh, in_specs=placed, out_specs=P(("grp", "ep", "dp"), None), check_vma=False
     )

time: 442 us -> 119 us (0.27)
  the two profiles are of different devices: /device:TPU:11 before, /device:TPU:0 now
where the time goes in v2:
time: 119 us; the launch traced here: 118 us
  starting transfers between devices  43 us (36%)
  Pallas kernels  39.1 us (33%)
  waiting for transfers between devices  30 us (25%)
  local copies, waits for them, and re-layouts  4.33 us (4%)
  other arithmetic  1.68 us (1%)
    ppermute x28, starting transfers between devices, go(): return lax.ppermute(x, 'ep', ahead if way > 0 else back)  36.4 us
    pallas_call x5, Pallas kernels, expert_call(): pl.pallas_call(functools.partial(expert_kernel, columns), out_shape=[jax....  26.6 us
    ppermute x28, waiting for transfers between devices, go(): return lax.ppermute(x, 'ep', ahead if way > 0 else back)  20.7 us
    ppermute x3, waiting for transfers between devices, gather_gates(): lax.ppermute(dense, 'ep', [(i, i ^ 1 << step) for i in range(ep_size)])  7.81 us
    ppermute x3, starting transfers between devices, gather_gates(): lax.ppermute(dense, 'ep', [(i, i ^ 1 << step) for i in range(ep_size)])  6.04 us
    pallas_call x3, Pallas kernels, gather_gates(): pl.pallas_call(join_kernel, out_shape=jax.ShapeDtypeStruct((2 << step, de...  4.06 us
    pallas_call x1, Pallas kernels, load_call(): pl.pallas_call(load_kernel, out_shape=[jax.ShapeDtypeStruct(x.shape, x.dt...  3.87 us
    pallas_call x1, Pallas kernels, gathered_body(): pl.pallas_call(gate_kernel, out_shape=jax.ShapeDtypeStruct((2, tok_rows,...  3.33 us
  transfers between devices with their start and end apart: 34, of which 14 were waited for; matrix products, arithmetic and copies ran while one was open for 2% of the time, Pallas kernels for 33%

profile of v2, /device:TPU:0, one launch (start us, length us, event | category | flops | bytes accessed | tf_op | source)
XLA Modules:
  0.0 118.3 jit_solution(17776222491375426183)
XLA Ops:
  0.0 0.5 collective-permute-start.15
  0.5 2.0 %fusion = (bf16[64,2048]{1,0:T(8,128)(2,1)S(1)}, bf16[64,2048]{1,0:T(8,128)(2,1)}) fusion(bf16[128,2048]{1,0:T(8,128)(2,1)} %param.7), kind=kLoop, calls=%fused_computation.13 | loop fusion | bytes 1048576 | tf_op jit(solution)/shard_map/slice | solution.py:312
  2.5 2.9 %collective-permute-start.1 = (bf16[64,2048]{1,0:T(8,128)(2,1)}, bf16[64,2048]{1,0:T(8,128)(2,1)}, u32[]{:S(2)}, u32[]{:S(2)}) collective-permute-start(bf16[64,2048]{1,0:T(8,128)(2,1)} %get-tuple-element.70.refs_1_), channel_id=1, source_target_pairs={{4,0},{8,4},{12,8},{14,12},{10,14},{6,10},{2,6},{0,2},{5,1},{9,5},... | collective-permute-start | bytes 786440 | tf_op jit(solution)/shard_map/ppermute | solution.py:288
  5.5 0.1 collective-permute-start
  5.6 2.0 %collective-permute-start.10 = (bf16[64,2048]{1,0:T(8,128)(2,1)S(1)}, bf16[64,2048]{1,0:T(8,128)(2,1)}, u32[]{:S(2)}, u32[]{:S(2)}) collective-permute-start(bf16[64,2048]{1,0:T(8,128)(2,1)S(1)} %get-tuple-element.58.refs_0_), channel_id=1, source_target_pairs={{0,4},{4,8},{8,12},{12,14},{14,10},{10,6},{6,2},{2,0},{1,5},{5,9},... | collective-permute-start | bytes 786440 | tf_op jit(solution)/shard_map/ppermute | solution.py:288
  7.6 4.8 %collective-permute-done.1.refs_3_ = bf16[64,2048]{1,0:T(8,128)(2,1)} collective-permute-done((bf16[64,2048]{1,0:T(8,128)(2,1)}, bf16[64,2048]{1,0:T(8,128)(2,1)}, u32[]{:S(2)}, u32[]{:S(2)}) %collective-permute-start.1) | collective-permute-done | bytes 262176 | tf_op jit(solution)/shard_map/ppermute | solution.py:288
  12.4 1.7 %collective-permute-start.4 = (bf16[64,2048]{1,0:T(8,128)(2,1)}, bf16[64,2048]{1,0:T(8,128)(2,1)}, u32[]{:S(2)}, u32[]{:S(2)}) collective-permute-start(bf16[64,2048]{1,0:T(8,128)(2,1)} %collective-permute-done.1.refs_3_), channel_id=1, source_target_pairs={{4,0},{8,4},{12,8},{14,12},{10,14},{6,10},{2,6},{0,2},{5,1},{9,5},... | collective-permute-start | bytes 786440 | tf_op jit(solution)/shard_map/ppermute | solution.py:288
  14.0 1.3 %shard_map.73.mine_ref = f32[1,16,128]{2,1,0:T(8,128)} custom-call(s32[8,128]{1,0:T(8,128)} %bitcast.3, f32[8,128]{1,0:T(8,128)} %bitcast.4), custom_call_target="tpu_custom_call" | custom-call | tf_op jit(solution)/shard_map/pallas_call | solution.py:295
  15.3 1.6 %collective-permute-start.2 = (f32[1,16,128]{2,1,0:T(8,128)}, f32[1,16,128]{2,1,0:T(8,128)S(1)}, u32[]{:S(2)}, u32[]{:S(2)}) collective-permute-start(f32[1,16,128]{2,1,0:T(8,128)} %shard_map.73.mine_ref), channel_id=1, source_target_pairs={{0,2},{2,0},{4,6},{6,4},{8,10},{10,8},{12,14},{14,12},{1,3},{3,1},... | collective-permute-start | bytes 24584 | tf_op jit(solution)/shard_map/ppermute | solution.py:303
  16.9 2.5 %collective-permute-done.2.theirs_ref = f32[1,16,128]{2,1,0:T(8,128)S(1)} collective-permute-done((f32[1,16,128]{2,1,0:T(8,128)}, f32[1,16,128]{2,1,0:T(8,128)S(1)}, u32[]{:S(2)}, u32[]{:S(2)}) %collective-permute-start.2) | collective-permute-done | bytes 8224 | tf_op jit(solution)/shard_map/ppermute | solution.py:303
  19.4 0.9 collective-permute-start.3
  20.3 1.3 %shard_map.74.mine_ref = f32[2,16,128]{2,1,0:T(8,128)} custom-call(f32[1,16,128]{2,1,0:T(8,128)} %shard_map.73.mine_ref, f32[1,16,128]{2,1,0:T(8,128)} %copy-done.8), custom_call_target="tpu_custom_call" | custom-call | tf_op jit(solution)/shard_map/pallas_call | solution.py:304
  21.7 1.6 %collective-permute-start.5 = (f32[2,16,128]{2,1,0:T(8,128)}, f32[2,16,128]{2,1,0:T(8,128)S(1)}, u32[]{:S(2)}, u32[]{:S(2)}) collective-permute-start(f32[2,16,128]{2,1,0:T(8,128)} %shard_map.74.mine_ref), channel_id=1, source_target_pairs={{0,4},{2,6},{4,0},{6,2},{8,12},{10,14},{12,8},{14,10},{1,5},{3,7},... | collective-permute-start | bytes 49160 | tf_op jit(solution)/shard_map/ppermute | solution.py:303
  23.2 2.4 %collective-permute-done.5.theirs_ref = f32[2,16,128]{2,1,0:T(8,128)S(1)} collective-permute-done((f32[2,16,128]{2,1,0:T(8,128)}, f32[2,16,128]{2,1,0:T(8,128)S(1)}, u32[]{:S(2)}, u32[]{:S(2)}) %collective-permute-start.5) | collective-permute-done | bytes 16416 | tf_op jit(solution)/shard_map/ppermute | solution.py:303
  25.6 1.9 %collective-permute-start.11 = (bf16[64,2048]{1,0:T(8,128)(2,1)}, bf16[64,2048]{1,0:T(8,128)(2,1)}, u32[]{:S(2)}, u32[]{:S(2)}) collective-permute-start(bf16[64,2048]{1,0:T(8,128)(2,1)} %collective-permute-done.10.refs_0_), channel_id=1, source_target_pairs={{0,4},{4,8},{8,12},{12,14},{14,10},{10,6},{6,2},{2,0},{1,5},{5,9},... | collective-permute-start | bytes 786440 | tf_op jit(solution)/shard_map/ppermute | solution.py:288
  27.5 1.4 %collective-permute-start.18 = (bf16[64,2048]{1,0:T(8,128)(2,1)S(1)}, bf16[64,2048]{1,0:T(8,128)(2,1)}, u32[]{:S(2)}, u32[]{:S(2)}) collective-permute-start(bf16[64,2048]{1,0:T(8,128)(2,1)S(1)} %get-tuple-element.58.refs_0_), channel_id=1, source_target_pairs={{4,0},{8,4},{12,8},{14,12},{10,14},{6,10},{2,6},{0,2},{5,1},{9,5},... | collective-permute-start | bytes 786440 | tf_op jit(solution)/shard_map/ppermute | solution.py:288
  29.0 2.0 %collective-permute-start.7 = (bf16[64,2048]{1,0:T(8,128)(2,1)}, bf16[64,2048]{1,0:T(8,128)(2,1)}, u32[]{:S(2)}, u32[]{:S(2)}) collective-permute-start(bf16[64,2048]{1,0:T(8,128)(2,1)} %collective-permute-done.4.refs_3_), channel_id=1, source_target_pairs={{4,0},{8,4},{12,8},{14,12},{10,14},{6,10},{2,6},{0,2},{5,1},{9,5},... | collective-permute-start | bytes 786440 | tf_op jit(solution)/shard_map/ppermute | solution.py:288
  30.9 1.3 %shard_map.75.mine_ref = f32[4,16,128]{2,1,0:T(8,128)} custom-call(f32[2,16,128]{2,1,0:T(8,128)} %shard_map.74.mine_ref, f32[2,16,128]{2,1,0:T(8,128)} %copy-done.7), custom_call_target="tpu_custom_call" | custom-call | tf_op jit(solution)/shard_map/pallas_call | solution.py:304
  32.3 1.3 %collective-permute-done.11.refs_0_ = bf16[64,2048]{1,0:T(8,128)(2,1)} collective-permute-done((bf16[64,2048]{1,0:T(8,128)(2,1)}, bf16[64,2048]{1,0:T(8,128)(2,1)}, u32[]{:S(2)}, u32[]{:S(2)}) %collective-permute-start.11) | collective-permute-done | bytes 262176 | tf_op jit(solution)/shard_map/ppermute | solution.py:288
  33.6 2.9 %collective-permute-start.8 = (f32[4,16,128]{2,1,0:T(8,128)}, f32[4,16,128]{2,1,0:T(8,128)S(1)}, u32[]{:S(2)}, u32[]{:S(2)}) collective-permute-start(f32[4,16,128]{2,1,0:T(8,128)} %shard_map.75.mine_ref), channel_id=1, source_target_pairs={{0,8},{2,10},{4,12},{6,14},{8,0},{10,2},{12,4},{14,6},{1,9},{3,11}... | collective-permute-start | bytes 98312 | tf_op jit(solution)/shard_map/ppermute | solution.py:303
  36.5 0.3 collective-permute-done.18.refs_2_
  36.7 2.5 %collective-permute-start.12 = (bf16[64,2048]{1,0:T(8,128)(2,1)}, bf16[64,2048]{1,0:T(8,128)(2,1)}, u32[]{:S(2)}, u32[]{:S(2)}) collective-permute-start(bf16[64,2048]{1,0:T(8,128)(2,1)} %collective-permute-done.11.refs_0_), channel_id=1, source_target_pairs={{0,4},{4,8},{8,12},{12,14},{14,10},{10,6},{6,2},{2,0},{1,5},{5,9},... | collective-permute-start | bytes 786440 | tf_op jit(solution)/shard_map/ppermute | solution.py:288
  39.3 2.9 %collective-permute-done.8.theirs_ref = f32[4,16,128]{2,1,0:T(8,128)S(1)} collective-permute-done((f32[4,16,128]{2,1,0:T(8,128)}, f32[4,16,128]{2,1,0:T(8,128)S(1)}, u32[]{:S(2)}, u32[]{:S(2)}) %collective-permute-start.8) | collective-permute-done | bytes 32800 | tf_op jit(solution)/shard_map/ppermute | solution.py:303
  42.2 2.6 %collective-permute-start.6 = (bf16[64,2048]{1,0:T(8,128)(2,1)}, bf16[64,2048]{1,0:T(8,128)(2,1)S(1)}, u32[]{:S(2)}, u32[]{:S(2)}) collective-permute-start(bf16[64,2048]{1,0:T(8,128)(2,1)} %collective-permute-done.3.refs_1_), channel_id=1, source_target_pairs={{0,4},{4,8},{8,12},{12,14},{14,10},{10,6},{6,2},{2,0},{1,5},{5,9},... | collective-permute-start | bytes 786440 | tf_op jit(solution)/shard_map/ppermute | solution.py:288
  44.8 1.5 %collective-permute-done.12.refs_0_ = bf16[64,2048]{1,0:T(8,128)(2,1)} collective-permute-done((bf16[64,2048]{1,0:T(8,128)(2,1)}, bf16[64,2048]{1,0:T(8,128)(2,1)}, u32[]{:S(2)}, u32[]{:S(2)}) %collective-permute-start.12) | collective-permute-done | bytes 262176 | tf_op jit(solution)/shard_map/ppermute | solution.py:288
  46.3 2.5 %collective-permute-start.13 = (bf16[64,2048]{1,0:T(8,128)(2,1)}, bf16[64,2048]{1,0:T(8,128)(2,1)}, u32[]{:S(2)}, u32[]{:S(2)}) collective-permute-start(bf16[64,2048]{1,0:T(8,128)(2,1)} %collective-permute-done.12.refs_0_), channel_id=1, source_target_pairs={{0,4},{4,8},{8,12},{12,14},{14,10},{10,6},{6,2},{2,0},{1,5},{5,9},... | collective-permute-start | bytes 786440 | tf_op jit(solution)/shard_map/ppermute | solution.py:288
  48.8 3.0 %collective-permute-done.6.refs_1_ = bf16[64,2048]{1,0:T(8,128)(2,1)S(1)} collective-permute-done((bf16[64,2048]{1,0:T(8,128)(2,1)}, bf16[64,2048]{1,0:T(8,128)(2,1)S(1)}, u32[]{:S(2)}, u32[]{:S(2)}) %collective-permute-start.6) | collective-permute-done | bytes 262176 | tf_op jit(solution)/shard_map/ppermute | solution.py:288
  51.7 0.7 copy-done.3
  52.4 1.4 %shard_map.76.mine_ref = f32[8,16,128]{2,1,0:T(8,128)} custom-call(f32[4,16,128]{2,1,0:T(8,128)} %shard_map.75.mine_ref, f32[4,16,128]{2,1,0:T(8,128)} %copy-done.6), custom_call_target="tpu_custom_call" | custom-call | tf_op jit(solution)/shard_map/pallas_call | solution.py:304
  53.8 1.5 %collective-permute-done.9.theirs_ref = f32[8,16,128]{2,1,0:T(8,128)S(1)} collective-permute-done((f32[8,16,128]{2,1,0:T(8,128)}, f32[8,16,128]{2,1,0:T(8,128)S(1)}, u32[]{:S(2)}, u32[]{:S(2)}) %collective-permute-start.9) | collective-permute-done | bytes 65568 | tf_op jit(solution)/shard_map/ppermute | solution.py:285
  55.3 0.8 collective-permute-start.20
  56.1 3.3 %shard_map.77.gates_ref = f32[2,128,8]{2,1,0:T(8,128)} custom-call(s32[1]{0:T(128)} %bitcast.info_ref, s32[16]{0:T(128)} %old_ref.1, s32[16]{0:T(128)} %new_ref.1, f32[8,16,128]{2,1,0:T(8,128)} %shard_map.76.mine_ref, f32[8,16,128]{2,1,0:T(8,128)} %copy-done.5), custom_call_target="tpu_custom_call" | custom-call | tf_op jit(solution)/shard_map/pallas_call | solution.py:326
  59.4 3.9 %shard_map.78 = (bf16[1,2048,1536]{2,1,0:T(8,128)(2,1)S(1)}, bf16[1,768,2048]{2,1,0:T(8,128)(2,1)S(1)}) custom-call(bf16[1,2048,1536]{2,1,0:T(8,128)(2,1)} %collective-permute-done.15.refs_0_, bf16[1,768,2048]{2,1,0:T(8,128)(2,1)} %collective-permute-done.16.refs_1_), custom_call_target="tpu_custom_call" | custom-call | bytes 18874368 | tf_op jit(solution)/shard_map/pallas_call | solution.py:191
  63.3 1.6 %copy-done = bf16[1,2048,1536]{2,1,0:T(8,128)(2,1)S(1)} copy-done((bf16[1,2048,1536]{2,1,0:T(8,128)(2,1)S(1)}, bf16[1,2048,1536]{2,1,0:T(8,128)(2,1)}, u32[]{:S(2)}) %copy-start) | copy-done | bytes 6291480
  64.9 3.9 %shard_map.79 = (bf16[64,2048]{1,0:T(8,128)(2,1)S(1)}, bf16[64,2048]{1,0:T(8,128)(2,1)S(1)}) custom-call(f32[2,128,8]{2,1,0:T(8,128)S(1)} %copy-done.2, bf16[64,2048]{1,0:T(8,128)(2,1)} %collective-permute-done.13.refs_0_, bf16[64,2048]{1,0:T(8,128)(2,1)} %collective-permute-done.14.refs_1_, bf16[1,2048,1536]{2,1,0:T(8,128)(2,1)S(1)} %copy-done, ...), custom_call_target="tpu_custom_call" | custom-call | flops 2415919104 | bytes 18874368 | tf_op jit(solution)/shard_map/pallas_call | solution.py:250
  68.8 1.8 %collective-permute-start.22 = (bf16[64,2048]{1,0:T(8,128)(2,1)S(1)}, bf16[64,2048]{1,0:T(8,128)(2,1)S(1)}, u32[]{:S(2)}, u32[]{:S(2)}) collective-permute-start(bf16[64,2048]{1,0:T(8,128)(2,1)S(1)} %get-tuple-element.45), channel_id=1, source_target_pairs={{4,0},{8,4},{12,8},{14,12},{10,14},{6,10},{2,6},{0,2},{5,1},{9,5},... | collective-permute-start | bytes 786440 | tf_op jit(solution)/shard_map/ppermute | solution.py:288
  70.6 0.3 collective-permute-start.17
  70.9 6.3 %shard_map.81 = (bf16[64,2048]{1,0:T(8,128)(2,1)S(1)}, bf16[64,2048]{1,0:T(8,128)(2,1)S(1)}, bf16[64,2048]{1,0:T(8,128)(2,1)S(1)}, bf16[64,2048]{1,0:T(8,128)(2,1)S(1)}) custom-call(f32[2,128,8]{2,1,0:T(8,128)S(1)} %copy-done.2, bf16[64,2048]{1,0:T(8,128)(2,1)} %collective-permute-done.12.refs_0_, bf16[64,2048]{1,0:T(8,128)(2,1)S(1)} %copy-done.4, ...), custom_call_target="tpu_custom_call" | custom-call | flops 4831838208 | bytes 18874368 | tf_op jit(solution)/shard_map/pallas_call | solution.py:250
  77.1 1.8 %collective-permute-start.26 = (bf16[64,2048]{1,0:T(8,128)(2,1)S(1)}, bf16[64,2048]{1,0:T(8,128)(2,1)S(1)}, u32[]{:S(2)}, u32[]{:S(2)}) collective-permute-start(bf16[64,2048]{1,0:T(8,128)(2,1)S(1)} %get-tuple-element.62), channel_id=1, source_target_pairs={{4,0},{8,4},{12,8},{14,12},{10,14},{6,10},{2,6},{0,2},{5,1},{9,5},... | collective-permute-start | bytes 786440 | tf_op jit(solution)/shard_map/ppermute | solution.py:288
  78.9 0.4 collective-permute-start.31
  79.3 6.3 %shard_map.80 = (bf16[64,2048]{1,0:T(8,128)(2,1)S(1)}, bf16[64,2048]{1,0:T(8,128)(2,1)S(1)}, bf16[64,2048]{1,0:T(8,128)(2,1)S(1)}, bf16[64,2048]{1,0:T(8,128)(2,1)S(1)}) custom-call(f32[2,128,8]{2,1,0:T(8,128)S(1)} %copy-done.2, bf16[64,2048]{1,0:T(8,128)(2,1)} %collective-permute-done.11.refs_0_, bf16[64,2048]{1,0:T(8,128)(2,1)} %collective-permute-done.3.refs_1_, ...), custom_call_target="tpu_custom_call" | custom-call | flops 4831838208 | bytes 18874368 | tf_op jit(solution)/shard_map/pallas_call | solution.py:250
  85.7 0.1 add_convert_fusion.11
  85.7 1.8 %collective-permute-start.21 = (bf16[64,2048]{1,0:T(8,128)(2,1)S(1)}, bf16[64,2048]{1,0:T(8,128)(2,1)S(1)}, u32[]{:S(2)}, u32[]{:S(2)}) collective-permute-start(bf16[64,2048]{1,0:T(8,128)(2,1)S(1)} %add_convert_fusion.11), channel_id=1, source_target_pairs={{0,4},{4,8},{8,12},{12,14},{14,10},{10,6},{6,2},{2,0},{1,5},{5,9},... | collective-permute-start | bytes 786440 | tf_op jit(solution)/shard_map/ppermute | solution.py:288
  87.6 0.3 collective-permute-start.23
  87.9 0.1 add_convert_fusion.6
  88.0 1.7 %collective-permute-start.27 = (bf16[64,2048]{1,0:T(8,128)(2,1)S(1)}, bf16[64,2048]{1,0:T(8,128)(2,1)S(1)}, u32[]{:S(2)}, u32[]{:S(2)}) collective-permute-start(bf16[64,2048]{1,0:T(8,128)(2,1)S(1)} %add_convert_fusion.6), channel_id=1, source_target_pairs={{4,0},{8,4},{12,8},{14,12},{10,14},{6,10},{2,6},{0,2},{5,1},{9,5},... | collective-permute-start | bytes 786440 | tf_op jit(solution)/shard_map/ppermute | solution.py:288
  89.8 0.4 collective-permute-start.32
  90.2 6.3 %shard_map.82 = (bf16[64,2048]{1,0:T(8,128)(2,1)S(1)}, bf16[64,2048]{1,0:T(8,128)(2,1)S(1)}, bf16[64,2048]{1,0:T(8,128)(2,1)S(1)}, bf16[64,2048]{1,0:T(8,128)(2,1)S(1)}) custom-call(f32[2,128,8]{2,1,0:T(8,128)S(1)} %copy-done.2, bf16[64,2048]{1,0:T(8,128)(2,1)} %collective-permute-done.10.refs_0_, bf16[64,2048]{1,0:T(8,128)(2,1)} %collective-permute-done.refs_1_, ...), custom_call_target="tpu_custom_call" | custom-call | flops 4831838208 | bytes 18874368 | tf_op jit(solution)/shard_map/pallas_call | solution.py:250
  96.5 0.4 collective-permute-done.23
  97.0 1.8 %collective-permute-start.24 = (bf16[64,2048]{1,0:T(8,128)(2,1)S(1)}, bf16[64,2048]{1,0:T(8,128)(2,1)S(1)}, u32[]{:S(2)}, u32[]{:S(2)}) collective-permute-start(bf16[64,2048]{1,0:T(8,128)(2,1)S(1)} %add_convert_fusion.9), channel_id=1, source_target_pairs={{0,4},{4,8},{8,12},{12,14},{14,10},{10,6},{6,2},{2,0},{1,5},{5,9},... | collective-permute-start | bytes 786440 | tf_op jit(solution)/shard_map/ppermute | solution.py:288
  98.8 0.4 collective-permute-start.29
  99.2 2.7 %collective-permute-done.27 = bf16[64,2048]{1,0:T(8,128)(2,1)S(1)} collective-permute-done((bf16[64,2048]{1,0:T(8,128)(2,1)S(1)}, bf16[64,2048]{1,0:T(8,128)(2,1)S(1)}, u32[]{:S(2)}, u32[]{:S(2)}) %collective-permute-start.27) | collective-permute-done | bytes 262176 | tf_op jit(solution)/shard_map/ppermute | solution.py:288
  101.9 0.4 collective-permute-start.28
  102.4 2.0 %collective-permute-start.33 = (bf16[64,2048]{1,0:T(8,128)(2,1)S(1)}, bf16[64,2048]{1,0:T(8,128)(2,1)S(1)}, u32[]{:S(2)}, u32[]{:S(2)}) collective-permute-start(bf16[64,2048]{1,0:T(8,128)(2,1)S(1)} %add_convert_fusion.1), channel_id=1, source_target_pairs={{0,4},{4,8},{8,12},{12,14},{14,10},{10,6},{6,2},{2,0},{1,5},{5,9},... | collective-permute-start | bytes 786440 | tf_op jit(solution)/shard_map/ppermute | solution.py:288
  104.4 3.8 %shard_map.83 = (bf16[64,2048]{1,0:T(8,128)(2,1)S(1)}, bf16[64,2048]{1,0:T(8,128)(2,1)S(1)}) custom-call(f32[2,128,8]{2,1,0:T(8,128)S(1)} %copy-done.2, bf16[64,2048]{1,0:T(8,128)(2,1)S(1)} %get-tuple-element.58.refs_0_, bf16[64,2048]{1,0:T(8,128)(2,1)} %get-tuple-element.70.refs_1_, bf16[1,2048,1536]{2,1,0:T(8,128)(2,1)S(1)} %copy-done, ...), custom_call_target="tpu_custom_call" | custom-call | flops 2415919104 | bytes 18874368 | tf_op jit(solution)/shard_map/pallas_call | solution.py:250
  108.1 0.1 add_convert_fusion.7
  108.2 1.5 %collective-permute-start.25 = (bf16[64,2048]{1,0:T(8,128)(2,1)S(1)}, bf16[64,2048]{1,0:T(8,128)(2,1)S(1)}, u32[]{:S(2)}, u32[]{:S(2)}) collective-permute-start(bf16[64,2048]{1,0:T(8,128)(2,1)S(1)} %add_convert_fusion.7), channel_id=1, source_target_pairs={{0,4},{4,8},{8,12},{12,14},{14,10},{10,6},{6,2},{2,0},{1,5},{5,9},... | collective-permute-start | bytes 786440 | tf_op jit(solution)/shard_map/ppermute | solution.py:288
  109.8 0.6 collective-permute-start.30
  110.4 3.3 %collective-permute-done.28 = bf16[64,2048]{1,0:T(8,128)(2,1)S(1)} collective-permute-done((bf16[64,2048]{1,0:T(8,128)(2,1)S(1)}, bf16[64,2048]{1,0:T(8,128)(2,1)S(1)}, u32[]{:S(2)}, u32[]{:S(2)}) %collective-permute-start.28) | collective-permute-done | bytes 262176 | tf_op jit(solution)/shard_map/ppermute | solution.py:288
  113.7 2.1 %collective-permute-done.25 = bf16[64,2048]{1,0:T(8,128)(2,1)S(1)} collective-permute-done((bf16[64,2048]{1,0:T(8,128)(2,1)S(1)}, bf16[64,2048]{1,0:T(8,128)(2,1)S(1)}, u32[]{:S(2)}, u32[]{:S(2)}) %collective-permute-start.25) | collective-permute-done | bytes 262176 | tf_op jit(solution)/shard_map/ppermute | solution.py:288
  115.8 0.1 add_convert_fusion.4
  115.9 1.4 %collective-permute-done.30 = bf16[64,2048]{1,0:T(8,128)(2,1)S(1)} collective-permute-done((bf16[64,2048]{1,0:T(8,128)(2,1)S(1)}, bf16[64,2048]{1,0:T(8,128)(2,1)S(1)}, u32[]{:S(2)}, u32[]{:S(2)}) %collective-permute-start.30) | collective-permute-done | bytes 262176 | tf_op jit(solution)/shard_map/ppermute | solution.py:288
  117.3 0.1 add_convert_fusion
  117.4 0.8 pad_maximum_fusion
  (47 shorter events, 0.6 us)
Async XLA Ops:
  0.0 63.3 %copy-start.1 = (bf16[1,768,2048]{2,1,0:T(8,128)(2,1)S(1)}, bf16[1,768,2048]{2,1,0:T(8,128)(2,1)}, u32[]{:S(2)}) copy-start(bf16[1,768,2048]{2,1,0:T(8,128)(2,1)} %refs_3_.3) | copy-start | bytes 9437188
  0.0 59.4 %collective-permute-start.15 = (bf16[1,2048,1536]{2,1,0:T(8,128)(2,1)}, bf16[1,2048,1536]{2,1,0:T(8,128)(2,1)}, u32[]{:S(2)}, u32[]{:S(2)}) collective-permute-start(bf16[1,2048,1536]{2,1,0:T(8,128)(2,1)} %refs_2_.3), channel_id=1, source_target_pairs={{0,1},{1,0},{2,3},{3,2},{4,5},{5,4},{6,7},{7,6},{8,9},{9,8},{10,11... | collective-permute-start | bytes 18874376 | tf_op jit(solution)/shard_map/ppermute | solution.py:285
  0.5 59.0 %collective-permute-start.16 = (bf16[1,768,2048]{2,1,0:T(8,128)(2,1)}, bf16[1,768,2048]{2,1,0:T(8,128)(2,1)}, u32[]{:S(2)}, u32[]{:S(2)}) collective-permute-start(bf16[1,768,2048]{2,1,0:T(8,128)(2,1)} %refs_3_.3), channel_id=1, source_target_pairs={{0,1},{1,0},{2,3},{3,2},{4,5},{5,4},{6,7},{7,6},{8,9},{9,8},{10,11... | collective-permute-start | bytes 9437192 | tf_op jit(solution)/shard_map/ppermute | solution.py:285
  2.5 9.8 %collective-permute-start.1 = (bf16[64,2048]{1,0:T(8,128)(2,1)}, bf16[64,2048]{1,0:T(8,128)(2,1)}, u32[]{:S(2)}, u32[]{:S(2)}) collective-permute-start(bf16[64,2048]{1,0:T(8,128)(2,1)} %get-tuple-element.70.refs_1_), channel_id=1, source_target_pairs={{4,0},{8,4},{12,8},{14,12},{10,14},{6,10},{2,6},{0,2},{5,1},{9,5},... | collective-permute-start | bytes 786440 | tf_op jit(solution)/shard_map/ppermute | solution.py:288
  5.5 9.9 %collective-permute-start = (bf16[64,2048]{1,0:T(8,128)(2,1)}, bf16[64,2048]{1,0:T(8,128)(2,1)}, u32[]{:S(2)}, u32[]{:S(2)}) collective-permute-start(bf16[64,2048]{1,0:T(8,128)(2,1)} %get-tuple-element.70.refs_1_), channel_id=1, source_target_pairs={{0,4},{4,8},{8,12},{12,14},{14,10},{10,6},{6,2},{2,0},{1,5},{5,9},... | collective-permute-start | bytes 786440 | tf_op jit(solution)/shard_map/ppermute | solution.py:288
  5.6 16.1 %collective-permute-start.10 = (bf16[64,2048]{1,0:T(8,128)(2,1)S(1)}, bf16[64,2048]{1,0:T(8,128)(2,1)}, u32[]{:S(2)}, u32[]{:S(2)}) collective-permute-start(bf16[64,2048]{1,0:T(8,128)(2,1)S(1)} %get-tuple-element.58.refs_0_), channel_id=1, source_target_pairs={{0,4},{4,8},{8,12},{12,14},{14,10},{10,6},{6,2},{2,0},{1,5},{5,9},... | collective-permute-start | bytes 786440 | tf_op jit(solution)/shard_map/ppermute | solution.py:288
  12.4 15.2 %collective-permute-start.4 = (bf16[64,2048]{1,0:T(8,128)(2,1)}, bf16[64,2048]{1,0:T(8,128)(2,1)}, u32[]{:S(2)}, u32[]{:S(2)}) collective-permute-start(bf16[64,2048]{1,0:T(8,128)(2,1)} %collective-permute-done.1.refs_3_), channel_id=1, source_target_pairs={{4,0},{8,4},{12,8},{14,12},{10,14},{6,10},{2,6},{0,2},{5,1},{9,5},... | collective-permute-start | bytes 786440 | tf_op jit(solution)/shard_map/ppermute | solution.py:288
  15.3 4.1 %collective-permute-start.2 = (f32[1,16,128]{2,1,0:T(8,128)}, f32[1,16,128]{2,1,0:T(8,128)S(1)}, u32[]{:S(2)}, u32[]{:S(2)}) collective-permute-start(f32[1,16,128]{2,1,0:T(8,128)} %shard_map.73.mine_ref), channel_id=1, source_target_pairs={{0,2},{2,0},{4,6},{6,4},{8,10},{10,8},{12,14},{14,12},{1,3},{3,1},... | collective-permute-start | bytes 24584 | tf_op jit(solution)/shard_map/ppermute | solution.py:303
  19.4 0.9 copy-start.8
  19.4 9.5 %collective-permute-start.3 = (bf16[64,2048]{1,0:T(8,128)(2,1)}, bf16[64,2048]{1,0:T(8,128)(2,1)}, u32[]{:S(2)}, u32[]{:S(2)}) collective-permute-start(bf16[64,2048]{1,0:T(8,128)(2,1)} %collective-permute-done.refs_1_), channel_id=1, source_target_pairs={{0,4},{4,8},{8,12},{12,14},{14,10},{10,6},{6,2},{2,0},{1,5},{5,9},... | collective-permute-start | bytes 786440 | tf_op jit(solution)/shard_map/ppermute | solution.py:288
  21.7 4.0 %collective-permute-start.5 = (f32[2,16,128]{2,1,0:T(8,128)}, f32[2,16,128]{2,1,0:T(8,128)S(1)}, u32[]{:S(2)}, u32[]{:S(2)}) collective-permute-start(f32[2,16,128]{2,1,0:T(8,128)} %shard_map.74.mine_ref), channel_id=1, source_target_pairs={{0,4},{2,6},{4,0},{6,2},{8,12},{10,14},{12,8},{14,10},{1,5},{3,7},... | collective-permute-start | bytes 49160 | tf_op jit(solution)/shard_map/ppermute | solution.py:303
  25.6 5.3 %copy-start.7 = (f32[2,16,128]{2,1,0:T(8,128)}, f32[2,16,128]{2,1,0:T(8,128)S(1)}, u32[]{:S(2)}) copy-start(f32[2,16,128]{2,1,0:T(8,128)S(1)} %collective-permute-done.5.theirs_ref) | copy-start | bytes 49156
  25.6 8.0 %collective-permute-start.11 = (bf16[64,2048]{1,0:T(8,128)(2,1)}, bf16[64,2048]{1,0:T(8,128)(2,1)}, u32[]{:S(2)}, u32[]{:S(2)}) collective-permute-start(bf16[64,2048]{1,0:T(8,128)(2,1)} %collective-permute-done.10.refs_0_), channel_id=1, source_target_pairs={{0,4},{4,8},{8,12},{12,14},{14,10},{10,6},{6,2},{2,0},{1,5},{5,9},... | collective-permute-start | bytes 786440 | tf_op jit(solution)/shard_map/ppermute | solution.py:288
  27.5 9.2 %collective-permute-start.18 = (bf16[64,2048]{1,0:T(8,128)(2,1)S(1)}, bf16[64,2048]{1,0:T(8,128)(2,1)}, u32[]{:S(2)}, u32[]{:S(2)}) collective-permute-start(bf16[64,2048]{1,0:T(8,128)(2,1)S(1)} %get-tuple-element.58.refs_0_), channel_id=1, source_target_pairs={{4,0},{8,4},{12,8},{14,12},{10,14},{6,10},{2,6},{0,2},{5,1},{9,5},... | collective-permute-start | bytes 786440 | tf_op jit(solution)/shard_map/ppermute | solution.py:288
  29.0 15.8 %collective-permute-start.7 = (bf16[64,2048]{1,0:T(8,128)(2,1)}, bf16[64,2048]{1,0:T(8,128)(2,1)}, u32[]{:S(2)}, u32[]{:S(2)}) collective-permute-start(bf16[64,2048]{1,0:T(8,128)(2,1)} %collective-permute-done.4.refs_3_), channel_id=1, source_target_pairs={{4,0},{8,4},{12,8},{14,12},{10,14},{6,10},{2,6},{0,2},{5,1},{9,5},... | collective-permute-start | bytes 786440 | tf_op jit(solution)/shard_map/ppermute | solution.py:288
  33.6 8.6 %collective-permute-start.8 = (f32[4,16,128]{2,1,0:T(8,128)}, f32[4,16,128]{2,1,0:T(8,128)S(1)}, u32[]{:S(2)}, u32[]{:S(2)}) collective-permute-start(f32[4,16,128]{2,1,0:T(8,128)} %shard_map.75.mine_ref), channel_id=1, source_target_pairs={{0,8},{2,10},{4,12},{6,14},{8,0},{10,2},{12,4},{14,6},{1,9},{3,11}... | collective-permute-start | bytes 98312 | tf_op jit(solution)/shard_map/ppermute | solution.py:303
  36.7 9.5 %collective-permute-start.12 = (bf16[64,2048]{1,0:T(8,128)(2,1)}, bf16[64,2048]{1,0:T(8,128)(2,1)}, u32[]{:S(2)}, u32[]{:S(2)}) collective-permute-start(bf16[64,2048]{1,0:T(8,128)(2,1)} %collective-permute-done.11.refs_0_), channel_id=1, source_target_pairs={{0,4},{4,8},{8,12},{12,14},{14,10},{10,6},{6,2},{2,0},{1,5},{5,9},... | collective-permute-start | bytes 786440 | tf_op jit(solution)/shard_map/ppermute | solution.py:288
  42.2 10.3 %copy-start.6 = (f32[4,16,128]{2,1,0:T(8,128)}, f32[4,16,128]{2,1,0:T(8,128)S(1)}, u32[]{:S(2)}) copy-start(f32[4,16,128]{2,1,0:T(8,128)S(1)} %collective-permute-done.8.theirs_ref) | copy-start | bytes 98308
  42.2 9.5 %collective-permute-start.6 = (bf16[64,2048]{1,0:T(8,128)(2,1)}, bf16[64,2048]{1,0:T(8,128)(2,1)S(1)}, u32[]{:S(2)}, u32[]{:S(2)}) collective-permute-start(bf16[64,2048]{1,0:T(8,128)(2,1)} %collective-permute-done.3.refs_1_), channel_id=1, source_target_pairs={{0,4},{4,8},{8,12},{12,14},{14,10},{10,6},{6,2},{2,0},{1,5},{5,9},... | collective-permute-start | bytes 786440 | tf_op jit(solution)/shard_map/ppermute | solution.py:288
  44.8 9.1 %collective-permute-start.19 = (bf16[64,2048]{1,0:T(8,128)(2,1)}, bf16[64,2048]{1,0:T(8,128)(2,1)}, u32[]{:S(2)}, u32[]{:S(2)}) collective-permute-start(bf16[64,2048]{1,0:T(8,128)(2,1)} %collective-permute-done.18.refs_2_), channel_id=1, source_target_pairs={{4,0},{8,4},{12,8},{14,12},{10,14},{6,10},{2,6},{0,2},{5,1},{9,5},... | collective-permute-start | bytes 786440 | tf_op jit(solution)/shard_map/ppermute | solution.py:288
  46.3 13.1 %collective-permute-start.13 = (bf16[64,2048]{1,0:T(8,128)(2,1)}, bf16[64,2048]{1,0:T(8,128)(2,1)}, u32[]{:S(2)}, u32[]{:S(2)}) collective-permute-start(bf16[64,2048]{1,0:T(8,128)(2,1)} %collective-permute-done.12.refs_0_), channel_id=1, source_target_pairs={{0,4},{4,8},{8,12},{12,14},{14,10},{10,6},{6,2},{2,0},{1,5},{5,9},... | collective-permute-start | bytes 786440 | tf_op jit(solution)/shard_map/ppermute | solution.py:288
  51.7 0.7 copy-start.3
  52.4 10.9 %collective-permute-start.14 = (bf16[64,2048]{1,0:T(8,128)(2,1)}, bf16[64,2048]{1,0:T(8,128)(2,1)}, u32[]{:S(2)}, u32[]{:S(2)}) collective-permute-start(bf16[64,2048]{1,0:T(8,128)(2,1)} %collective-permute-done.7.refs_3_), channel_id=1, source_target_pairs={{4,0},{8,4},{12,8},{14,12},{10,14},{6,10},{2,6},{0,2},{5,1},{9,5},... | collective-permute-start | bytes 786440 | tf_op jit(solution)/shard_map/ppermute | solution.py:288
  53.8 1.5 %collective-permute-start.9 = (f32[8,16,128]{2,1,0:T(8,128)}, f32[8,16,128]{2,1,0:T(8,128)S(1)}, u32[]{:S(2)}, u32[]{:S(2)}) collective-permute-start(f32[8,16,128]{2,1,0:T(8,128)} %shard_map.76.mine_ref), channel_id=1, source_target_pairs={{0,1},{1,0},{2,3},{3,2},{4,5},{5,4},{6,7},{7,6},{8,9},{9,8},{10,11... | collective-permute-start | bytes 196616 | tf_op jit(solution)/shard_map/ppermute | solution.py:285
  55.3 0.8 copy-start.5
  55.3 15.6 %collective-permute-start.20 = (bf16[64,2048]{1,0:T(8,128)(2,1)}, bf16[64,2048]{1,0:T(8,128)(2,1)}, u32[]{:S(2)}, u32[]{:S(2)}) collective-permute-start(bf16[64,2048]{1,0:T(8,128)(2,1)} %collective-permute-done.19.refs_2_), channel_id=1, source_target_pairs={{4,0},{8,4},{12,8},{14,12},{10,14},{6,10},{2,6},{0,2},{5,1},{9,5},... | collective-permute-start | bytes 786440 | tf_op jit(solution)/shard_map/ppermute | solution.py:288
  59.4 5.5 %copy-start = (bf16[1,2048,1536]{2,1,0:T(8,128)(2,1)S(1)}, bf16[1,2048,1536]{2,1,0:T(8,128)(2,1)}, u32[]{:S(2)}) copy-start(bf16[1,2048,1536]{2,1,0:T(8,128)(2,1)} %refs_2_.3) | copy-start | bytes 18874372
  59.4 5.5 %copy-start.2 = (f32[2,128,8]{2,1,0:T(8,128)S(1)}, f32[2,128,8]{2,1,0:T(8,128)}, u32[]{:S(2)}) copy-start(f32[2,128,8]{2,1,0:T(8,128)} %shard_map.77.gates_ref) | copy-start | bytes 24580
  64.9 6.0 %copy-start.4 = (bf16[64,2048]{1,0:T(8,128)(2,1)S(1)}, bf16[64,2048]{1,0:T(8,128)(2,1)}, u32[]{:S(2)}) copy-start(bf16[64,2048]{1,0:T(8,128)(2,1)} %copy-done.3) | copy-start | bytes 786436
  68.8 16.8 %collective-permute-start.22 = (bf16[64,2048]{1,0:T(8,128)(2,1)S(1)}, bf16[64,2048]{1,0:T(8,128)(2,1)S(1)}, u32[]{:S(2)}, u32[]{:S(2)}) collective-permute-start(bf16[64,2048]{1,0:T(8,128)(2,1)S(1)} %get-tuple-element.45), channel_id=1, source_target_pairs={{4,0},{8,4},{12,8},{14,12},{10,14},{6,10},{2,6},{0,2},{5,1},{9,5},... | collective-permute-start | bytes 786440 | tf_op jit(solution)/shard_map/ppermute | solution.py:288
  70.6 15.1 %collective-permute-start.17 = (bf16[64,2048]{1,0:T(8,128)(2,1)S(1)}, bf16[64,2048]{1,0:T(8,128)(2,1)S(1)}, u32[]{:S(2)}, u32[]{:S(2)}) collective-permute-start(bf16[64,2048]{1,0:T(8,128)(2,1)S(1)} %get-tuple-element.44), channel_id=1, source_target_pairs={{0,4},{4,8},{8,12},{12,14},{14,10},{10,6},{6,2},{2,0},{1,5},{5,9},... | collective-permute-start | bytes 786440 | tf_op jit(solution)/shard_map/ppermute | solution.py:288
  77.1 10.8 %collective-permute-start.26 = (bf16[64,2048]{1,0:T(8,128)(2,1)S(1)}, bf16[64,2048]{1,0:T(8,128)(2,1)S(1)}, u32[]{:S(2)}, u32[]{:S(2)}) collective-permute-start(bf16[64,2048]{1,0:T(8,128)(2,1)S(1)} %get-tuple-element.62), channel_id=1, source_target_pairs={{4,0},{8,4},{12,8},{14,12},{10,14},{6,10},{2,6},{0,2},{5,1},{9,5},... | collective-permute-start | bytes 786440 | tf_op jit(solution)/shard_map/ppermute | solution.py:288
  78.9 10.8 %collective-permute-start.31 = (bf16[64,2048]{1,0:T(8,128)(2,1)S(1)}, bf16[64,2048]{1,0:T(8,128)(2,1)S(1)}, u32[]{:S(2)}, u32[]{:S(2)}) collective-permute-start(bf16[64,2048]{1,0:T(8,128)(2,1)S(1)} %get-tuple-element.66), channel_id=1, source_target_pairs={{0,4},{4,8},{8,12},{12,14},{14,10},{10,6},{6,2},{2,0},{1,5},{5,9},... | collective-permute-start | bytes 786440 | tf_op jit(solution)/shard_map/ppermute | solution.py:288
  85.7 10.8 %collective-permute-start.21 = (bf16[64,2048]{1,0:T(8,128)(2,1)S(1)}, bf16[64,2048]{1,0:T(8,128)(2,1)S(1)}, u32[]{:S(2)}, u32[]{:S(2)}) collective-permute-start(bf16[64,2048]{1,0:T(8,128)(2,1)S(1)} %add_convert_fusion.11), channel_id=1, source_target_pairs={{0,4},{4,8},{8,12},{12,14},{14,10},{10,6},{6,2},{2,0},{1,5},{5,9},... | collective-permute-start | bytes 786440 | tf_op jit(solution)/shard_map/ppermute | solution.py:288
  87.6 9.3 %collective-permute-start.23 = (bf16[64,2048]{1,0:T(8,128)(2,1)S(1)}, bf16[64,2048]{1,0:T(8,128)(2,1)S(1)}, u32[]{:S(2)}, u32[]{:S(2)}) collective-permute-start(bf16[64,2048]{1,0:T(8,128)(2,1)S(1)} %add_convert_fusion.10), channel_id=1, source_target_pairs={{4,0},{8,4},{12,8},{14,12},{10,14},{6,10},{2,6},{0,2},{5,1},{9,5},... | collective-permute-start | bytes 786440 | tf_op jit(solution)/shard_map/ppermute | solution.py:288
  88.0 13.9 %collective-permute-start.27 = (bf16[64,2048]{1,0:T(8,128)(2,1)S(1)}, bf16[64,2048]{1,0:T(8,128)(2,1)S(1)}, u32[]{:S(2)}, u32[]{:S(2)}) collective-permute-start(bf16[64,2048]{1,0:T(8,128)(2,1)S(1)} %add_convert_fusion.6), channel_id=1, source_target_pairs={{4,0},{8,4},{12,8},{14,12},{10,14},{6,10},{2,6},{0,2},{5,1},{9,5},... | collective-permute-start | bytes 786440 | tf_op jit(solution)/shard_map/ppermute | solution.py:288
  89.8 12.5 %collective-permute-start.32 = (bf16[64,2048]{1,0:T(8,128)(2,1)S(1)}, bf16[64,2048]{1,0:T(8,128)(2,1)S(1)}, u32[]{:S(2)}, u32[]{:S(2)}) collective-permute-start(bf16[64,2048]{1,0:T(8,128)(2,1)S(1)} %add_convert_fusion.2), channel_id=1, source_target_pairs={{0,4},{4,8},{8,12},{12,14},{14,10},{10,6},{6,2},{2,0},{1,5},{5,9},... | collective-permute-start | bytes 786440 | tf_op jit(solution)/shard_map/ppermute | solution.py:288
  97.0 11.1 %collective-permute-start.24 = (bf16[64,2048]{1,0:T(8,128)(2,1)S(1)}, bf16[64,2048]{1,0:T(8,128)(2,1)S(1)}, u32[]{:S(2)}, u32[]{:S(2)}) collective-permute-start(bf16[64,2048]{1,0:T(8,128)(2,1)S(1)} %add_convert_fusion.9), channel_id=1, source_target_pairs={{0,4},{4,8},{8,12},{12,14},{14,10},{10,6},{6,2},{2,0},{1,5},{5,9},... | collective-permute-start | bytes 786440 | tf_op jit(solution)/shard_map/ppermute | solution.py:288
  98.8 10.9 %collective-permute-start.29 = (bf16[64,2048]{1,0:T(8,128)(2,1)S(1)}, bf16[64,2048]{1,0:T(8,128)(2,1)S(1)}, u32[]{:S(2)}, u32[]{:S(2)}) collective-permute-start(bf16[64,2048]{1,0:T(8,128)(2,1)S(1)} %add_convert_fusion.8), channel_id=1, source_target_pairs={{4,0},{8,4},{12,8},{14,12},{10,14},{6,10},{2,6},{0,2},{5,1},{9,5},... | collective-permute-start | bytes 786440 | tf_op jit(solution)/shard_map/ppermute | solution.py:288
  101.9 11.8 %collective-permute-start.28 = (bf16[64,2048]{1,0:T(8,128)(2,1)S(1)}, bf16[64,2048]{1,0:T(8,128)(2,1)S(1)}, u32[]{:S(2)}, u32[]{:S(2)}) collective-permute-start(bf16[64,2048]{1,0:T(8,128)(2,1)S(1)} %add_convert_fusion.5), channel_id=1, source_target_pairs={{4,0},{8,4},{12,8},{14,12},{10,14},{6,10},{2,6},{0,2},{5,1},{9,5},... | collective-permute-start | bytes 786440 | tf_op jit(solution)/shard_map/ppermute | solution.py:288
  102.4 13.5 %collective-permute-start.33 = (bf16[64,2048]{1,0:T(8,128)(2,1)S(1)}, bf16[64,2048]{1,0:T(8,128)(2,1)S(1)}, u32[]{:S(2)}, u32[]{:S(2)}) collective-permute-start(bf16[64,2048]{1,0:T(8,128)(2,1)S(1)} %add_convert_fusion.1), channel_id=1, source_target_pairs={{0,4},{4,8},{8,12},{12,14},{14,10},{10,6},{6,2},{2,0},{1,5},{5,9},... | collective-permute-start | bytes 786440 | tf_op jit(solution)/shard_map/ppermute | solution.py:288
  108.2 7.6 %collective-permute-start.25 = (bf16[64,2048]{1,0:T(8,128)(2,1)S(1)}, bf16[64,2048]{1,0:T(8,128)(2,1)S(1)}, u32[]{:S(2)}, u32[]{:S(2)}) collective-permute-start(bf16[64,2048]{1,0:T(8,128)(2,1)S(1)} %add_convert_fusion.7), channel_id=1, source_target_pairs={{0,4},{4,8},{8,12},{12,14},{14,10},{10,6},{6,2},{2,0},{1,5},{5,9},... | collective-permute-start | bytes 786440 | tf_op jit(solution)/shard_map/ppermute | solution.py:288
  109.8 7.5 %collective-permute-start.30 = (bf16[64,2048]{1,0:T(8,128)(2,1)S(1)}, bf16[64,2048]{1,0:T(8,128)(2,1)S(1)}, u32[]{:S(2)}, u32[]{:S(2)}) collective-permute-start(bf16[64,2048]{1,0:T(8,128)(2,1)S(1)} %add_convert_fusion.3), channel_id=1, source_target_pairs={{4,0},{8,4},{12,8},{14,12},{10,14},{6,10},{2,6},{0,2},{5,1},{9,5},... | collective-permute-start | bytes 786440 | tf_op jit(solution)/shard_map/ppermute | solution.py:288

commit v3 on v0

--- a/solution.py
+++ b/solution.py
@@ -1,6 +1,10 @@
+import functools
+
 import jax
 import jax.numpy as jnp
 from jax import lax
+from jax.experimental import pallas as pl
+from jax.experimental.pallas import tpu as pltpu
 from jax.sharding import PartitionSpec as P
 
 BLOCK = 128
@@ -15,7 +19,7 @@
     return jnp.dot(hidden, out_weights, preferred_element_type=jnp.float32).astype(jnp.bfloat16)
 
 
-def body(tokens, expert_ids, route_gates, expert_in, expert_out, old_place, new_place):
+def routed_body(tokens, expert_ids, route_gates, expert_in, expert_out, old_place, new_place):
     ep_size = lax.axis_size("ep")
     dp_size = lax.axis_size("dp")
     devices = ep_size * dp_size
@@ -112,6 +116,385 @@
     return jnp.sum(weighted.reshape(tok_rows, top_count, model_width), axis=1).astype(jnp.bfloat16)
 
 
+LANES = 128
+
+
+def pack_kernel(experts, ids_ref, gates_ref, mate_ref, tokens_ref, out_ref, second_ref, copied):
+    half, width = out_ref.shape[0], tokens_ref.shape[1]
+    copies = [
+        pltpu.make_async_copy(
+            tokens_ref.at[pl.ds(0, half)], out_ref.at[:, pl.ds(0, width)], copied.at[0]
+        ),
+        pltpu.make_async_copy(tokens_ref.at[pl.ds(half, half)], second_ref, copied.at[1]),
+    ]
+    for copy in copies:
+        copy.start()
+    lane = lax.broadcasted_iota(jnp.int32, (2 * half, LANES), 1)
+    expert = (lane % experts).astype(jnp.float32)
+    ids, gates, mate = (
+        ref[...].astype(jnp.float32).T for ref in (ids_ref, gates_ref, mate_ref)
+    )
+    dense = jnp.zeros((2 * half, LANES), jnp.float32)
+    named = jnp.zeros((2 * half, LANES), jnp.float32)
+    for k in range(ids.shape[1]):
+        dense += jnp.where(ids[:, k : k + 1] == expert, gates[:, k : k + 1], 0.0)
+        named += jnp.where(mate[:, k : k + 1] == expert, 1.0, 0.0)
+    lane = lane[:half]
+    dense = jnp.where(lane < 3 * experts, dense[:half], dense[half:])
+    high = dense.astype(jnp.bfloat16).astype(jnp.float32)
+    middle = (dense - high).astype(jnp.bfloat16).astype(jnp.float32)
+    piece = lane // experts % 3
+    packed = jnp.where(piece == 0, high, jnp.where(piece == 1, middle, dense - high - middle))
+    totals = jnp.sum(named, axis=0, keepdims=True)
+    packed = jnp.where(lane < 6 * experts, packed, jnp.where(lane < 7 * experts, totals, 0.0))
+    out_ref[:, width:] = packed.astype(jnp.bfloat16)
+    for copy in copies:
+        copy.wait()
+
+
+def served_gates(info_ref, old_ref, new_ref, packs):
+    count, half = len(packs), packs[0].shape[0]
+    experts = old_ref.shape[0]
+    own = info_ref[0]
+    kind, ep = own % 2, own // 2
+    row = lax.broadcasted_iota(jnp.int32, (LANES, LANES), 0)
+    col = lax.broadcasted_iota(jnp.int32, (LANES, LANES), 1)
+
+    def at_expert(table, index):
+        found = jnp.zeros(index.shape, jnp.int32)
+        for e in range(experts):
+            found = jnp.where(index == e, table[e], found)
+        return found
+
+    col_q, col_h, col_d = col // (2 * count), col // count % 2, col % count
+    wanted = (
+        (col < 4 * count)
+        & (row < 6 * experts)
+        & (row // (3 * experts) == col_h)
+        & (at_expert(old_ref, row % experts) == (own ^ col_q))
+    )
+    place = jnp.where(ep % 2 == 0, ep // 2, count - (ep + 1) // 2)
+
+    def source(d):
+        turn = (place + d) % count
+        return jnp.where(2 * turn < count, 2 * turn, 2 * (count - turn) - 1)
+
+    row_q, row_h, row_d = row // (2 * count), row // count % 2, row % count
+    first = source(row_d) * 2 + row_h
+    second = source(col_d) * 2 + col_h
+    before = (row < 4 * count) & (row_q == col_q) & (first < second)
+    lane = lax.broadcasted_iota(jnp.int32, (8, LANES), 1)
+    old, new = at_expert(old_ref, lane % experts), at_expert(new_ref, lane % experts)
+    above = (
+        lax.broadcasted_iota(jnp.int32, (half, half), 1)
+        < lax.broadcasted_iota(jnp.int32, (half, half), 0)
+    )
+
+    def product(a, b):
+        return jnp.dot(
+            a.astype(jnp.bfloat16), b.astype(jnp.bfloat16), preferred_element_type=jnp.float32
+        )
+
+    def mask(x):
+        return jnp.where(x, 1.0, 0.0)
+
+    gates = jnp.zeros((half, LANES), jnp.float32)
+    booked = jnp.zeros((8, LANES), jnp.float32)
+    for d in range(count):
+        gates += product(packs[d], mask(wanted & (col_d == d)))
+        booked += packs[d][:8].astype(jnp.float32)
+    chosen = mask(gates > 0.0)
+    totals = jnp.broadcast_to(jnp.sum(chosen, axis=0, keepdims=True), (8, LANES))
+    rank = product(mask(above), chosen) + product(totals, mask(before))[:1]
+    home_rows = jnp.zeros((1, LANES), jnp.int32)
+    for q in range(2):
+        mine = (old == (own ^ q)) & (lane < experts)
+        server = jnp.sum(jnp.where(mine, new, 0), axis=1, keepdims=True)
+        theirs = (old == server) & (lane >= 6 * experts) & (lane < 7 * experts)
+        home = jnp.sum(jnp.where(theirs, booked, 0.0), axis=1, keepdims=True)[:1].astype(jnp.int32)
+        padded = ((home + (BLOCK - 1)) // BLOCK) * BLOCK
+        home_rows = jnp.where(col_q[:1] == q, padded, home_rows)
+    position = rank.astype(jnp.int32) + jnp.where(kind == 0, 0, home_rows)
+    return jnp.where(position < SERVE_BLOCKS * BLOCK, gates, 0.0)
+
+
+def load_kernel(places, in_ref, down_ref, *refs):
+    *blocks, in_out, down_out, packs, sems = refs
+    width = blocks[0].shape[1] - LANES
+    copies = [
+        pltpu.make_async_copy(ref.at[:, pl.ds(width, LANES)], packs.at[d], sems.at[i])
+        for i, (d, ref) in enumerate(zip(places, blocks))
+    ]
+    copies.append(pltpu.make_async_copy(in_ref, in_out, sems.at[len(blocks)]))
+    copies.append(pltpu.make_async_copy(down_ref, down_out, sems.at[len(blocks) + 1]))
+    for copy in copies:
+        copy.start()
+    for copy in copies:
+        copy.wait()
+
+
+def load_call(weights, blocks):
+    half, dtype = blocks[0].shape[0], blocks[0].dtype
+    return pl.pallas_call(
+        functools.partial(load_kernel, tuple(blocks)),
+        out_shape=[jax.ShapeDtypeStruct(x.shape, x.dtype) for x in weights]
+        + [jax.ShapeDtypeStruct((len(blocks) + 1, half, LANES), dtype)],
+        in_specs=[pl.BlockSpec(memory_space=pl.ANY)] * (2 + len(blocks)),
+        out_specs=[pl.BlockSpec(memory_space=pltpu.VMEM)] * 3,
+        scratch_shapes=[pltpu.SemaphoreType.DMA((2 + len(blocks),))],
+        compiler_params=pltpu.CompilerParams(vmem_limit_bytes=16 * 2**20),
+        cost_estimate=pl.CostEstimate(
+            flops=0, bytes_accessed=sum(4 * x.size for x in weights), transcendentals=0
+        ),
+    )(*weights, *blocks.values())
+
+
+def gate_lanes(q, column):
+    block, count = column
+    return [(2 * q + h) * count + block for h in range(2)]
+
+
+def expert_kernel(blocks, columns, first, *refs):
+    refs = list(refs)
+    halves = 2 * blocks
+    if first:
+        info_ref, old_ref, new_ref, packs_ref, *refs = refs
+        gates_ref, pack, pack_sem = refs.pop(halves + 4), *refs[-2:]
+        refs = refs[:-2]
+        pack_copy = pltpu.make_async_copy(
+            refs[0].at[:, pl.ds(refs[1].shape[1], LANES)], pack, pack_sem
+        )
+        pack_copy.start()
+    elif columns:
+        gates_ref, *refs = refs
+    x_all, hidden, total, x_sems = refs[-4:]
+    x_refs, weights, out_refs = refs[:halves], refs[halves : halves + 4], refs[halves + 4 : -4]
+    half = x_all.shape[0] // halves
+    rows = 2 * half
+    hidden_units, width = hidden.shape[1], x_all.shape[1]
+    tile, step = hidden_units // 3, width // 4
+    copies = [
+        pltpu.make_async_copy(
+            ref.at[:, pl.ds(0, x_all.shape[1])], x_all.at[pl.ds(i * half, half)], x_sems.at[i]
+        )
+        for i, ref in enumerate(x_refs)
+    ]
+    for copy in copies:
+        copy.start()
+    if first:
+        pack_copy.wait()
+        at = columns[0][0]
+        gates_ref[...] = served_gates(
+            info_ref,
+            old_ref,
+            new_ref,
+            [pack[...] if d == at else packs_ref[d] for d in range(packs_ref.shape[0])],
+        )
+    for copy in copies:
+        copy.wait()
+    for q in range(2):
+        in_ref, down_ref = weights[2 * q : 2 * q + 2]
+        for f in range(0, hidden_units, tile):
+            x = x_all[...]
+            gate = jnp.dot(x, in_ref[0, :, f : f + tile], preferred_element_type=jnp.float32)
+            up = jnp.dot(
+                x,
+                in_ref[0, :, hidden_units + f : hidden_units + f + tile],
+                preferred_element_type=jnp.float32,
+            )
+            hidden[:, f : f + tile] = (gate / (1.0 + jnp.exp(-gate)) * up).astype(jnp.bfloat16)
+        if columns:
+            column = jnp.concatenate(
+                [gates_ref[:, at : at + 1] for d in columns for at in gate_lanes(q, d)]
+            )
+        for n in range(0, width, step):
+            out = jnp.dot(
+                hidden[...], down_ref[0, :, n : n + step], preferred_element_type=jnp.float32
+            )
+            out = out.astype(jnp.bfloat16)
+            if not columns:
+                for i in range(blocks):
+                    out_refs[q * blocks + i][:, n : n + step] = out[i * rows : (i + 1) * rows]
+                continue
+            out = out.astype(jnp.float32) * column
+            if q == 0:
+                total[:, n : n + step] = out
+            else:
+                out = (total[:, n : n + step] + out).astype(jnp.bfloat16)
+                for i, ref in enumerate(out_refs):
+                    ref[:, n : n + step] = out[i * half : (i + 1) * half]
+
+
+def expert_call(halves, weights, columns=(), gates=(), tables=()):
+    half, width = halves[1].shape
+    hidden_units = weights[1].shape[1]
+    blocks = len(halves) // 2
+    rows = half * len(halves)
+    vmem = pl.BlockSpec(memory_space=pltpu.VMEM)
+    out = jax.ShapeDtypeStruct((half if columns else 2 * half, width), jnp.bfloat16)
+    made = [jax.ShapeDtypeStruct((half, LANES), jnp.float32)] if tables else []
+    return pl.pallas_call(
+        functools.partial(expert_kernel, blocks, columns, bool(tables)),
+        out_shape=made + [out] * len(halves),
+        in_specs=([pl.BlockSpec(memory_space=pltpu.SMEM)] * 3 + [vmem] if tables else [])
+        + [vmem] * len(gates)
+        + [pl.BlockSpec(memory_space=pl.ANY)] * len(halves)
+        + [vmem] * 4,
+        out_specs=[vmem] * (len(made) + len(halves)),
+        scratch_shapes=[
+            pltpu.VMEM((rows, width), jnp.bfloat16),
+            pltpu.VMEM((rows, hidden_units), jnp.bfloat16),
+            pltpu.VMEM((rows, width), jnp.float32),
+            pltpu.SemaphoreType.DMA((len(halves),)),
+        ]
+        + ([pltpu.VMEM((half, LANES), jnp.bfloat16), pltpu.SemaphoreType.DMA] if tables else []),
+        compiler_params=pltpu.CompilerParams(vmem_limit_bytes=16 * 2**20),
+        cost_estimate=pl.CostEstimate(
+            flops=2 * 2 * rows * width * 3 * hidden_units,
+            bytes_accessed=2 * 2 * 3 * width * hidden_units,
+            transcendentals=0,
+        ),
+    )(*tables, *gates, *halves, *weights)
+
+
+def sum_kernel(spec, gates_ref, *refs):
+    refs = list(refs)
+    outs = refs[len(refs) - len(spec) :]
+    for at, (d, h, came) in enumerate(spec):
+        so_far, refs = refs[:came], refs[came:]
+        made, refs = refs[:2], refs[2:]
+        rows = slice(h * outs[at].shape[0], (h + 1) * outs[at].shape[0])
+        total = None
+        for q in range(2):
+            lane = gate_lanes(q, d)[h]
+            term = made[q][rows, :].astype(jnp.float32) * gates_ref[:, lane : lane + 1]
+            total = term if total is None else total + term
+        for ref in so_far:
+            total = total + ref[...].astype(jnp.float32)
+        outs[at][...] = total.astype(jnp.bfloat16)
+
+
+def sum_call(gates, items):
+    half, width = items[0][3][0].shape[0] // 2, items[0][3][0].shape[1]
+    spec = [(d, h, len(came)) for d, h, came, _ in items]
+    arrays = [x for _, _, came, made in items for x in [*came, *made]]
+    return pl.pallas_call(
+        functools.partial(sum_kernel, spec),
+        out_shape=[jax.ShapeDtypeStruct((half, width), jnp.bfloat16)] * len(items),
+        in_specs=[pl.BlockSpec(memory_space=pltpu.VMEM)] * (1 + len(arrays)),
+        out_specs=[pl.BlockSpec(memory_space=pltpu.VMEM)] * len(items),
+        compiler_params=pltpu.CompilerParams(vmem_limit_bytes=16 * 2**20),
+        cost_estimate=pl.CostEstimate(
+            flops=0, bytes_accessed=8 * half * width * len(items), transcendentals=0
+        ),
+    )(gates, *arrays)
+
+
+def gathered_body(tokens, expert_ids, route_gates, expert_in, expert_out, old_place, new_place):
+    ep_size = lax.axis_size("ep")
+    devices = ep_size * 2
+    tok_rows = expert_ids.shape[0]
+    half = tok_rows // 2
+    reach = ep_size // 2
+    ring = [*range(0, ep_size, 2), *range(ep_size - 1, 0, -2)]
+    ahead = [(ring[i], ring[(i + 1) % ep_size]) for i in range(ep_size)]
+    back = [(b, a) for a, b in ahead]
+    ep = lax.axis_index("ep")
+    own = ep * 2 + lax.axis_index("dp")
+
+    def swap_cores(x):
+        return lax.ppermute(x, "dp", [(0, 1), (1, 0)])
+
+    def go(x, way):
+        return lax.ppermute(x, "ep", ahead if way > 0 else back)
+
+    def after(x, *others):
+        return lax.optimization_barrier((x, *others))[0]
+
+    vmem = pl.BlockSpec(memory_space=pltpu.VMEM)
+
+    ids, any_space = expert_ids.T, pl.BlockSpec(memory_space=pl.ANY)
+    packed, second = pl.pallas_call(
+        functools.partial(pack_kernel, devices),
+        out_shape=[
+            jax.ShapeDtypeStruct((half, tokens.shape[1] + extra), tokens.dtype)
+            for extra in (LANES, 0)
+        ],
+        in_specs=[vmem] * 3 + [any_space],
+        out_specs=[vmem] * 2,
+        scratch_shapes=[pltpu.SemaphoreType.DMA((2,))],
+    )(ids, route_gates.T, swap_cores(ids), tokens)
+
+    weights = (expert_in, expert_out, *[swap_cores(after(w, packed)) for w in (expert_in, expert_out)])
+    held = {0: [packed, second]}
+
+    def pass_on(d, *waits):
+        held[-d] = [go(after(x, *w), 1) for x, w in zip(held[1 - d], waits)]
+        held[d] = [go(after(x, *w), -1) for x, w in zip(held[d - 1], waits)]
+
+    for d in range(1, reach):
+        pass_on(d, [], [])
+    last = reach - 1
+    held[reach] = [go(held[-last][0], 1), go(held[last][1], -1)]
+    come = [held[way * last][0] for way in (1, -1)]
+    *loaded, packs = load_call(
+        [after(w, *come) for w in weights[2:]],
+        {d % ep_size: held[d][0] for d in range(-last, reach)},
+    )
+    weights = (*weights[:2], *loaded)
+    apart = expert_call([x for d in (-last, last) for x in held[d]], weights)
+    apart = {-last: apart[::2], last: apart[1::2]}
+    gates, *outs = expert_call(
+        held[reach],
+        weights,
+        ((reach, ep_size),),
+        tables=(after(own.reshape(1), apart[last][0]), old_place, new_place, packs),
+    )
+    part = {reach: outs}
+
+    def compute(distances, *waits):
+        halves = [x for d in distances for x in held[d]]
+        outs = expert_call(
+            [after(halves[0], *waits), *halves[1:]],
+            weights,
+            tuple((d % ep_size, ep_size) for d in distances),
+            (gates,),
+        )
+        for i, d in enumerate(distances):
+            part[d] = outs[2 * i : 2 * i + 2]
+
+    def gated(half_of, came):
+        outs = sum_call(
+            gates, [
+                ((way * last % ep_size, ep_size), half_of[way], came[way], apart[way * last])
+                for way in (1, -1)
+            ],
+        )
+        return dict(zip((1, -1), outs))
+
+    def add(*xs):
+        return sum(x.astype(jnp.float32) for x in xs).astype(jnp.bfloat16)
+
+    far, near = {1: 0, -1: 1}, {1: 1, -1: 0}
+    moving = {way: part[reach][far[way]] for way in (1, -1)}
+    late = gated(near, {1: [], -1: []})
+    for d in range(last, 0, -1):
+        if d < last:
+            late = {way: add(late[way], part[way * d][near[way]]) for way in (1, -1)}
+        compute([1 - d, d - 1] if d > 1 else [0], *moving.values())
+        moving = {way: go(x, way) for way, x in moving.items()}
+        late = {way: go(x, way) for way, x in late.items()}
+        moving = {way: after(x, part[1 - d][0]) for way, x in moving.items()}
+        if d == last:
+            moving = gated(far, {way: [x] for way, x in moving.items()})
+        else:
+            moving = {way: add(x, part[way * d][far[way]]) for way, x in moving.items()}
+    moving = {way: go(x, way) for way, x in moving.items()}
+    return jnp.concatenate(
+        [add(part[0][0], moving[1], late[-1]), add(part[0][1], moving[-1], late[1])]
+    )
+
+
 def solution(mesh):
     placed = (
         P(("grp", "ep", "dp"), None),
@@ -122,6 +505,12 @@
         P(),
         P(),
     )
+
+    def body(tokens, expert_ids, *rest):
+        devices = lax.axis_size("ep") * lax.axis_size("dp")
+        gathered = devices <= 2 * expert_ids.shape[1] and 7 * devices <= LANES
+        return (gathered_body if gathered else routed_body)(tokens, expert_ids, *rest)
+
     return jax.shard_map(
         body, mesh=mesh, in_specs=placed, out_specs=P(("grp", "ep", "dp"), None), check_vma=False
     )

time: 442 us -> 103 us (0.23)
  the two profiles are of different devices: /device:TPU:11 before, /device:TPU:0 now
where the time goes in v3:
time: 103 us
  starting transfers between devices  37.5 us (36%)
  Pallas kernels  31.2 us (30%)
  waiting for transfers between devices  28.9 us (28%)
  local copies, waits for them, and re-layouts  3.69 us (4%)
  other arithmetic  1.56 us (2%)
    ppermute x28, starting transfers between devices, go(): return lax.ppermute(x, 'ep', ahead if way > 0 else back)  36.4 us
    ppermute x28, waiting for transfers between devices, go(): return lax.ppermute(x, 'ep', ahead if way > 0 else back)  27.9 us
    pallas_call x5, Pallas kernels, expert_call(): pl.pallas_call(functools.partial(expert_kernel, blocks, columns, bool(tab...  24.3 us
    pallas_call x1, Pallas kernels, load_call(): pl.pallas_call(functools.partial(load_kernel, tuple(blocks)), out_shape=[...  3.82 us
    unnamed x30, local copies, waits for them, and re-layouts  3.69 us
    pallas_call x1, Pallas kernels, gathered_body(): pl.pallas_call(functools.partial(pack_kernel, devices), out_shape=[jax.Sh...  2.56 us
  transfers between devices with their start and end apart: 31, of which 12 were waited for; matrix products, arithmetic and copies ran while one was open for 1% of the time, Pallas kernels for 24%

profile of v3, /device:TPU:0, one launch (start us, length us, event | category | flops | bytes accessed | tf_op | source)
XLA Modules:
  0.0 103.1 jit_solution(89661664942664191)
XLA Ops:
  0.0 0.5 collective-permute-start
  0.5 1.0 %collective-permute-done.mate_ref = s32[8,128]{1,0:T(8,128)S(1)} collective-permute-done((s32[8,128]{1,0:T(8,128)}, s32[8,128]{1,0:T(8,128)S(1)}, u32[]{:S(2)}, u32[]{:S(2)}) %collective-permute-start) | collective-permute-done | bytes 4128 | tf_op jit(solution)/shard_map/ppermute | solution.py:406
  1.5 0.6 copy-done.12
  2.1 2.6 %shard_map.73 = (bf16[64,2176]{1,0:T(8,128)(2,1)}, bf16[64,2048]{1,0:T(8,128)(2,1)}) custom-call(s32[8,128]{1,0:T(8,128)} %bitcast.6, f32[8,128]{1,0:T(8,128)} %bitcast.7, s32[8,128]{1,0:T(8,128)} %copy-done.12, bf16[128,2048]{1,0:T(8,128)(2,1)} %tokens_ref.1), custom_call_target="tpu_custom_call" | custom-call | tf_op jit(solution)/shard_map/pallas_call | solution.py:417
  4.6 0.4 collective-permute-start.13
  5.0 0.2 collective-permute-start.14
  5.2 2.8 %collective-permute-start.10 = (bf16[64,2048]{1,0:T(8,128)(2,1)}, bf16[64,2048]{1,0:T(8,128)(2,1)S(1)}, u32[]{:S(2)}, u32[]{:S(2)}) collective-permute-start(bf16[64,2048]{1,0:T(8,128)(2,1)} %get-tuple-element.46.refs_2_), channel_id=1, source_target_pairs={{4,0},{8,4},{12,8},{14,12},{10,14},{6,10},{2,6},{0,2},{5,1},{9,5},... | collective-permute-start | bytes 786440 | tf_op jit(solution)/shard_map/ppermute | solution.py:409
  8.0 0.1 collective-permute-start.1
  8.1 1.9 %collective-permute-start.7 = (bf16[64,2176]{1,0:T(8,128)(2,1)}, bf16[64,2176]{1,0:T(8,128)(2,1)S(1)}, u32[]{:S(2)}, u32[]{:S(2)}) collective-permute-start(bf16[64,2176]{1,0:T(8,128)(2,1)} %get-tuple-element.74.refs_3_.refs_1_), channel_id=1, source_target_pairs={{4,0},{8,4},{12,8},{14,12},{10,14},{6,10},{2,6},{0,2},{5,1},{9,5},... | collective-permute-start | bytes 835592 | tf_op jit(solution)/shard_map/ppermute | solution.py:409
  10.1 5.4 %collective-permute-done.10.refs_4_ = bf16[64,2048]{1,0:T(8,128)(2,1)S(1)} collective-permute-done((bf16[64,2048]{1,0:T(8,128)(2,1)}, bf16[64,2048]{1,0:T(8,128)(2,1)S(1)}, u32[]{:S(2)}, u32[]{:S(2)}) %collective-permute-start.10) | collective-permute-done | bytes 262176 | tf_op jit(solution)/shard_map/ppermute | solution.py:409
  15.4 2.1 %collective-permute-start.4 = (bf16[64,2048]{1,0:T(8,128)(2,1)}, bf16[64,2048]{1,0:T(8,128)(2,1)S(1)}, u32[]{:S(2)}, u32[]{:S(2)}) collective-permute-start(bf16[64,2048]{1,0:T(8,128)(2,1)} %get-tuple-element.46.refs_2_), channel_id=1, source_target_pairs={{0,4},{4,8},{8,12},{12,14},{14,10},{10,6},{6,2},{2,0},{1,5},{5,9},... | collective-permute-start | bytes 786440 | tf_op jit(solution)/shard_map/ppermute | solution.py:409
  17.5 0.8 collective-permute-start.11
  18.3 0.7 copy-done.4
  19.0 2.4 %collective-permute-done.7.refs_4_.refs_3_ = bf16[64,2176]{1,0:T(8,128)(2,1)S(1)} collective-permute-done((bf16[64,2176]{1,0:T(8,128)(2,1)}, bf16[64,2176]{1,0:T(8,128)(2,1)S(1)}, u32[]{:S(2)}, u32[]{:S(2)}) %collective-permute-start.7) | collective-permute-done | bytes 278560 | tf_op jit(solution)/shard_map/ppermute | solution.py:409
  21.4 2.1 %collective-permute-start.2 = (bf16[64,2176]{1,0:T(8,128)(2,1)S(1)}, bf16[64,2176]{1,0:T(8,128)(2,1)S(1)}, u32[]{:S(2)}, u32[]{:S(2)}) collective-permute-start(bf16[64,2176]{1,0:T(8,128)(2,1)S(1)} %collective-permute-done.1.refs_2_.refs_1_), channel_id=1, source_target_pairs={{0,4},{4,8},{8,12},{12,14},{14,10},{10,6},{6,2},{2,0},{1,5},{5,9},... | collective-permute-start | bytes 835592 | tf_op jit(solution)/shard_map/ppermute | solution.py:409
  23.5 0.9 collective-permute-start.8
  24.4 2.6 %collective-permute-done.11.refs_4_ = bf16[64,2048]{1,0:T(8,128)(2,1)S(1)} collective-permute-done((bf16[64,2048]{1,0:T(8,128)(2,1)S(1)}, bf16[64,2048]{1,0:T(8,128)(2,1)S(1)}, u32[]{:S(2)}, u32[]{:S(2)}) %collective-permute-start.11) | collective-permute-done | bytes 262176 | tf_op jit(solution)/shard_map/ppermute | solution.py:409
  27.0 2.1 %collective-permute-start.5 = (bf16[64,2048]{1,0:T(8,128)(2,1)S(1)}, bf16[64,2048]{1,0:T(8,128)(2,1)}, u32[]{:S(2)}, u32[]{:S(2)}) collective-permute-start(bf16[64,2048]{1,0:T(8,128)(2,1)S(1)} %collective-permute-done.4.refs_2_), channel_id=1, source_target_pairs={{0,4},{4,8},{8,12},{12,14},{14,10},{10,6},{6,2},{2,0},{1,5},{5,9},... | collective-permute-start | bytes 786440 | tf_op jit(solution)/shard_map/ppermute | solution.py:409
  29.1 0.7 copy-done.6
  29.8 1.0 collective-permute-start.12
  30.8 0.7 copy-done.8
  31.5 1.6 %collective-permute-done.8.refs_5_.refs_3_ = bf16[64,2176]{1,0:T(8,128)(2,1)S(1)} collective-permute-done((bf16[64,2176]{1,0:T(8,128)(2,1)S(1)}, bf16[64,2176]{1,0:T(8,128)(2,1)S(1)}, u32[]{:S(2)}, u32[]{:S(2)}) %collective-permute-start.8) | collective-permute-done | bytes 278560 | tf_op jit(solution)/shard_map/ppermute | solution.py:409
  33.1 2.0 %collective-permute-start.3 = (bf16[64,2176]{1,0:T(8,128)(2,1)S(1)}, bf16[64,2176]{1,0:T(8,128)(2,1)S(1)}, u32[]{:S(2)}, u32[]{:S(2)}) collective-permute-start(bf16[64,2176]{1,0:T(8,128)(2,1)S(1)} %collective-permute-done.2.refs_1_), channel_id=1, source_target_pairs={{0,4},{4,8},{8,12},{12,14},{14,10},{10,6},{6,2},{2,0},{1,5},{5,9},... | collective-permute-start | bytes 835592 | tf_op jit(solution)/shard_map/ppermute | solution.py:409
  35.0 1.2 %collective-permute-start.9 = (bf16[64,2176]{1,0:T(8,128)(2,1)S(1)}, bf16[64,2176]{1,0:T(8,128)(2,1)}, u32[]{:S(2)}, u32[]{:S(2)}) collective-permute-start(bf16[64,2176]{1,0:T(8,128)(2,1)S(1)} %collective-permute-done.8.refs_5_.refs_3_), channel_id=1, source_target_pairs={{4,0},{8,4},{12,8},{14,12},{10,14},{6,10},{2,6},{0,2},{5,1},{9,5},... | collective-permute-start | bytes 835592 | tf_op jit(solution)/shard_map/ppermute | solution.py:409
  36.2 2.9 %collective-permute-done.12.refs_3_ = bf16[64,2048]{1,0:T(8,128)(2,1)} collective-permute-done((bf16[64,2048]{1,0:T(8,128)(2,1)S(1)}, bf16[64,2048]{1,0:T(8,128)(2,1)}, u32[]{:S(2)}, u32[]{:S(2)}) %collective-permute-start.12) | collective-permute-done | bytes 262176 | tf_op jit(solution)/shard_map/ppermute | solution.py:409
  39.1 1.6 %collective-permute-start.6 = (bf16[64,2048]{1,0:T(8,128)(2,1)}, bf16[64,2048]{1,0:T(8,128)(2,1)}, u32[]{:S(2)}, u32[]{:S(2)}) collective-permute-start(bf16[64,2048]{1,0:T(8,128)(2,1)} %collective-permute-done.5.refs_2_), channel_id=1, source_target_pairs={{0,4},{4,8},{8,12},{12,14},{14,10},{10,6},{6,2},{2,0},{1,5},{5,9},... | collective-permute-start | bytes 786440 | tf_op jit(solution)/shard_map/ppermute | solution.py:409
  40.8 0.4 collective-permute-done.3.refs_0_
  41.2 1.1 %collective-permute-start.16 = (bf16[64,2048]{1,0:T(8,128)(2,1)}, bf16[64,2048]{1,0:T(8,128)(2,1)S(1)}, u32[]{:S(2)}, u32[]{:S(2)}) collective-permute-start(bf16[64,2048]{1,0:T(8,128)(2,1)} %collective-permute-done.12.refs_3_), channel_id=1, source_target_pairs={{4,0},{8,4},{12,8},{14,12},{10,14},{6,10},{2,6},{0,2},{5,1},{9,5},... | collective-permute-start | bytes 786440 | tf_op jit(solution)/shard_map/ppermute | solution.py:409
  42.3 2.8 %collective-permute-done.9.refs_6_.refs_2_ = bf16[64,2176]{1,0:T(8,128)(2,1)} collective-permute-done((bf16[64,2176]{1,0:T(8,128)(2,1)S(1)}, bf16[64,2176]{1,0:T(8,128)(2,1)}, u32[]{:S(2)}, u32[]{:S(2)}) %collective-permute-start.9) | collective-permute-done | bytes 278560 | tf_op jit(solution)/shard_map/ppermute | solution.py:409
  45.1 1.6 %collective-permute-start.15 = (bf16[64,2176]{1,0:T(8,128)(2,1)S(1)}, bf16[64,2176]{1,0:T(8,128)(2,1)S(1)}, u32[]{:S(2)}, u32[]{:S(2)}) collective-permute-start(bf16[64,2176]{1,0:T(8,128)(2,1)S(1)} %collective-permute-done.3.refs_0_), channel_id=1, source_target_pairs={{0,4},{4,8},{8,12},{12,14},{14,10},{10,6},{6,2},{2,0},{1,5},{5,9},... | collective-permute-start | bytes 835592 | tf_op jit(solution)/shard_map/ppermute | solution.py:409
  46.7 1.0 copy-done.1
  47.7 3.8 %shard_map.74 = (bf16[1,2048,1536]{2,1,0:T(8,128)(2,1)S(1)}, bf16[1,768,2048]{2,1,0:T(8,128)(2,1)S(1)}, bf16[8,64,128]{2,1,0:T(8,128)(2,1)S(1)}) custom-call(bf16[1,2048,1536]{2,1,0:T(8,128)(2,1)} %collective-permute-done.13.in_ref, bf16[1,768,2048]{2,1,0:T(8,128)(2,1)} %collective-permute-done.14.down_ref, ...), custom_call_target="tpu_custom_call" | custom-call | bytes 18874368 | tf_op jit(solution)/shard_map/pallas_call | solution.py:238
  51.6 6.2 %shard_map.75 = (bf16[128,2048]{1,0:T(8,128)(2,1)S(1)}, bf16[128,2048]{1,0:T(8,128)(2,1)S(1)}, bf16[128,2048]{1,0:T(8,128)(2,1)S(1)}, bf16[128,2048]{1,0:T(8,128)(2,1)S(1)}) custom-call(bf16[64,2176]{1,0:T(8,128)(2,1)S(1)} %collective-permute-done.3.refs_0_, bf16[64,2048]{1,0:T(8,128)(2,1)} %collective-permute-done.6.refs_1_, ...), custom_call_target="tpu_custom_call" | custom-call | flops 4831838208 | bytes 18874368 | tf_op jit(solution)/shard_map/pallas_call | solution.py:336
  57.9 3.9 %shard_map.76 = (f32[64,128]{1,0:T(8,128)S(1)}, bf16[64,2048]{1,0:T(8,128)(2,1)S(1)}, bf16[64,2048]{1,0:T(8,128)(2,1)S(1)}) custom-call(s32[1]{0:T(128)} %bitcast.refs_0_, s32[16]{0:T(128)S(1)} %copy-done.10, s32[16]{0:T(128)S(1)} %copy-done.11, bf16[8,64,128]{2,1,0:T(8,128)(2,1)S(1)} %get-tuple-element.55.refs_3_, ...), custom_call_target="tpu_custom_call" | custom-call | flops 2415919104 | bytes 18874368 | tf_op jit(solution)/shard_map/pallas_call | solution.py:336
  61.8 0.4 collective-permute-start.18
  62.2 1.6 %collective-permute-start.17 = (bf16[64,2048]{1,0:T(8,128)(2,1)S(1)}, bf16[64,2048]{1,0:T(8,128)(2,1)S(1)}, u32[]{:S(2)}, u32[]{:S(2)}) collective-permute-start(bf16[64,2048]{1,0:T(8,128)(2,1)S(1)} %get-tuple-element.57), channel_id=1, source_target_pairs={{0,4},{4,8},{8,12},{12,14},{14,10},{10,6},{6,2},{2,0},{1,5},{5,9},... | collective-permute-start | bytes 786440 | tf_op jit(solution)/shard_map/ppermute | solution.py:409
  63.8 0.3 shard_map.81
  64.1 0.4 collective-permute-start.23
  64.5 1.6 %collective-permute-start.28 = (bf16[64,2048]{1,0:T(8,128)(2,1)S(1)}, bf16[64,2048]{1,0:T(8,128)(2,1)S(1)}, u32[]{:S(2)}, u32[]{:S(2)}) collective-permute-start(bf16[64,2048]{1,0:T(8,128)(2,1)S(1)} %get-tuple-element.82), channel_id=1, source_target_pairs={{0,4},{4,8},{8,12},{12,14},{14,10},{10,6},{6,2},{2,0},{1,5},{5,9},... | collective-permute-start | bytes 786440 | tf_op jit(solution)/shard_map/ppermute | solution.py:409
  66.2 6.1 %shard_map.77 = (bf16[64,2048]{1,0:T(8,128)(2,1)S(1)}, bf16[64,2048]{1,0:T(8,128)(2,1)S(1)}, bf16[64,2048]{1,0:T(8,128)(2,1)S(1)}, bf16[64,2048]{1,0:T(8,128)(2,1)S(1)}) custom-call(f32[64,128]{1,0:T(8,128)S(1)} %get-tuple-element.56.refs_0_.gates_ref, bf16[64,2176]{1,0:T(8,128)(2,1)S(1)} %collective-permute-done.2.refs_1_, ...), custom_call_target="tpu_custom_call" | custom-call | flops 4831838208 | bytes 18874368 | tf_op jit(solution)/shard_map/pallas_call | solution.py:336
  72.3 0.3 shard_map.78
  72.7 1.6 %collective-permute-start.19 = (bf16[64,2048]{1,0:T(8,128)(2,1)S(1)}, bf16[64,2048]{1,0:T(8,128)(2,1)S(1)}, u32[]{:S(2)}, u32[]{:S(2)}) collective-permute-start(bf16[64,2048]{1,0:T(8,128)(2,1)S(1)} %get-tuple-element.66), channel_id=1, source_target_pairs={{0,4},{4,8},{8,12},{12,14},{14,10},{10,6},{6,2},{2,0},{1,5},{5,9},... | collective-permute-start | bytes 786440 | tf_op jit(solution)/shard_map/ppermute | solution.py:409
  74.3 0.5 collective-permute-start.20
  74.7 0.1 add_convert_fusion.6
  74.8 0.5 collective-permute-start.24
  75.3 0.1 add_convert_fusion.2
  75.4 1.8 %collective-permute-start.29 = (bf16[64,2048]{1,0:T(8,128)(2,1)S(1)}, bf16[64,2048]{1,0:T(8,128)(2,1)S(1)}, u32[]{:S(2)}, u32[]{:S(2)}) collective-permute-start(bf16[64,2048]{1,0:T(8,128)(2,1)S(1)} %add_convert_fusion.2), channel_id=1, source_target_pairs={{0,4},{4,8},{8,12},{12,14},{14,10},{10,6},{6,2},{2,0},{1,5},{5,9},... | collective-permute-start | bytes 786440 | tf_op jit(solution)/shard_map/ppermute | solution.py:409
  77.3 5.2 %shard_map.79 = (bf16[64,2048]{1,0:T(8,128)(2,1)S(1)}, bf16[64,2048]{1,0:T(8,128)(2,1)S(1)}, bf16[64,2048]{1,0:T(8,128)(2,1)S(1)}, bf16[64,2048]{1,0:T(8,128)(2,1)S(1)}) custom-call(f32[64,128]{1,0:T(8,128)S(1)} %get-tuple-element.56.refs_0_.gates_ref, bf16[64,2176]{1,0:T(8,128)(2,1)S(1)} %collective-permute-done.1.refs_2_.refs_1_, ...), custom_call_target="tpu_custom_call" | custom-call | flops 4831838208 | bytes 18874368 | tf_op jit(solution)/shard_map/pallas_call | solution.py:336
  82.5 0.1 add_convert_fusion.9
  82.6 1.7 %collective-permute-start.21 = (bf16[64,2048]{1,0:T(8,128)(2,1)S(1)}, bf16[64,2048]{1,0:T(8,128)(2,1)S(1)}, u32[]{:S(2)}, u32[]{:S(2)}) collective-permute-start(bf16[64,2048]{1,0:T(8,128)(2,1)S(1)} %add_convert_fusion.9), channel_id=1, source_target_pairs={{0,4},{4,8},{8,12},{12,14},{14,10},{10,6},{6,2},{2,0},{1,5},{5,9},... | collective-permute-start | bytes 786440 | tf_op jit(solution)/shard_map/ppermute | solution.py:409
  84.4 0.4 collective-permute-start.26
  84.8 2.9 %collective-permute-done.24 = bf16[64,2048]{1,0:T(8,128)(2,1)S(1)} collective-permute-done((bf16[64,2048]{1,0:T(8,128)(2,1)S(1)}, bf16[64,2048]{1,0:T(8,128)(2,1)S(1)}, u32[]{:S(2)}, u32[]{:S(2)}) %collective-permute-start.24) | collective-permute-done | bytes 262176 | tf_op jit(solution)/shard_map/ppermute | solution.py:409
  87.7 0.1 add_convert_fusion.5
  87.7 0.4 collective-permute-start.25
  88.2 2.0 %collective-permute-start.30 = (bf16[64,2048]{1,0:T(8,128)(2,1)S(1)}, bf16[64,2048]{1,0:T(8,128)(2,1)S(1)}, u32[]{:S(2)}, u32[]{:S(2)}) collective-permute-start(bf16[64,2048]{1,0:T(8,128)(2,1)S(1)} %add_convert_fusion.1), channel_id=1, source_target_pairs={{0,4},{4,8},{8,12},{12,14},{14,10},{10,6},{6,2},{2,0},{1,5},{5,9},... | collective-permute-start | bytes 786440 | tf_op jit(solution)/shard_map/ppermute | solution.py:409
  90.2 2.8 %shard_map.80 = (bf16[64,2048]{1,0:T(8,128)(2,1)S(1)}, bf16[64,2048]{1,0:T(8,128)(2,1)S(1)}) custom-call(f32[64,128]{1,0:T(8,128)S(1)} %get-tuple-element.56.refs_0_.gates_ref, bf16[64,2176]{1,0:T(8,128)(2,1)S(1)} %copy-done.2, bf16[64,2048]{1,0:T(8,128)(2,1)S(1)} %copy-done.3, bf16[1,2048,1536]{2,1,0:T(8,128)(2,1)S(1)} %bitcast.4, ...), custom_call_target="tpu_custom_call" | custom-call | flops 2415919104 | bytes 18874368 | tf_op jit(solution)/shard_map/pallas_call | solution.py:336
  93.0 0.2 collective-permute-done.21
  93.3 1.6 %collective-permute-start.22 = (bf16[64,2048]{1,0:T(8,128)(2,1)S(1)}, bf16[64,2048]{1,0:T(8,128)(2,1)S(1)}, u32[]{:S(2)}, u32[]{:S(2)}) collective-permute-start(bf16[64,2048]{1,0:T(8,128)(2,1)S(1)} %add_convert_fusion.7), channel_id=1, source_target_pairs={{0,4},{4,8},{8,12},{12,14},{14,10},{10,6},{6,2},{2,0},{1,5},{5,9},... | collective-permute-start | bytes 786440 | tf_op jit(solution)/shard_map/ppermute | solution.py:409
  94.9 0.5 collective-permute-start.27
  95.5 3.7 %collective-permute-done.25 = bf16[64,2048]{1,0:T(8,128)(2,1)S(1)} collective-permute-done((bf16[64,2048]{1,0:T(8,128)(2,1)S(1)}, bf16[64,2048]{1,0:T(8,128)(2,1)S(1)}, u32[]{:S(2)}, u32[]{:S(2)}) %collective-permute-start.25) | collective-permute-done | bytes 262176 | tf_op jit(solution)/shard_map/ppermute | solution.py:409
  99.2 2.9 %collective-permute-done.22 = bf16[64,2048]{1,0:T(8,128)(2,1)S(1)} collective-permute-done((bf16[64,2048]{1,0:T(8,128)(2,1)S(1)}, bf16[64,2048]{1,0:T(8,128)(2,1)S(1)}, u32[]{:S(2)}, u32[]{:S(2)}) %collective-permute-start.22) | collective-permute-done | bytes 262176 | tf_op jit(solution)/shard_map/ppermute | solution.py:409
  102.1 0.1 add_convert_fusion.4
  102.2 0.1 add_convert_fusion
  102.3 0.8 pad_maximum_fusion
  (49 shorter events, 0.4 us)
Async XLA Ops:
  0.0 51.5 %slice-start = ((s8[6291456]{0:T(1024)(128)(4,1)}), s8[2097152]{0:T(1024)(128)(4,1)S(1)}, s32[]{:S(2)}) async-start(s8[6291456]{0:T(1024)(128)(4,1)} %bitcast.3), calls=%async_computation | async-start | bytes 4194304
  0.0 1.5 %collective-permute-start = (s32[8,128]{1,0:T(8,128)}, s32[8,128]{1,0:T(8,128)S(1)}, u32[]{:S(2)}, u32[]{:S(2)}) collective-permute-start(s32[8,128]{1,0:T(8,128)} %bitcast.5), channel_id=1, source_target_pairs={{0,1},{1,0},{2,3},{3,2},{4,5},{5,4},{6,7},{7,6},{8,9},{9,8},{10,11... | collective-permute-start | bytes 12296 | tf_op jit(solution)/shard_map/ppermute | solution.py:406
  1.5 0.6 copy-start.12
  4.6 42.1 %collective-permute-start.13 = (bf16[1,2048,1536]{2,1,0:T(8,128)(2,1)}, bf16[1,2048,1536]{2,1,0:T(8,128)(2,1)}, u32[]{:S(2)}, u32[]{:S(2)}) collective-permute-start(bf16[1,2048,1536]{2,1,0:T(8,128)(2,1)} %refs_3_.1), channel_id=1, source_target_pairs={{0,1},{1,0},{2,3},{3,2},{4,5},{5,4},{6,7},{7,6},{8,9},{9,8},{10,11... | collective-permute-start | bytes 18874376 | tf_op jit(solution)/shard_map/ppermute | solution.py:406
  5.0 41.7 %collective-permute-start.14 = (bf16[1,768,2048]{2,1,0:T(8,128)(2,1)}, bf16[1,768,2048]{2,1,0:T(8,128)(2,1)}, u32[]{:S(2)}, u32[]{:S(2)}) collective-permute-start(bf16[1,768,2048]{2,1,0:T(8,128)(2,1)} %refs_4_.3), channel_id=1, source_target_pairs={{0,1},{1,0},{2,3},{3,2},{4,5},{5,4},{6,7},{7,6},{8,9},{9,8},{10,11... | collective-permute-start | bytes 9437192 | tf_op jit(solution)/shard_map/ppermute | solution.py:406
  5.2 10.2 %collective-permute-start.10 = (bf16[64,2048]{1,0:T(8,128)(2,1)}, bf16[64,2048]{1,0:T(8,128)(2,1)S(1)}, u32[]{:S(2)}, u32[]{:S(2)}) collective-permute-start(bf16[64,2048]{1,0:T(8,128)(2,1)} %get-tuple-element.46.refs_2_), channel_id=1, source_target_pairs={{4,0},{8,4},{12,8},{14,12},{10,14},{6,10},{2,6},{0,2},{5,1},{9,5},... | collective-permute-start | bytes 786440 | tf_op jit(solution)/shard_map/ppermute | solution.py:409
  8.0 9.5 %collective-permute-start.1 = (bf16[64,2176]{1,0:T(8,128)(2,1)}, bf16[64,2176]{1,0:T(8,128)(2,1)S(1)}, u32[]{:S(2)}, u32[]{:S(2)}) collective-permute-start(bf16[64,2176]{1,0:T(8,128)(2,1)} %get-tuple-element.74.refs_3_.refs_1_), channel_id=1, source_target_pairs={{0,4},{4,8},{8,12},{12,14},{14,10},{10,6},{6,2},{2,0},{1,5},{5,9},... | collective-permute-start | bytes 835592 | tf_op jit(solution)/shard_map/ppermute | solution.py:409
  8.1 13.3 %collective-permute-start.7 = (bf16[64,2176]{1,0:T(8,128)(2,1)}, bf16[64,2176]{1,0:T(8,128)(2,1)S(1)}, u32[]{:S(2)}, u32[]{:S(2)}) collective-permute-start(bf16[64,2176]{1,0:T(8,128)(2,1)} %get-tuple-element.74.refs_3_.refs_1_), channel_id=1, source_target_pairs={{4,0},{8,4},{12,8},{14,12},{10,14},{6,10},{2,6},{0,2},{5,1},{9,5},... | collective-permute-start | bytes 835592 | tf_op jit(solution)/shard_map/ppermute | solution.py:409
  15.4 8.0 %collective-permute-start.4 = (bf16[64,2048]{1,0:T(8,128)(2,1)}, bf16[64,2048]{1,0:T(8,128)(2,1)S(1)}, u32[]{:S(2)}, u32[]{:S(2)}) collective-permute-start(bf16[64,2048]{1,0:T(8,128)(2,1)} %get-tuple-element.46.refs_2_), channel_id=1, source_target_pairs={{0,4},{4,8},{8,12},{12,14},{14,10},{10,6},{6,2},{2,0},{1,5},{5,9},... | collective-permute-start | bytes 786440 | tf_op jit(solution)/shard_map/ppermute | solution.py:409
  17.5 9.5 %collective-permute-start.11 = (bf16[64,2048]{1,0:T(8,128)(2,1)S(1)}, bf16[64,2048]{1,0:T(8,128)(2,1)S(1)}, u32[]{:S(2)}, u32[]{:S(2)}) collective-permute-start(bf16[64,2048]{1,0:T(8,128)(2,1)S(1)} %collective-permute-done.10.refs_4_), channel_id=1, source_target_pairs={{4,0},{8,4},{12,8},{14,12},{10,14},{6,10},{2,6},{0,2},{5,1},{9,5},... | collective-permute-start | bytes 786440 | tf_op jit(solution)/shard_map/ppermute | solution.py:409
  18.3 0.7 copy-start.4
  21.4 8.4 %collective-permute-start.2 = (bf16[64,2176]{1,0:T(8,128)(2,1)S(1)}, bf16[64,2176]{1,0:T(8,128)(2,1)S(1)}, u32[]{:S(2)}, u32[]{:S(2)}) collective-permute-start(bf16[64,2176]{1,0:T(8,128)(2,1)S(1)} %collective-permute-done.1.refs_2_.refs_1_), channel_id=1, source_target_pairs={{0,4},{4,8},{8,12},{12,14},{14,10},{10,6},{6,2},{2,0},{1,5},{5,9},... | collective-permute-start | bytes 835592 | tf_op jit(solution)/shard_map/ppermute | solution.py:409
  23.5 9.6 %collective-permute-start.8 = (bf16[64,2176]{1,0:T(8,128)(2,1)S(1)}, bf16[64,2176]{1,0:T(8,128)(2,1)S(1)}, u32[]{:S(2)}, u32[]{:S(2)}) collective-permute-start(bf16[64,2176]{1,0:T(8,128)(2,1)S(1)} %collective-permute-done.7.refs_4_.refs_3_), channel_id=1, source_target_pairs={{4,0},{8,4},{12,8},{14,12},{10,14},{6,10},{2,6},{0,2},{5,1},{9,5},... | collective-permute-start | bytes 835592 | tf_op jit(solution)/shard_map/ppermute | solution.py:409
  27.0 8.0 %collective-permute-start.5 = (bf16[64,2048]{1,0:T(8,128)(2,1)S(1)}, bf16[64,2048]{1,0:T(8,128)(2,1)}, u32[]{:S(2)}, u32[]{:S(2)}) collective-permute-start(bf16[64,2048]{1,0:T(8,128)(2,1)S(1)} %collective-permute-done.4.refs_2_), channel_id=1, source_target_pairs={{0,4},{4,8},{8,12},{12,14},{14,10},{10,6},{6,2},{2,0},{1,5},{5,9},... | collective-permute-start | bytes 786440 | tf_op jit(solution)/shard_map/ppermute | solution.py:409
  29.1 0.7 copy-start.6
  29.8 9.3 %collective-permute-start.12 = (bf16[64,2048]{1,0:T(8,128)(2,1)S(1)}, bf16[64,2048]{1,0:T(8,128)(2,1)}, u32[]{:S(2)}, u32[]{:S(2)}) collective-permute-start(bf16[64,2048]{1,0:T(8,128)(2,1)S(1)} %collective-permute-done.11.refs_4_), channel_id=1, source_target_pairs={{4,0},{8,4},{12,8},{14,12},{10,14},{6,10},{2,6},{0,2},{5,1},{9,5},... | collective-permute-start | bytes 786440 | tf_op jit(solution)/shard_map/ppermute | solution.py:409
  30.8 0.7 copy-start.8
  33.1 8.1 %collective-permute-start.3 = (bf16[64,2176]{1,0:T(8,128)(2,1)S(1)}, bf16[64,2176]{1,0:T(8,128)(2,1)S(1)}, u32[]{:S(2)}, u32[]{:S(2)}) collective-permute-start(bf16[64,2176]{1,0:T(8,128)(2,1)S(1)} %collective-permute-done.2.refs_1_), channel_id=1, source_target_pairs={{0,4},{4,8},{8,12},{12,14},{14,10},{10,6},{6,2},{2,0},{1,5},{5,9},... | collective-permute-start | bytes 835592 | tf_op jit(solution)/shard_map/ppermute | solution.py:409
  35.0 10.1 %collective-permute-start.9 = (bf16[64,2176]{1,0:T(8,128)(2,1)S(1)}, bf16[64,2176]{1,0:T(8,128)(2,1)}, u32[]{:S(2)}, u32[]{:S(2)}) collective-permute-start(bf16[64,2176]{1,0:T(8,128)(2,1)S(1)} %collective-permute-done.8.refs_5_.refs_3_), channel_id=1, source_target_pairs={{4,0},{8,4},{12,8},{14,12},{10,14},{6,10},{2,6},{0,2},{5,1},{9,5},... | collective-permute-start | bytes 835592 | tf_op jit(solution)/shard_map/ppermute | solution.py:409
  39.1 12.4 %collective-permute-start.6 = (bf16[64,2048]{1,0:T(8,128)(2,1)}, bf16[64,2048]{1,0:T(8,128)(2,1)}, u32[]{:S(2)}, u32[]{:S(2)}) collective-permute-start(bf16[64,2048]{1,0:T(8,128)(2,1)} %collective-permute-done.5.refs_2_), channel_id=1, source_target_pairs={{0,4},{4,8},{8,12},{12,14},{14,10},{10,6},{6,2},{2,0},{1,5},{5,9},... | collective-permute-start | bytes 786440 | tf_op jit(solution)/shard_map/ppermute | solution.py:409
  40.8 10.8 %slice-start.1 = ((s8[6291456]{0:T(1024)(128)(4,1)}), s8[4194304]{0:T(1024)(128)(4,1)S(1)}, s32[]{:S(2)}) async-start(s8[6291456]{0:T(1024)(128)(4,1)} %bitcast.3), calls=%async_computation.1 | async-start | bytes 8388608
  40.8 10.8 %copy-start = (bf16[1,768,2048]{2,1,0:T(8,128)(2,1)S(1)}, bf16[1,768,2048]{2,1,0:T(8,128)(2,1)}, u32[]{:S(2)}) copy-start(bf16[1,768,2048]{2,1,0:T(8,128)(2,1)} %refs_4_.3) | copy-start | bytes 9437188
  41.2 16.7 %collective-permute-start.16 = (bf16[64,2048]{1,0:T(8,128)(2,1)}, bf16[64,2048]{1,0:T(8,128)(2,1)S(1)}, u32[]{:S(2)}, u32[]{:S(2)}) collective-permute-start(bf16[64,2048]{1,0:T(8,128)(2,1)} %collective-permute-done.12.refs_3_), channel_id=1, source_target_pairs={{4,0},{8,4},{12,8},{14,12},{10,14},{6,10},{2,6},{0,2},{5,1},{9,5},... | collective-permute-start | bytes 786440 | tf_op jit(solution)/shard_map/ppermute | solution.py:409
  45.1 12.7 %collective-permute-start.15 = (bf16[64,2176]{1,0:T(8,128)(2,1)S(1)}, bf16[64,2176]{1,0:T(8,128)(2,1)S(1)}, u32[]{:S(2)}, u32[]{:S(2)}) collective-permute-start(bf16[64,2176]{1,0:T(8,128)(2,1)S(1)} %collective-permute-done.3.refs_0_), channel_id=1, source_target_pairs={{0,4},{4,8},{8,12},{12,14},{14,10},{10,6},{6,2},{2,0},{1,5},{5,9},... | collective-permute-start | bytes 835592 | tf_op jit(solution)/shard_map/ppermute | solution.py:409
  46.7 1.0 copy-start.1
  51.6 6.3 %copy-start.10 = (s32[16]{0:T(128)S(1)}, s32[16]{0:T(128)}, u32[]{:S(2)}) copy-start(s32[16]{0:T(128)} %refs_1_.1) | copy-start | bytes 196
  51.6 6.3 %copy-start.11 = (s32[16]{0:T(128)S(1)}, s32[16]{0:T(128)}, u32[]{:S(2)}) copy-start(s32[16]{0:T(128)} %refs_2_.1) | copy-start | bytes 196
  57.9 8.3 %copy-start.9 = (bf16[64,2048]{1,0:T(8,128)(2,1)S(1)}, bf16[64,2048]{1,0:T(8,128)(2,1)}, u32[]{:S(2)}) copy-start(bf16[64,2048]{1,0:T(8,128)(2,1)} %copy-done.8) | copy-start | bytes 786436
  61.8 10.5 %collective-permute-start.18 = (bf16[64,2048]{1,0:T(8,128)(2,1)S(1)}, bf16[64,2048]{1,0:T(8,128)(2,1)S(1)}, u32[]{:S(2)}, u32[]{:S(2)}) collective-permute-start(bf16[64,2048]{1,0:T(8,128)(2,1)S(1)} %get-tuple-element.58), channel_id=1, source_target_pairs={{4,0},{8,4},{12,8},{14,12},{10,14},{6,10},{2,6},{0,2},{5,1},{9,5},... | collective-permute-start | bytes 786440 | tf_op jit(solution)/shard_map/ppermute | solution.py:409
  62.2 10.1 %collective-permute-start.17 = (bf16[64,2048]{1,0:T(8,128)(2,1)S(1)}, bf16[64,2048]{1,0:T(8,128)(2,1)S(1)}, u32[]{:S(2)}, u32[]{:S(2)}) collective-permute-start(bf16[64,2048]{1,0:T(8,128)(2,1)S(1)} %get-tuple-element.57), channel_id=1, source_target_pairs={{0,4},{4,8},{8,12},{12,14},{14,10},{10,6},{6,2},{2,0},{1,5},{5,9},... | collective-permute-start | bytes 786440 | tf_op jit(solution)/shard_map/ppermute | solution.py:409
  64.1 10.6 %collective-permute-start.23 = (bf16[64,2048]{1,0:T(8,128)(2,1)S(1)}, bf16[64,2048]{1,0:T(8,128)(2,1)S(1)}, u32[]{:S(2)}, u32[]{:S(2)}) collective-permute-start(bf16[64,2048]{1,0:T(8,128)(2,1)S(1)} %get-tuple-element.78), channel_id=1, source_target_pairs={{4,0},{8,4},{12,8},{14,12},{10,14},{6,10},{2,6},{0,2},{5,1},{9,5},... | collective-permute-start | bytes 786440 | tf_op jit(solution)/shard_map/ppermute | solution.py:409
  64.5 12.7 %copy-start.5 = (bf16[64,2048]{1,0:T(8,128)(2,1)S(1)}, bf16[64,2048]{1,0:T(8,128)(2,1)}, u32[]{:S(2)}) copy-start(bf16[64,2048]{1,0:T(8,128)(2,1)} %copy-done.4) | copy-start | bytes 786436
  64.5 12.7 %copy-start.7 = (bf16[64,2048]{1,0:T(8,128)(2,1)S(1)}, bf16[64,2048]{1,0:T(8,128)(2,1)}, u32[]{:S(2)}) copy-start(bf16[64,2048]{1,0:T(8,128)(2,1)} %copy-done.6) | copy-start | bytes 786436
  64.5 10.8 %collective-permute-start.28 = (bf16[64,2048]{1,0:T(8,128)(2,1)S(1)}, bf16[64,2048]{1,0:T(8,128)(2,1)S(1)}, u32[]{:S(2)}, u32[]{:S(2)}) collective-permute-start(bf16[64,2048]{1,0:T(8,128)(2,1)S(1)} %get-tuple-element.82), channel_id=1, source_target_pairs={{0,4},{4,8},{8,12},{12,14},{14,10},{10,6},{6,2},{2,0},{1,5},{5,9},... | collective-permute-start | bytes 786440 | tf_op jit(solution)/shard_map/ppermute | solution.py:409
  72.7 9.8 %collective-permute-start.19 = (bf16[64,2048]{1,0:T(8,128)(2,1)S(1)}, bf16[64,2048]{1,0:T(8,128)(2,1)S(1)}, u32[]{:S(2)}, u32[]{:S(2)}) collective-permute-start(bf16[64,2048]{1,0:T(8,128)(2,1)S(1)} %get-tuple-element.66), channel_id=1, source_target_pairs={{0,4},{4,8},{8,12},{12,14},{14,10},{10,6},{6,2},{2,0},{1,5},{5,9},... | collective-permute-start | bytes 786440 | tf_op jit(solution)/shard_map/ppermute | solution.py:409
  74.3 8.2 %collective-permute-start.20 = (bf16[64,2048]{1,0:T(8,128)(2,1)S(1)}, bf16[64,2048]{1,0:T(8,128)(2,1)S(1)}, u32[]{:S(2)}, u32[]{:S(2)}) collective-permute-start(bf16[64,2048]{1,0:T(8,128)(2,1)S(1)} %get-tuple-element.67), channel_id=1, source_target_pairs={{4,0},{8,4},{12,8},{14,12},{10,14},{6,10},{2,6},{0,2},{5,1},{9,5},... | collective-permute-start | bytes 786440 | tf_op jit(solution)/shard_map/ppermute | solution.py:409
  74.8 12.9 %collective-permute-start.24 = (bf16[64,2048]{1,0:T(8,128)(2,1)S(1)}, bf16[64,2048]{1,0:T(8,128)(2,1)S(1)}, u32[]{:S(2)}, u32[]{:S(2)}) collective-permute-start(bf16[64,2048]{1,0:T(8,128)(2,1)S(1)} %add_convert_fusion.6), channel_id=1, source_target_pairs={{4,0},{8,4},{12,8},{14,12},{10,14},{6,10},{2,6},{0,2},{5,1},{9,5},... | collective-permute-start | bytes 786440 | tf_op jit(solution)/shard_map/ppermute | solution.py:409
  75.4 14.8 %copy-start.2 = (bf16[64,2176]{1,0:T(8,128)(2,1)S(1)}, bf16[64,2176]{1,0:T(8,128)(2,1)}, u32[]{:S(2)}) copy-start(bf16[64,2176]{1,0:T(8,128)(2,1)} %get-tuple-element.74.refs_3_.refs_1_) | copy-start | bytes 835588
  75.4 14.7 %copy-start.3 = (bf16[64,2048]{1,0:T(8,128)(2,1)S(1)}, bf16[64,2048]{1,0:T(8,128)(2,1)}, u32[]{:S(2)}) copy-start(bf16[64,2048]{1,0:T(8,128)(2,1)} %get-tuple-element.46.refs_2_) | copy-start | bytes 786436
  75.4 12.7 %collective-permute-start.29 = (bf16[64,2048]{1,0:T(8,128)(2,1)S(1)}, bf16[64,2048]{1,0:T(8,128)(2,1)S(1)}, u32[]{:S(2)}, u32[]{:S(2)}) collective-permute-start(bf16[64,2048]{1,0:T(8,128)(2,1)S(1)} %add_convert_fusion.2), channel_id=1, source_target_pairs={{0,4},{4,8},{8,12},{12,14},{14,10},{10,6},{6,2},{2,0},{1,5},{5,9},... | collective-permute-start | bytes 786440 | tf_op jit(solution)/shard_map/ppermute | solution.py:409
  82.6 10.6 %collective-permute-start.21 = (bf16[64,2048]{1,0:T(8,128)(2,1)S(1)}, bf16[64,2048]{1,0:T(8,128)(2,1)S(1)}, u32[]{:S(2)}, u32[]{:S(2)}) collective-permute-start(bf16[64,2048]{1,0:T(8,128)(2,1)S(1)} %add_convert_fusion.9), channel_id=1, source_target_pairs={{0,4},{4,8},{8,12},{12,14},{14,10},{10,6},{6,2},{2,0},{1,5},{5,9},... | collective-permute-start | bytes 786440 | tf_op jit(solution)/shard_map/ppermute | solution.py:409
  84.4 10.5 %collective-permute-start.26 = (bf16[64,2048]{1,0:T(8,128)(2,1)S(1)}, bf16[64,2048]{1,0:T(8,128)(2,1)S(1)}, u32[]{:S(2)}, u32[]{:S(2)}) collective-permute-start(bf16[64,2048]{1,0:T(8,128)(2,1)S(1)} %add_convert_fusion.8), channel_id=1, source_target_pairs={{4,0},{8,4},{12,8},{14,12},{10,14},{6,10},{2,6},{0,2},{5,1},{9,5},... | collective-permute-start | bytes 786440 | tf_op jit(solution)/shard_map/ppermute | solution.py:409
  87.7 11.5 %collective-permute-start.25 = (bf16[64,2048]{1,0:T(8,128)(2,1)S(1)}, bf16[64,2048]{1,0:T(8,128)(2,1)S(1)}, u32[]{:S(2)}, u32[]{:S(2)}) collective-permute-start(bf16[64,2048]{1,0:T(8,128)(2,1)S(1)} %add_convert_fusion.5), channel_id=1, source_target_pairs={{4,0},{8,4},{12,8},{14,12},{10,14},{6,10},{2,6},{0,2},{5,1},{9,5},... | collective-permute-start | bytes 786440 | tf_op jit(solution)/shard_map/ppermute | solution.py:409
  88.2 14.0 %collective-permute-start.30 = (bf16[64,2048]{1,0:T(8,128)(2,1)S(1)}, bf16[64,2048]{1,0:T(8,128)(2,1)S(1)}, u32[]{:S(2)}, u32[]{:S(2)}) collective-permute-start(bf16[64,2048]{1,0:T(8,128)(2,1)S(1)} %add_convert_fusion.1), channel_id=1, source_target_pairs={{0,4},{4,8},{8,12},{12,14},{14,10},{10,6},{6,2},{2,0},{1,5},{5,9},... | collective-permute-start | bytes 786440 | tf_op jit(solution)/shard_map/ppermute | solution.py:409
  93.3 8.8 %collective-permute-start.22 = (bf16[64,2048]{1,0:T(8,128)(2,1)S(1)}, bf16[64,2048]{1,0:T(8,128)(2,1)S(1)}, u32[]{:S(2)}, u32[]{:S(2)}) collective-permute-start(bf16[64,2048]{1,0:T(8,128)(2,1)S(1)} %add_convert_fusion.7), channel_id=1, source_target_pairs={{0,4},{4,8},{8,12},{12,14},{14,10},{10,6},{6,2},{2,0},{1,5},{5,9},... | collective-permute-start | bytes 786440 | tf_op jit(solution)/shard_map/ppermute | solution.py:409
  94.9 7.2 %collective-permute-start.27 = (bf16[64,2048]{1,0:T(8,128)(2,1)S(1)}, bf16[64,2048]{1,0:T(8,128)(2,1)S(1)}, u32[]{:S(2)}, u32[]{:S(2)}) collective-permute-start(bf16[64,2048]{1,0:T(8,128)(2,1)S(1)} %add_convert_fusion.3), channel_id=1, source_target_pairs={{4,0},{8,4},{12,8},{14,12},{10,14},{6,10},{2,6},{0,2},{5,1},{9,5},... | collective-permute-start | bytes 786440 | tf_op jit(solution)/shard_map/ppermute | solution.py:409

commit v4 on v3

--- a/solution.py
+++ b/solution.py
@@ -432,9 +432,12 @@
         held[-d] = [go(after(x, *w), 1) for x, w in zip(held[1 - d], waits)]
         held[d] = [go(after(x, *w), -1) for x, w in zip(held[d - 1], waits)]
 
+    last = reach - 1
     for d in range(1, reach):
+        if d == last:
+            for way in (1, -1):
+                held[way * (d - 1)][1] = after(held[way * (d - 1)][1], *weights[2:])
         pass_on(d, [], [])
-    last = reach - 1
     held[reach] = [go(held[-last][0], 1), go(held[last][1], -1)]
     come = [held[way * last][0] for way in (1, -1)]
     *loaded, packs = load_call(

time: 103 us -> 103 us (level)
  local copies, waits for them, and re-layouts: 3.69 us -> 12.7 us
  waiting for transfers between devices: 28.9 us -> 25.8 us
  starting transfers between devices: 37.5 us -> 34.5 us
  Pallas kernels: 31.2 us -> 28.3 us
    unnamed x30 -> x34, local copies, waits for them, and re-layouts: 3.69 us -> 12.7 us
    ppermute x28, waiting for transfers between devices: 27.9 us -> 24.8 us  [go(): return lax.ppermute(x, 'ep', ahead if way > 0 else back)]
    pallas_call x1, Pallas kernels: 3.82 us -> 0.82 us  [load_call(): pl.pallas_call(functools.partial(load_kernel, tuple(blocks)), out_shape=[...]
    ppermute x28, starting transfers between devices: 36.4 us -> 33.5 us  [go(): return lax.ppermute(x, 'ep', ahead if way > 0 else back)]
  transfers between devices with their start and end apart: 31 -> 31, of which waited for: 12 -> 12; matrix products, arithmetic and copies ran while one was open for 1% -> 1% of each run, Pallas kernels for 24% -> 21%
where the time goes in v4:
time: 103 us
  starting transfers between devices  34.5 us (33%)
  Pallas kernels  28.3 us (27%)
  waiting for transfers between devices  25.8 us (25%)
  local copies, waits for them, and re-layouts  12.7 us (12%)
  other arithmetic  1.56 us (2%)
    ppermute x28, starting transfers between devices, go(): return lax.ppermute(x, 'ep', ahead if way > 0 else back)  33.5 us
    ppermute x28, waiting for transfers between devices, go(): return lax.ppermute(x, 'ep', ahead if way > 0 else back)  24.8 us
    pallas_call x5, Pallas kernels, expert_call(): pl.pallas_call(functools.partial(expert_kernel, blocks, columns, bool(tab...  24.3 us
    unnamed x34, local copies, waits for them, and re-layouts  12.7 us
    pallas_call x1, Pallas kernels, gathered_body(): pl.pallas_call(functools.partial(pack_kernel, devices), out_shape=[jax.Sh...  2.56 us
  transfers between devices with their start and end apart: 31, of which 12 were waited for; matrix products, arithmetic and copies ran while one was open for 1% of the time, Pallas kernels for 21%

profile of v4, /device:TPU:0, one launch (start us, length us, event | category | flops | bytes accessed | tf_op | source)
XLA Modules:
  0.0 103.2 jit_solution(7635902000786850235)
XLA Ops:
  0.0 0.5 collective-permute-start
  0.5 1.0 %collective-permute-done.mate_ref = s32[8,128]{1,0:T(8,128)S(1)} collective-permute-done((s32[8,128]{1,0:T(8,128)}, s32[8,128]{1,0:T(8,128)S(1)}, u32[]{:S(2)}, u32[]{:S(2)}) %collective-permute-start) | collective-permute-done | bytes 4128 | tf_op jit(solution)/shard_map/ppermute | solution.py:406
  1.5 0.6 copy-done.14
  2.1 2.6 %shard_map.73 = (bf16[64,2176]{1,0:T(8,128)(2,1)}, bf16[64,2048]{1,0:T(8,128)(2,1)}) custom-call(s32[8,128]{1,0:T(8,128)} %bitcast.6, f32[8,128]{1,0:T(8,128)} %bitcast.7, s32[8,128]{1,0:T(8,128)} %copy-done.14, bf16[128,2048]{1,0:T(8,128)(2,1)} %tokens_ref.1), custom_call_target="tpu_custom_call" | custom-call | tf_op jit(solution)/shard_map/pallas_call | solution.py:417
  4.6 0.4 collective-permute-start.6
  5.0 0.2 collective-permute-start.7
  5.2 2.9 %collective-permute-start.1 = (bf16[64,2176]{1,0:T(8,128)(2,1)}, bf16[64,2176]{1,0:T(8,128)(2,1)S(1)}, u32[]{:S(2)}, u32[]{:S(2)}) collective-permute-start(bf16[64,2176]{1,0:T(8,128)(2,1)} %get-tuple-element.78.refs_3_.refs_1_), channel_id=1, source_target_pairs={{0,4},{4,8},{8,12},{12,14},{14,10},{10,6},{6,2},{2,0},{1,5},{5,9},... | collective-permute-start | bytes 835592 | tf_op jit(solution)/shard_map/ppermute | solution.py:409
  8.1 1.9 %collective-permute-start.12 = (bf16[64,2048]{1,0:T(8,128)(2,1)}, bf16[64,2048]{1,0:T(8,128)(2,1)S(1)}, u32[]{:S(2)}, u32[]{:S(2)}) collective-permute-start(bf16[64,2048]{1,0:T(8,128)(2,1)} %get-tuple-element.48.refs_2_), channel_id=1, source_target_pairs={{4,0},{8,4},{12,8},{14,12},{10,14},{6,10},{2,6},{0,2},{5,1},{9,5},... | collective-permute-start | bytes 786440 | tf_op jit(solution)/shard_map/ppermute | solution.py:409
  10.1 5.2 %collective-permute-done.1.refs_2_.refs_1_ = bf16[64,2176]{1,0:T(8,128)(2,1)S(1)} collective-permute-done((bf16[64,2176]{1,0:T(8,128)(2,1)}, bf16[64,2176]{1,0:T(8,128)(2,1)S(1)}, u32[]{:S(2)}, u32[]{:S(2)}) %collective-permute-start.1) | collective-permute-done | bytes 278560 | tf_op jit(solution)/shard_map/ppermute | solution.py:409
  15.2 1.8 %collective-permute-start.4 = (bf16[64,2048]{1,0:T(8,128)(2,1)}, bf16[64,2048]{1,0:T(8,128)(2,1)S(1)}, u32[]{:S(2)}, u32[]{:S(2)}) collective-permute-start(bf16[64,2048]{1,0:T(8,128)(2,1)} %get-tuple-element.48.refs_2_), channel_id=1, source_target_pairs={{0,4},{4,8},{8,12},{12,14},{14,10},{10,6},{6,2},{2,0},{1,5},{5,9},... | collective-permute-start | bytes 786440 | tf_op jit(solution)/shard_map/ppermute | solution.py:409
  17.1 0.8 collective-permute-done.9.refs_4_.refs_3_
  17.9 1.6 %collective-permute-start.2 = (bf16[64,2176]{1,0:T(8,128)(2,1)S(1)}, bf16[64,2176]{1,0:T(8,128)(2,1)S(1)}, u32[]{:S(2)}, u32[]{:S(2)}) collective-permute-start(bf16[64,2176]{1,0:T(8,128)(2,1)S(1)} %collective-permute-done.1.refs_2_.refs_1_), channel_id=1, source_target_pairs={{0,4},{4,8},{8,12},{12,14},{14,10},{10,6},{6,2},{2,0},{1,5},{5,9},... | collective-permute-start | bytes 835592 | tf_op jit(solution)/shard_map/ppermute | solution.py:409
  19.5 2.9 %collective-permute-done.12.refs_4_ = bf16[64,2048]{1,0:T(8,128)(2,1)S(1)} collective-permute-done((bf16[64,2048]{1,0:T(8,128)(2,1)}, bf16[64,2048]{1,0:T(8,128)(2,1)S(1)}, u32[]{:S(2)}, u32[]{:S(2)}) %collective-permute-start.12) | collective-permute-done | bytes 262176 | tf_op jit(solution)/shard_map/ppermute | solution.py:409
  22.4 0.3 collective-permute-start.10
  22.7 1.9 %collective-permute-done.4.refs_2_ = bf16[64,2048]{1,0:T(8,128)(2,1)S(1)} collective-permute-done((bf16[64,2048]{1,0:T(8,128)(2,1)}, bf16[64,2048]{1,0:T(8,128)(2,1)S(1)}, u32[]{:S(2)}, u32[]{:S(2)}) %collective-permute-start.4) | collective-permute-done | bytes 262176 | tf_op jit(solution)/shard_map/ppermute | solution.py:409
  24.7 1.8 %collective-permute-start.13 = (bf16[64,2048]{1,0:T(8,128)(2,1)S(1)}, bf16[64,2048]{1,0:T(8,128)(2,1)}, u32[]{:S(2)}, u32[]{:S(2)}) collective-permute-start(bf16[64,2048]{1,0:T(8,128)(2,1)S(1)} %collective-permute-done.12.refs_4_), channel_id=1, source_target_pairs={{4,0},{8,4},{12,8},{14,12},{10,14},{6,10},{2,6},{0,2},{5,1},{9,5},... | collective-permute-start | bytes 786440 | tf_op jit(solution)/shard_map/ppermute | solution.py:409
  26.4 0.7 copy-done.8
  27.2 2.1 %collective-permute-done.2.refs_1_ = bf16[64,2176]{1,0:T(8,128)(2,1)S(1)} collective-permute-done((bf16[64,2176]{1,0:T(8,128)(2,1)S(1)}, bf16[64,2176]{1,0:T(8,128)(2,1)S(1)}, u32[]{:S(2)}, u32[]{:S(2)}) %collective-permute-start.2) | collective-permute-done | bytes 278560 | tf_op jit(solution)/shard_map/ppermute | solution.py:409
  29.3 1.5 %collective-permute-start.5 = (bf16[64,2048]{1,0:T(8,128)(2,1)S(1)}, bf16[64,2048]{1,0:T(8,128)(2,1)}, u32[]{:S(2)}, u32[]{:S(2)}) collective-permute-start(bf16[64,2048]{1,0:T(8,128)(2,1)S(1)} %collective-permute-done.4.refs_2_), channel_id=1, source_target_pairs={{0,4},{4,8},{8,12},{12,14},{14,10},{10,6},{6,2},{2,0},{1,5},{5,9},... | collective-permute-start | bytes 786440 | tf_op jit(solution)/shard_map/ppermute | solution.py:409
  30.8 0.7 copy-done.10
  31.5 0.5 collective-permute-done.10.refs_5_.refs_3_
  32.0 1.6 %collective-permute-start.3 = (bf16[64,2176]{1,0:T(8,128)(2,1)S(1)}, bf16[64,2176]{1,0:T(8,128)(2,1)S(1)}, u32[]{:S(2)}, u32[]{:S(2)}) collective-permute-start(bf16[64,2176]{1,0:T(8,128)(2,1)S(1)} %collective-permute-done.2.refs_1_), channel_id=1, source_target_pairs={{0,4},{4,8},{8,12},{12,14},{14,10},{10,6},{6,2},{2,0},{1,5},{5,9},... | collective-permute-start | bytes 835592 | tf_op jit(solution)/shard_map/ppermute | solution.py:409
  33.6 2.1 %collective-permute-done.13.refs_4_ = bf16[64,2048]{1,0:T(8,128)(2,1)} collective-permute-done((bf16[64,2048]{1,0:T(8,128)(2,1)S(1)}, bf16[64,2048]{1,0:T(8,128)(2,1)}, u32[]{:S(2)}, u32[]{:S(2)}) %collective-permute-start.13) | collective-permute-done | bytes 262176 | tf_op jit(solution)/shard_map/ppermute | solution.py:409
  35.7 0.6 collective-permute-start.11
  36.4 1.7 %copy-done.3 = bf16[1,768,2048]{2,1,0:T(8,128)(2,1)} copy-done((bf16[1,768,2048]{2,1,0:T(8,128)(2,1)}, bf16[1,768,2048]{2,1,0:T(8,128)(2,1)S(1)}, u32[]{:S(2)}) %copy-start.3) | copy-done | bytes 3145752
  38.1 2.7 %copy-done.1 = bf16[1,2048,1536]{2,1,0:T(8,128)(2,1)} copy-done((bf16[1,2048,1536]{2,1,0:T(8,128)(2,1)}, bf16[1,2048,1536]{2,1,0:T(8,128)(2,1)S(1)}, u32[]{:S(2)}) %copy-start.1) | copy-done | bytes 6291480
  40.7 1.3 %collective-permute-start.14 = (bf16[64,2048]{1,0:T(8,128)(2,1)}, bf16[64,2048]{1,0:T(8,128)(2,1)}, u32[]{:S(2)}, u32[]{:S(2)}) collective-permute-start(bf16[64,2048]{1,0:T(8,128)(2,1)} %collective-permute-done.13.refs_4_), channel_id=1, source_target_pairs={{4,0},{8,4},{12,8},{14,12},{10,14},{6,10},{2,6},{0,2},{5,1},{9,5},... | collective-permute-start | bytes 786440 | tf_op jit(solution)/shard_map/ppermute | solution.py:409
  42.0 0.7 collective-permute-start.8
  42.8 1.4 %collective-permute-start.15 = (bf16[64,2176]{1,0:T(8,128)(2,1)S(1)}, bf16[64,2176]{1,0:T(8,128)(2,1)S(1)}, u32[]{:S(2)}, u32[]{:S(2)}) collective-permute-start(bf16[64,2176]{1,0:T(8,128)(2,1)S(1)} %collective-permute-done.3.refs_0_), channel_id=1, source_target_pairs={{0,4},{4,8},{8,12},{12,14},{14,10},{10,6},{6,2},{2,0},{1,5},{5,9},... | collective-permute-start | bytes 835592 | tf_op jit(solution)/shard_map/ppermute | solution.py:409
  44.2 3.4 %copy-done.2 = bf16[1,2048,1536]{2,1,0:T(8,128)(2,1)S(1)} copy-done((bf16[1,2048,1536]{2,1,0:T(8,128)(2,1)S(1)}, bf16[1,2048,1536]{2,1,0:T(8,128)(2,1)}, u32[]{:S(2)}) %copy-start.2) | copy-done | bytes 6291480
  47.6 1.9 %copy-done.4 = bf16[1,768,2048]{2,1,0:T(8,128)(2,1)S(1)} copy-done((bf16[1,768,2048]{2,1,0:T(8,128)(2,1)S(1)}, bf16[1,768,2048]{2,1,0:T(8,128)(2,1)}, u32[]{:S(2)}) %copy-start.4) | copy-done | bytes 3145752
  49.5 1.0 copy-done.5
  50.4 0.8 shard_map.74
  51.3 0.5 collective-permute-start.16
  51.8 6.2 %shard_map.75 = (bf16[128,2048]{1,0:T(8,128)(2,1)S(1)}, bf16[128,2048]{1,0:T(8,128)(2,1)S(1)}, bf16[128,2048]{1,0:T(8,128)(2,1)S(1)}, bf16[128,2048]{1,0:T(8,128)(2,1)S(1)}) custom-call(bf16[64,2176]{1,0:T(8,128)(2,1)S(1)} %collective-permute-done.3.refs_0_, bf16[64,2048]{1,0:T(8,128)(2,1)} %collective-permute-done.8.refs_1_, ...), custom_call_target="tpu_custom_call" | custom-call | flops 4831838208 | bytes 18874368 | tf_op jit(solution)/shard_map/pallas_call | solution.py:336
  58.1 3.9 %shard_map.76 = (f32[64,128]{1,0:T(8,128)S(1)}, bf16[64,2048]{1,0:T(8,128)(2,1)S(1)}, bf16[64,2048]{1,0:T(8,128)(2,1)S(1)}) custom-call(s32[1]{0:T(128)} %bitcast.refs_0_, s32[16]{0:T(128)S(1)} %copy-done.12, s32[16]{0:T(128)S(1)} %copy-done.13, bf16[8,64,128]{2,1,0:T(8,128)(2,1)S(1)} %get-tuple-element.59.refs_3_, ...), custom_call_target="tpu_custom_call" | custom-call | flops 2415919104 | bytes 18874368 | tf_op jit(solution)/shard_map/pallas_call | solution.py:336
  62.0 1.6 %collective-permute-start.18 = (bf16[64,2048]{1,0:T(8,128)(2,1)S(1)}, bf16[64,2048]{1,0:T(8,128)(2,1)S(1)}, u32[]{:S(2)}, u32[]{:S(2)}) collective-permute-start(bf16[64,2048]{1,0:T(8,128)(2,1)S(1)} %get-tuple-element.62), channel_id=1, source_target_pairs={{4,0},{8,4},{12,8},{14,12},{10,14},{6,10},{2,6},{0,2},{5,1},{9,5},... | collective-permute-start | bytes 786440 | tf_op jit(solution)/shard_map/ppermute | solution.py:409
  63.6 0.5 collective-permute-start.17
  64.1 0.3 shard_map.81
  64.3 1.6 %collective-permute-start.23 = (bf16[64,2048]{1,0:T(8,128)(2,1)S(1)}, bf16[64,2048]{1,0:T(8,128)(2,1)S(1)}, u32[]{:S(2)}, u32[]{:S(2)}) collective-permute-start(bf16[64,2048]{1,0:T(8,128)(2,1)S(1)} %get-tuple-element.82), channel_id=1, source_target_pairs={{4,0},{8,4},{12,8},{14,12},{10,14},{6,10},{2,6},{0,2},{5,1},{9,5},... | collective-permute-start | bytes 786440 | tf_op jit(solution)/shard_map/ppermute | solution.py:409
  65.9 0.5 collective-permute-start.28
  66.4 6.2 %shard_map.77 = (bf16[64,2048]{1,0:T(8,128)(2,1)S(1)}, bf16[64,2048]{1,0:T(8,128)(2,1)S(1)}, bf16[64,2048]{1,0:T(8,128)(2,1)S(1)}, bf16[64,2048]{1,0:T(8,128)(2,1)S(1)}) custom-call(f32[64,128]{1,0:T(8,128)S(1)} %get-tuple-element.60.refs_0_.gates_ref, bf16[64,2176]{1,0:T(8,128)(2,1)S(1)} %collective-permute-done.2.refs_1_, ...), custom_call_target="tpu_custom_call" | custom-call | flops 4831838208 | bytes 18874368 | tf_op jit(solution)/shard_map/pallas_call | solution.py:336
  72.6 0.3 shard_map.78
  73.0 1.6 %collective-permute-start.19 = (bf16[64,2048]{1,0:T(8,128)(2,1)S(1)}, bf16[64,2048]{1,0:T(8,128)(2,1)S(1)}, u32[]{:S(2)}, u32[]{:S(2)}) collective-permute-start(bf16[64,2048]{1,0:T(8,128)(2,1)S(1)} %get-tuple-element.70), channel_id=1, source_target_pairs={{0,4},{4,8},{8,12},{12,14},{14,10},{10,6},{6,2},{2,0},{1,5},{5,9},... | collective-permute-start | bytes 786440 | tf_op jit(solution)/shard_map/ppermute | solution.py:409
  74.6 0.5 collective-permute-start.20
  75.1 1.6 %collective-permute-start.24 = (bf16[64,2048]{1,0:T(8,128)(2,1)S(1)}, bf16[64,2048]{1,0:T(8,128)(2,1)S(1)}, u32[]{:S(2)}, u32[]{:S(2)}) collective-permute-start(bf16[64,2048]{1,0:T(8,128)(2,1)S(1)} %add_convert_fusion.6), channel_id=1, source_target_pairs={{4,0},{8,4},{12,8},{14,12},{10,14},{6,10},{2,6},{0,2},{5,1},{9,5},... | collective-permute-start | bytes 786440 | tf_op jit(solution)/shard_map/ppermute | solution.py:409
  76.7 0.1 add_convert_fusion.2
  76.8 0.5 collective-permute-start.29
  77.3 5.2 %shard_map.79 = (bf16[64,2048]{1,0:T(8,128)(2,1)S(1)}, bf16[64,2048]{1,0:T(8,128)(2,1)S(1)}, bf16[64,2048]{1,0:T(8,128)(2,1)S(1)}, bf16[64,2048]{1,0:T(8,128)(2,1)S(1)}) custom-call(f32[64,128]{1,0:T(8,128)S(1)} %get-tuple-element.60.refs_0_.gates_ref, bf16[64,2176]{1,0:T(8,128)(2,1)S(1)} %collective-permute-done.1.refs_2_.refs_1_, ...), custom_call_target="tpu_custom_call" | custom-call | flops 4831838208 | bytes 18874368 | tf_op jit(solution)/shard_map/pallas_call | solution.py:336
  82.6 0.1 add_convert_fusion.9
  82.7 1.6 %collective-permute-start.21 = (bf16[64,2048]{1,0:T(8,128)(2,1)S(1)}, bf16[64,2048]{1,0:T(8,128)(2,1)S(1)}, u32[]{:S(2)}, u32[]{:S(2)}) collective-permute-start(bf16[64,2048]{1,0:T(8,128)(2,1)S(1)} %add_convert_fusion.9), channel_id=1, source_target_pairs={{0,4},{4,8},{8,12},{12,14},{14,10},{10,6},{6,2},{2,0},{1,5},{5,9},... | collective-permute-start | bytes 786440 | tf_op jit(solution)/shard_map/ppermute | solution.py:409
  84.4 0.5 collective-permute-start.26
  84.9 1.9 %collective-permute-done.24 = bf16[64,2048]{1,0:T(8,128)(2,1)S(1)} collective-permute-done((bf16[64,2048]{1,0:T(8,128)(2,1)S(1)}, bf16[64,2048]{1,0:T(8,128)(2,1)S(1)}, u32[]{:S(2)}, u32[]{:S(2)}) %collective-permute-start.24) | collective-permute-done | bytes 262176 | tf_op jit(solution)/shard_map/ppermute | solution.py:409
  86.8 2.4 %collective-permute-start.25 = (bf16[64,2048]{1,0:T(8,128)(2,1)S(1)}, bf16[64,2048]{1,0:T(8,128)(2,1)S(1)}, u32[]{:S(2)}, u32[]{:S(2)}) collective-permute-start(bf16[64,2048]{1,0:T(8,128)(2,1)S(1)} %add_convert_fusion.5), channel_id=1, source_target_pairs={{4,0},{8,4},{12,8},{14,12},{10,14},{6,10},{2,6},{0,2},{5,1},{9,5},... | collective-permute-start | bytes 786440 | tf_op jit(solution)/shard_map/ppermute | solution.py:409
  89.3 0.5 collective-permute-start.30
  89.8 2.9 %shard_map.80 = (bf16[64,2048]{1,0:T(8,128)(2,1)S(1)}, bf16[64,2048]{1,0:T(8,128)(2,1)S(1)}) custom-call(f32[64,128]{1,0:T(8,128)S(1)} %get-tuple-element.60.refs_0_.gates_ref, bf16[64,2176]{1,0:T(8,128)(2,1)S(1)} %copy-done.6, bf16[64,2048]{1,0:T(8,128)(2,1)S(1)} %copy-done.7, bf16[1,2048,1536]{2,1,0:T(8,128)(2,1)S(1)} %bitcast.4, ...), custom_call_target="tpu_custom_call" | custom-call | flops 2415919104 | bytes 18874368 | tf_op jit(solution)/shard_map/pallas_call | solution.py:336
  92.6 0.9 collective-permute-done.21
  93.6 1.6 %collective-permute-start.22 = (bf16[64,2048]{1,0:T(8,128)(2,1)S(1)}, bf16[64,2048]{1,0:T(8,128)(2,1)S(1)}, u32[]{:S(2)}, u32[]{:S(2)}) collective-permute-start(bf16[64,2048]{1,0:T(8,128)(2,1)S(1)} %add_convert_fusion.7), channel_id=1, source_target_pairs={{0,4},{4,8},{8,12},{12,14},{14,10},{10,6},{6,2},{2,0},{1,5},{5,9},... | collective-permute-start | bytes 786440 | tf_op jit(solution)/shard_map/ppermute | solution.py:409
  95.2 0.5 collective-permute-start.27
  95.8 2.3 %collective-permute-done.25 = bf16[64,2048]{1,0:T(8,128)(2,1)S(1)} collective-permute-done((bf16[64,2048]{1,0:T(8,128)(2,1)S(1)}, bf16[64,2048]{1,0:T(8,128)(2,1)S(1)}, u32[]{:S(2)}, u32[]{:S(2)}) %collective-permute-start.25) | collective-permute-done | bytes 262176 | tf_op jit(solution)/shard_map/ppermute | solution.py:409
  98.1 4.0 %collective-permute-done.22 = bf16[64,2048]{1,0:T(8,128)(2,1)S(1)} collective-permute-done((bf16[64,2048]{1,0:T(8,128)(2,1)S(1)}, bf16[64,2048]{1,0:T(8,128)(2,1)S(1)}, u32[]{:S(2)}, u32[]{:S(2)}) %collective-permute-start.22) | collective-permute-done | bytes 262176 | tf_op jit(solution)/shard_map/ppermute | solution.py:409
  102.1 0.1 add_convert_fusion.4
  102.2 0.1 add_convert_fusion
  102.3 0.8 pad_maximum_fusion
  (53 shorter events, 0.5 us)
Async XLA Ops:
  0.0 51.8 %slice-start = ((s8[6291456]{0:T(1024)(128)(4,1)}), s8[2097152]{0:T(1024)(128)(4,1)S(1)}, s32[]{:S(2)}) async-start(s8[6291456]{0:T(1024)(128)(4,1)} %bitcast.3), calls=%async_computation | async-start | bytes 4194304
  0.0 1.5 %collective-permute-start = (s32[8,128]{1,0:T(8,128)}, s32[8,128]{1,0:T(8,128)S(1)}, u32[]{:S(2)}, u32[]{:S(2)}) collective-permute-start(s32[8,128]{1,0:T(8,128)} %bitcast.5), channel_id=1, source_target_pairs={{0,1},{1,0},{2,3},{3,2},{4,5},{5,4},{6,7},{7,6},{8,9},{9,8},{10,11... | collective-permute-start | bytes 12296 | tf_op jit(solution)/shard_map/ppermute | solution.py:406
  1.5 0.6 copy-start.14
  4.6 33.4 %collective-permute-start.6 = (bf16[1,2048,1536]{2,1,0:T(8,128)(2,1)}, bf16[1,2048,1536]{2,1,0:T(8,128)(2,1)S(1)}, u32[]{:S(2)}, u32[]{:S(2)}) collective-permute-start(bf16[1,2048,1536]{2,1,0:T(8,128)(2,1)} %refs_3_.1), channel_id=1, source_target_pairs={{0,1},{1,0},{2,3},{3,2},{4,5},{5,4},{6,7},{7,6},{8,9},{9,8},{10,11... | collective-permute-start | bytes 18874376 | tf_op jit(solution)/shard_map/ppermute | solution.py:406
  5.0 31.3 %collective-permute-start.7 = (bf16[1,768,2048]{2,1,0:T(8,128)(2,1)}, bf16[1,768,2048]{2,1,0:T(8,128)(2,1)S(1)}, u32[]{:S(2)}, u32[]{:S(2)}) collective-permute-start(bf16[1,768,2048]{2,1,0:T(8,128)(2,1)} %refs_4_.3), channel_id=1, source_target_pairs={{0,1},{1,0},{2,3},{3,2},{4,5},{5,4},{6,7},{7,6},{8,9},{9,8},{10,11... | collective-permute-start | bytes 9437192 | tf_op jit(solution)/shard_map/ppermute | solution.py:406
  5.2 10.0 %collective-permute-start.1 = (bf16[64,2176]{1,0:T(8,128)(2,1)}, bf16[64,2176]{1,0:T(8,128)(2,1)S(1)}, u32[]{:S(2)}, u32[]{:S(2)}) collective-permute-start(bf16[64,2176]{1,0:T(8,128)(2,1)} %get-tuple-element.78.refs_3_.refs_1_), channel_id=1, source_target_pairs={{0,4},{4,8},{8,12},{12,14},{14,10},{10,6},{6,2},{2,0},{1,5},{5,9},... | collective-permute-start | bytes 835592 | tf_op jit(solution)/shard_map/ppermute | solution.py:409
  8.1 9.8 %collective-permute-start.9 = (bf16[64,2176]{1,0:T(8,128)(2,1)}, bf16[64,2176]{1,0:T(8,128)(2,1)S(1)}, u32[]{:S(2)}, u32[]{:S(2)}) collective-permute-start(bf16[64,2176]{1,0:T(8,128)(2,1)} %get-tuple-element.78.refs_3_.refs_1_), channel_id=1, source_target_pairs={{4,0},{8,4},{12,8},{14,12},{10,14},{6,10},{2,6},{0,2},{5,1},{9,5},... | collective-permute-start | bytes 835592 | tf_op jit(solution)/shard_map/ppermute | solution.py:409
  8.1 14.3 %collective-permute-start.12 = (bf16[64,2048]{1,0:T(8,128)(2,1)}, bf16[64,2048]{1,0:T(8,128)(2,1)S(1)}, u32[]{:S(2)}, u32[]{:S(2)}) collective-permute-start(bf16[64,2048]{1,0:T(8,128)(2,1)} %get-tuple-element.48.refs_2_), channel_id=1, source_target_pairs={{4,0},{8,4},{12,8},{14,12},{10,14},{6,10},{2,6},{0,2},{5,1},{9,5},... | collective-permute-start | bytes 786440 | tf_op jit(solution)/shard_map/ppermute | solution.py:409
  15.2 9.4 %collective-permute-start.4 = (bf16[64,2048]{1,0:T(8,128)(2,1)}, bf16[64,2048]{1,0:T(8,128)(2,1)S(1)}, u32[]{:S(2)}, u32[]{:S(2)}) collective-permute-start(bf16[64,2048]{1,0:T(8,128)(2,1)} %get-tuple-element.48.refs_2_), channel_id=1, source_target_pairs={{0,4},{4,8},{8,12},{12,14},{14,10},{10,6},{6,2},{2,0},{1,5},{5,9},... | collective-permute-start | bytes 786440 | tf_op jit(solution)/shard_map/ppermute | solution.py:409
  17.9 11.4 %collective-permute-start.2 = (bf16[64,2176]{1,0:T(8,128)(2,1)S(1)}, bf16[64,2176]{1,0:T(8,128)(2,1)S(1)}, u32[]{:S(2)}, u32[]{:S(2)}) collective-permute-start(bf16[64,2176]{1,0:T(8,128)(2,1)S(1)} %collective-permute-done.1.refs_2_.refs_1_), channel_id=1, source_target_pairs={{0,4},{4,8},{8,12},{12,14},{14,10},{10,6},{6,2},{2,0},{1,5},{5,9},... | collective-permute-start | bytes 835592 | tf_op jit(solution)/shard_map/ppermute | solution.py:409
  22.4 9.6 %collective-permute-start.10 = (bf16[64,2176]{1,0:T(8,128)(2,1)S(1)}, bf16[64,2176]{1,0:T(8,128)(2,1)S(1)}, u32[]{:S(2)}, u32[]{:S(2)}) collective-permute-start(bf16[64,2176]{1,0:T(8,128)(2,1)S(1)} %collective-permute-done.9.refs_4_.refs_3_), channel_id=1, source_target_pairs={{4,0},{8,4},{12,8},{14,12},{10,14},{6,10},{2,6},{0,2},{5,1},{9,5},... | collective-permute-start | bytes 835592 | tf_op jit(solution)/shard_map/ppermute | solution.py:409
  24.7 11.0 %collective-permute-start.13 = (bf16[64,2048]{1,0:T(8,128)(2,1)S(1)}, bf16[64,2048]{1,0:T(8,128)(2,1)}, u32[]{:S(2)}, u32[]{:S(2)}) collective-permute-start(bf16[64,2048]{1,0:T(8,128)(2,1)S(1)} %collective-permute-done.12.refs_4_), channel_id=1, source_target_pairs={{4,0},{8,4},{12,8},{14,12},{10,14},{6,10},{2,6},{0,2},{5,1},{9,5},... | collective-permute-start | bytes 786440 | tf_op jit(solution)/shard_map/ppermute | solution.py:409
  26.4 0.7 copy-start.8
  29.3 12.8 %collective-permute-start.5 = (bf16[64,2048]{1,0:T(8,128)(2,1)S(1)}, bf16[64,2048]{1,0:T(8,128)(2,1)}, u32[]{:S(2)}, u32[]{:S(2)}) collective-permute-start(bf16[64,2048]{1,0:T(8,128)(2,1)S(1)} %collective-permute-done.4.refs_2_), channel_id=1, source_target_pairs={{0,4},{4,8},{8,12},{12,14},{14,10},{10,6},{6,2},{2,0},{1,5},{5,9},... | collective-permute-start | bytes 786440 | tf_op jit(solution)/shard_map/ppermute | solution.py:409
  30.8 0.7 copy-start.10
  32.0 10.8 %collective-permute-start.3 = (bf16[64,2176]{1,0:T(8,128)(2,1)S(1)}, bf16[64,2176]{1,0:T(8,128)(2,1)S(1)}, u32[]{:S(2)}, u32[]{:S(2)}) collective-permute-start(bf16[64,2176]{1,0:T(8,128)(2,1)S(1)} %collective-permute-done.2.refs_1_), channel_id=1, source_target_pairs={{0,4},{4,8},{8,12},{12,14},{14,10},{10,6},{6,2},{2,0},{1,5},{5,9},... | collective-permute-start | bytes 835592 | tf_op jit(solution)/shard_map/ppermute | solution.py:409
  35.7 8.5 %collective-permute-start.11 = (bf16[64,2176]{1,0:T(8,128)(2,1)S(1)}, bf16[64,2176]{1,0:T(8,128)(2,1)}, u32[]{:S(2)}, u32[]{:S(2)}) collective-permute-start(bf16[64,2176]{1,0:T(8,128)(2,1)S(1)} %collective-permute-done.10.refs_5_.refs_3_), channel_id=1, source_target_pairs={{4,0},{8,4},{12,8},{14,12},{10,14},{6,10},{2,6},{0,2},{5,1},{9,5},... | collective-permute-start | bytes 835592 | tf_op jit(solution)/shard_map/ppermute | solution.py:409
  36.4 1.7 %copy-start.3 = (bf16[1,768,2048]{2,1,0:T(8,128)(2,1)}, bf16[1,768,2048]{2,1,0:T(8,128)(2,1)S(1)}, u32[]{:S(2)}) copy-start(bf16[1,768,2048]{2,1,0:T(8,128)(2,1)S(1)} %collective-permute-done.7.down_ref) | copy-start | bytes 9437188
  38.1 2.7 %copy-start.1 = (bf16[1,2048,1536]{2,1,0:T(8,128)(2,1)}, bf16[1,2048,1536]{2,1,0:T(8,128)(2,1)S(1)}, u32[]{:S(2)}) copy-start(bf16[1,2048,1536]{2,1,0:T(8,128)(2,1)S(1)} %collective-permute-done.6.in_ref) | copy-start | bytes 18874372
  40.7 10.5 %collective-permute-start.14 = (bf16[64,2048]{1,0:T(8,128)(2,1)}, bf16[64,2048]{1,0:T(8,128)(2,1)}, u32[]{:S(2)}, u32[]{:S(2)}) collective-permute-start(bf16[64,2048]{1,0:T(8,128)(2,1)} %collective-permute-done.13.refs_4_), channel_id=1, source_target_pairs={{4,0},{8,4},{12,8},{14,12},{10,14},{6,10},{2,6},{0,2},{5,1},{9,5},... | collective-permute-start | bytes 786440 | tf_op jit(solution)/shard_map/ppermute | solution.py:409
  42.0 9.7 %collective-permute-start.8 = (bf16[64,2048]{1,0:T(8,128)(2,1)}, bf16[64,2048]{1,0:T(8,128)(2,1)}, u32[]{:S(2)}, u32[]{:S(2)}) collective-permute-start(bf16[64,2048]{1,0:T(8,128)(2,1)} %collective-permute-done.5.refs_2_), channel_id=1, source_target_pairs={{0,4},{4,8},{8,12},{12,14},{14,10},{10,6},{6,2},{2,0},{1,5},{5,9},... | collective-permute-start | bytes 786440 | tf_op jit(solution)/shard_map/ppermute | solution.py:409
  42.8 9.0 %slice-start.1 = ((s8[6291456]{0:T(1024)(128)(4,1)}), s8[4194304]{0:T(1024)(128)(4,1)S(1)}, s32[]{:S(2)}) async-start(s8[6291456]{0:T(1024)(128)(4,1)} %bitcast.3), calls=%async_computation.1 | async-start | bytes 8388608
  42.8 9.0 %copy-start = (bf16[1,768,2048]{2,1,0:T(8,128)(2,1)S(1)}, bf16[1,768,2048]{2,1,0:T(8,128)(2,1)}, u32[]{:S(2)}) copy-start(bf16[1,768,2048]{2,1,0:T(8,128)(2,1)} %refs_4_.3) | copy-start | bytes 9437188
  42.8 15.3 %collective-permute-start.15 = (bf16[64,2176]{1,0:T(8,128)(2,1)S(1)}, bf16[64,2176]{1,0:T(8,128)(2,1)S(1)}, u32[]{:S(2)}, u32[]{:S(2)}) collective-permute-start(bf16[64,2176]{1,0:T(8,128)(2,1)S(1)} %collective-permute-done.3.refs_0_), channel_id=1, source_target_pairs={{0,4},{4,8},{8,12},{12,14},{14,10},{10,6},{6,2},{2,0},{1,5},{5,9},... | collective-permute-start | bytes 835592 | tf_op jit(solution)/shard_map/ppermute | solution.py:409
  44.2 3.4 %copy-start.2 = (bf16[1,2048,1536]{2,1,0:T(8,128)(2,1)S(1)}, bf16[1,2048,1536]{2,1,0:T(8,128)(2,1)}, u32[]{:S(2)}) copy-start(bf16[1,2048,1536]{2,1,0:T(8,128)(2,1)} %copy-done.1) | copy-start | bytes 18874372
  47.6 1.9 %copy-start.4 = (bf16[1,768,2048]{2,1,0:T(8,128)(2,1)S(1)}, bf16[1,768,2048]{2,1,0:T(8,128)(2,1)}, u32[]{:S(2)}) copy-start(bf16[1,768,2048]{2,1,0:T(8,128)(2,1)} %copy-done.3) | copy-start | bytes 9437188
  49.5 1.0 copy-start.5
  51.3 6.8 %collective-permute-start.16 = (bf16[64,2048]{1,0:T(8,128)(2,1)}, bf16[64,2048]{1,0:T(8,128)(2,1)S(1)}, u32[]{:S(2)}, u32[]{:S(2)}) collective-permute-start(bf16[64,2048]{1,0:T(8,128)(2,1)} %collective-permute-done.14.refs_3_), channel_id=1, source_target_pairs={{4,0},{8,4},{12,8},{14,12},{10,14},{6,10},{2,6},{0,2},{5,1},{9,5},... | collective-permute-start | bytes 786440 | tf_op jit(solution)/shard_map/ppermute | solution.py:409
  51.8 6.3 %copy-start.12 = (s32[16]{0:T(128)S(1)}, s32[16]{0:T(128)}, u32[]{:S(2)}) copy-start(s32[16]{0:T(128)} %refs_1_.1) | copy-start | bytes 196
  51.8 6.3 %copy-start.13 = (s32[16]{0:T(128)S(1)}, s32[16]{0:T(128)}, u32[]{:S(2)}) copy-start(s32[16]{0:T(128)} %refs_2_.1) | copy-start | bytes 196
  62.0 10.6 %collective-permute-start.18 = (bf16[64,2048]{1,0:T(8,128)(2,1)S(1)}, bf16[64,2048]{1,0:T(8,128)(2,1)S(1)}, u32[]{:S(2)}, u32[]{:S(2)}) collective-permute-start(bf16[64,2048]{1,0:T(8,128)(2,1)S(1)} %get-tuple-element.62), channel_id=1, source_target_pairs={{4,0},{8,4},{12,8},{14,12},{10,14},{6,10},{2,6},{0,2},{5,1},{9,5},... | collective-permute-start | bytes 786440 | tf_op jit(solution)/shard_map/ppermute | solution.py:409
  63.6 9.0 %collective-permute-start.17 = (bf16[64,2048]{1,0:T(8,128)(2,1)S(1)}, bf16[64,2048]{1,0:T(8,128)(2,1)S(1)}, u32[]{:S(2)}, u32[]{:S(2)}) collective-permute-start(bf16[64,2048]{1,0:T(8,128)(2,1)S(1)} %get-tuple-element.61), channel_id=1, source_target_pairs={{0,4},{4,8},{8,12},{12,14},{14,10},{10,6},{6,2},{2,0},{1,5},{5,9},... | collective-permute-start | bytes 786440 | tf_op jit(solution)/shard_map/ppermute | solution.py:409
  64.3 10.7 %collective-permute-start.23 = (bf16[64,2048]{1,0:T(8,128)(2,1)S(1)}, bf16[64,2048]{1,0:T(8,128)(2,1)S(1)}, u32[]{:S(2)}, u32[]{:S(2)}) collective-permute-start(bf16[64,2048]{1,0:T(8,128)(2,1)S(1)} %get-tuple-element.82), channel_id=1, source_target_pairs={{4,0},{8,4},{12,8},{14,12},{10,14},{6,10},{2,6},{0,2},{5,1},{9,5},... | collective-permute-start | bytes 786440 | tf_op jit(solution)/shard_map/ppermute | solution.py:409
  65.9 11.4 %copy-start.9 = (bf16[64,2048]{1,0:T(8,128)(2,1)S(1)}, bf16[64,2048]{1,0:T(8,128)(2,1)}, u32[]{:S(2)}) copy-start(bf16[64,2048]{1,0:T(8,128)(2,1)} %copy-done.8) | copy-start | bytes 786436
  65.9 11.4 %copy-start.11 = (bf16[64,2048]{1,0:T(8,128)(2,1)S(1)}, bf16[64,2048]{1,0:T(8,128)(2,1)}, u32[]{:S(2)}) copy-start(bf16[64,2048]{1,0:T(8,128)(2,1)} %copy-done.10) | copy-start | bytes 786436
  65.9 10.8 %collective-permute-start.28 = (bf16[64,2048]{1,0:T(8,128)(2,1)S(1)}, bf16[64,2048]{1,0:T(8,128)(2,1)S(1)}, u32[]{:S(2)}, u32[]{:S(2)}) collective-permute-start(bf16[64,2048]{1,0:T(8,128)(2,1)S(1)} %get-tuple-element.86), channel_id=1, source_target_pairs={{0,4},{4,8},{8,12},{12,14},{14,10},{10,6},{6,2},{2,0},{1,5},{5,9},... | collective-permute-start | bytes 786440 | tf_op jit(solution)/shard_map/ppermute | solution.py:409
  73.0 9.6 %collective-permute-start.19 = (bf16[64,2048]{1,0:T(8,128)(2,1)S(1)}, bf16[64,2048]{1,0:T(8,128)(2,1)S(1)}, u32[]{:S(2)}, u32[]{:S(2)}) collective-permute-start(bf16[64,2048]{1,0:T(8,128)(2,1)S(1)} %get-tuple-element.70), channel_id=1, source_target_pairs={{0,4},{4,8},{8,12},{12,14},{14,10},{10,6},{6,2},{2,0},{1,5},{5,9},... | collective-permute-start | bytes 786440 | tf_op jit(solution)/shard_map/ppermute | solution.py:409
  74.6 8.0 %collective-permute-start.20 = (bf16[64,2048]{1,0:T(8,128)(2,1)S(1)}, bf16[64,2048]{1,0:T(8,128)(2,1)S(1)}, u32[]{:S(2)}, u32[]{:S(2)}) collective-permute-start(bf16[64,2048]{1,0:T(8,128)(2,1)S(1)} %get-tuple-element.71), channel_id=1, source_target_pairs={{4,0},{8,4},{12,8},{14,12},{10,14},{6,10},{2,6},{0,2},{5,1},{9,5},... | collective-permute-start | bytes 786440 | tf_op jit(solution)/shard_map/ppermute | solution.py:409
  75.1 11.7 %collective-permute-start.24 = (bf16[64,2048]{1,0:T(8,128)(2,1)S(1)}, bf16[64,2048]{1,0:T(8,128)(2,1)S(1)}, u32[]{:S(2)}, u32[]{:S(2)}) collective-permute-start(bf16[64,2048]{1,0:T(8,128)(2,1)S(1)} %add_convert_fusion.6), channel_id=1, source_target_pairs={{4,0},{8,4},{12,8},{14,12},{10,14},{6,10},{2,6},{0,2},{5,1},{9,5},... | collective-permute-start | bytes 786440 | tf_op jit(solution)/shard_map/ppermute | solution.py:409
  76.8 13.0 %copy-start.6 = (bf16[64,2176]{1,0:T(8,128)(2,1)S(1)}, bf16[64,2176]{1,0:T(8,128)(2,1)}, u32[]{:S(2)}) copy-start(bf16[64,2176]{1,0:T(8,128)(2,1)} %get-tuple-element.78.refs_3_.refs_1_) | copy-start | bytes 835588
  76.8 13.0 %copy-start.7 = (bf16[64,2048]{1,0:T(8,128)(2,1)S(1)}, bf16[64,2048]{1,0:T(8,128)(2,1)}, u32[]{:S(2)}) copy-start(bf16[64,2048]{1,0:T(8,128)(2,1)} %get-tuple-element.48.refs_2_) | copy-start | bytes 786436
  76.8 12.4 %collective-permute-start.29 = (bf16[64,2048]{1,0:T(8,128)(2,1)S(1)}, bf16[64,2048]{1,0:T(8,128)(2,1)S(1)}, u32[]{:S(2)}, u32[]{:S(2)}) collective-permute-start(bf16[64,2048]{1,0:T(8,128)(2,1)S(1)} %add_convert_fusion.2), channel_id=1, source_target_pairs={{0,4},{4,8},{8,12},{12,14},{14,10},{10,6},{6,2},{2,0},{1,5},{5,9},... | collective-permute-start | bytes 786440 | tf_op jit(solution)/shard_map/ppermute | solution.py:409
  82.7 10.8 %collective-permute-start.21 = (bf16[64,2048]{1,0:T(8,128)(2,1)S(1)}, bf16[64,2048]{1,0:T(8,128)(2,1)S(1)}, u32[]{:S(2)}, u32[]{:S(2)}) collective-permute-start(bf16[64,2048]{1,0:T(8,128)(2,1)S(1)} %add_convert_fusion.9), channel_id=1, source_target_pairs={{0,4},{4,8},{8,12},{12,14},{14,10},{10,6},{6,2},{2,0},{1,5},{5,9},... | collective-permute-start | bytes 786440 | tf_op jit(solution)/shard_map/ppermute | solution.py:409
  84.4 10.8 %collective-permute-start.26 = (bf16[64,2048]{1,0:T(8,128)(2,1)S(1)}, bf16[64,2048]{1,0:T(8,128)(2,1)S(1)}, u32[]{:S(2)}, u32[]{:S(2)}) collective-permute-start(bf16[64,2048]{1,0:T(8,128)(2,1)S(1)} %add_convert_fusion.8), channel_id=1, source_target_pairs={{4,0},{8,4},{12,8},{14,12},{10,14},{6,10},{2,6},{0,2},{5,1},{9,5},... | collective-permute-start | bytes 786440 | tf_op jit(solution)/shard_map/ppermute | solution.py:409
  86.8 11.2 %collective-permute-start.25 = (bf16[64,2048]{1,0:T(8,128)(2,1)S(1)}, bf16[64,2048]{1,0:T(8,128)(2,1)S(1)}, u32[]{:S(2)}, u32[]{:S(2)}) collective-permute-start(bf16[64,2048]{1,0:T(8,128)(2,1)S(1)} %add_convert_fusion.5), channel_id=1, source_target_pairs={{4,0},{8,4},{12,8},{14,12},{10,14},{6,10},{2,6},{0,2},{5,1},{9,5},... | collective-permute-start | bytes 786440 | tf_op jit(solution)/shard_map/ppermute | solution.py:409
  89.3 12.9 %collective-permute-start.30 = (bf16[64,2048]{1,0:T(8,128)(2,1)S(1)}, bf16[64,2048]{1,0:T(8,128)(2,1)S(1)}, u32[]{:S(2)}, u32[]{:S(2)}) collective-permute-start(bf16[64,2048]{1,0:T(8,128)(2,1)S(1)} %add_convert_fusion.1), channel_id=1, source_target_pairs={{0,4},{4,8},{8,12},{12,14},{14,10},{10,6},{6,2},{2,0},{1,5},{5,9},... | collective-permute-start | bytes 786440 | tf_op jit(solution)/shard_map/ppermute | solution.py:409
  93.6 8.5 %collective-permute-start.22 = (bf16[64,2048]{1,0:T(8,128)(2,1)S(1)}, bf16[64,2048]{1,0:T(8,128)(2,1)S(1)}, u32[]{:S(2)}, u32[]{:S(2)}) collective-permute-start(bf16[64,2048]{1,0:T(8,128)(2,1)S(1)} %add_convert_fusion.7), channel_id=1, source_target_pairs={{0,4},{4,8},{8,12},{12,14},{14,10},{10,6},{6,2},{2,0},{1,5},{5,9},... | collective-permute-start | bytes 786440 | tf_op jit(solution)/shard_map/ppermute | solution.py:409
  95.2 7.0 %collective-permute-start.27 = (bf16[64,2048]{1,0:T(8,128)(2,1)S(1)}, bf16[64,2048]{1,0:T(8,128)(2,1)S(1)}, u32[]{:S(2)}, u32[]{:S(2)}) collective-permute-start(bf16[64,2048]{1,0:T(8,128)(2,1)S(1)} %add_convert_fusion.3), channel_id=1, source_target_pairs={{4,0},{8,4},{12,8},{14,12},{10,14},{6,10},{2,6},{0,2},{5,1},{9,5},... | collective-permute-start | bytes 786440 | tf_op jit(solution)/shard_map/ppermute | solution.py:409
